TPU v7x, 128 devices: a whole 4x4x4 slice. The times are simulated.
128 devices in a mesh: ea: 32 (over z, x_lo, y), row: 4 (over x_hi, core).
Axes of the slice: x: 4 (x_hi: 2, x_lo: 2; x = x_hi * 2 + x_lo), y: 4, z: 4, core: 2. Of those that a mesh axis runs over, the one named last changes fastest.
Arguments:
- image_tokens: bfloat16 [25216, 768], P(('ea', 'row')), may hold values from -6 to 6
- cotangent: bfloat16 [25216, 768], P(('ea', 'row')), may hold values from -6 to 6
- routes: int32 [2, 25216, 2], P(None, ('ea', 'row')), may hold values from 0 to 31, all different within a row; in each aligned block of 197 rows (0 to 196, 197 to 393, ..., all dimensions but the last counted through in order) at most 13 rows name the same one
- norm_gains: bfloat16 [2, 2, 768], P(None, None, 'ea'), may hold values from 0.099609375 to 1.8984375
- norm_biases: bfloat16 [2, 2, 768], P(None, None, 'ea'), may hold values from -4 to 4
- qkv_weight: bfloat16 [2, 768, 2304], P(None, 'ea'), may hold values from -0.21875 to 0.21875
- out_weight: bfloat16 [2, 768, 768], P(None, 'ea'), may hold values from -0.875 to 0.875
- router_weight: bfloat16 [2, 768, 32], P(None, 'ea'), may hold values from -0.15625 to 0.15625
- expert_in: bfloat16 [2, 32, 768, 3072], P(None, 'ea', None, 'row'), may hold values from -0.21875 to 0.21875
- expert_out: bfloat16 [2, 32, 3072, 768], P(None, 'ea', 'row'), may hold values from -2 to 2
Outputs:
- block_out: bfloat16 [25216, 768], P(('ea', 'row'))
- input_grad: float32 [25216, 768], P(('ea', 'row'))
- gains_grad: float32 [2, 2, 768], P(None, None, 'ea')
- biases_grad: float32 [2, 2, 768], P(None, None, 'ea')
- qkv_grad: float32 [2, 768, 2304], P(None, 'ea')
- out_grad: float32 [2, 768, 768], P(None, 'ea')
- router_grad: float32 [2, 768, 32], P(None, 'ea')
- expert_in_grad: float32 [2, 32, 768, 3072], P(None, 'ea', None, 'row')
- expert_out_grad: float32 [2, 32, 3072, 768], P(None, 'ea', 'row')
Inputs may be any that keep to these rules, and one draw needn't show every extreme that they name: `routes`: in each block, among the 197 tokens of one device (aligned blocks of rows), no expert is named more than 13 times, and a token's two experts differ.
All inputs are finite; a program needn't handle non-finite values.
Results may differ from a plain program's by a relative error of at most 0.03.
Values may be sent and summed in bfloat16 or wider, within the bound.
No kernel may reach another device: no remote copies, remote signals or barrier semaphores. Data moves between devices by JAX's collectives and lax.ppermute only.
A program may use at most 192 MiB of HBM per device.

v0:
```python
import jax
import jax.numpy as jnp
from jax import lax
from jax.sharding import PartitionSpec as P

HEADS = 12
HEAD = 64
SEQ = 197
LAYERS = 2


EPS = 1e-06
HIGH = lax.Precision.HIGHEST


def layer_norm(values, gain, bias):
    center = jnp.mean(values, axis=-1, keepdims=True)
    shifted = values - center
    spread = jnp.mean(shifted * shifted, axis=-1, keepdims=True)
    return shifted * lax.rsqrt(spread + EPS) * gain + bias


def exact_gelu(values):
    return jax.nn.gelu(values, approximate=False)


def slot_index(chosen, experts, capacity):
    flat = chosen.reshape(-1)
    onehot = (flat[:, None] == jnp.arange(experts, dtype=jnp.int32)[None, :]).astype(jnp.int32)
    before = jnp.cumsum(onehot, axis=0) - onehot
    return (flat * capacity + jnp.sum(before * onehot, axis=1), onehot.astype(jnp.float32))


def head_split(matrix, images):
    return matrix.reshape(images, SEQ, HEADS, HEAD)


def forward_block(state, dense, expert_w, chosen, experts, capacity):
    qkv_w, out_w, router_w, gains, biases = dense
    w_in, w_out = expert_w
    gains = gains.astype(jnp.float32)
    biases = biases.astype(jnp.float32)
    tokens_dev, width = state.shape
    images = tokens_dev // SEQ
    normed = layer_norm(state, gains[0], biases[0]).astype(jnp.bfloat16)
    projected = jnp.dot(normed, qkv_w, preferred_element_type=jnp.float32).astype(jnp.bfloat16)
    query = head_split(projected[:, :width], images)
    key_part = head_split(projected[:, width : 2 * width], images)
    value_part = head_split(projected[:, 2 * width :], images)
    scaled = jnp.einsum(
        "bqhd,bkhd->bhqk", query, key_part, preferred_element_type=jnp.float32
    ) * HEAD ** (-0.5)
    peak = jnp.max(scaled, axis=-1, keepdims=True)
    expo = jnp.exp(scaled - peak)
    total = jnp.sum(expo, axis=-1, keepdims=True)
    log_total = peak + jnp.log(total)
    shares = (expo / total).astype(jnp.bfloat16)
    mixed = jnp.einsum("bhqk,bkhd->bqhd", shares, value_part, preferred_element_type=jnp.float32)
    mixed = mixed.reshape(tokens_dev, width).astype(jnp.bfloat16)
    after_attn = state + jnp.dot(mixed, out_w, preferred_element_type=jnp.float32)
    normed_two = layer_norm(after_attn, gains[1], biases[1]).astype(jnp.bfloat16)
    router = jax.nn.softmax(
        jnp.dot(normed_two, router_w, preferred_element_type=jnp.float32), axis=-1
    )
    slots, onehot = slot_index(chosen, experts, capacity)
    gate_pair = jnp.sum(onehot * jnp.repeat(router, 2, axis=0), axis=1)
    outgoing = (
        jnp.zeros((experts * capacity, width), jnp.bfloat16)
        .at[slots]
        .set(jnp.repeat(normed_two, 2, axis=0))
    )
    arrived = lax.all_to_all(outgoing, "ea", split_axis=0, concat_axis=0, tiled=True)
    arrived = arrived.reshape(-1, w_in.shape[0], capacity, width)
    pre_act = jnp.einsum("secd,edf->secf", arrived, w_in, preferred_element_type=jnp.float32)
    hidden = exact_gelu(pre_act).astype(jnp.bfloat16)
    results = jnp.einsum(
        "secf,efd->secd", hidden, w_out, preferred_element_type=jnp.float32
    ).astype(jnp.bfloat16)
    returned = lax.all_to_all(
        results.reshape(-1, width), "ea", split_axis=0, concat_axis=0, tiled=True
    )
    picked = returned[slots].astype(jnp.float32)
    mixture = jnp.sum((gate_pair[:, None] * picked).reshape(tokens_dev, 2, width), axis=1)
    kept = (
        state,
        normed,
        projected,
        log_total,
        mixed,
        after_attn,
        normed_two,
        router,
        slots,
        onehot,
        gate_pair,
        picked,
        arrived,
        pre_act,
        hidden,
    )
    return (after_attn + mixture, kept)


def backward_block(grad_out, kept, dense, expert_w, experts, capacity):
    (
        state,
        normed,
        projected,
        log_total,
        mixed,
        after_attn,
        normed_two,
        router,
        slots,
        onehot,
        gate_pair,
        picked,
        arrived,
        pre_act,
        hidden,
    ) = kept
    qkv_w, out_w, router_w, gains, biases = dense
    w_in, w_out = expert_w
    gains = gains.astype(jnp.float32)
    biases = biases.astype(jnp.float32)
    tokens_dev, width = grad_out.shape
    images = tokens_dev // SEQ
    doubled = jnp.repeat(grad_out, 2, axis=0)
    grad_gate = jnp.sum(doubled * picked, axis=1)
    grad_rows = (gate_pair[:, None] * doubled).astype(jnp.bfloat16)
    outgoing = jnp.zeros((experts * capacity, width), jnp.bfloat16).at[slots].set(grad_rows)
    grad_results = lax.all_to_all(outgoing, "ea", split_axis=0, concat_axis=0, tiled=True).reshape(
        -1, w_in.shape[0], capacity, width
    )
    grad_hidden = jnp.einsum(
        "secd,efd->secf", grad_results, w_out, preferred_element_type=jnp.float32
    )
    gelu_pull = jax.vjp(exact_gelu, pre_act)[1]
    grad_pre = gelu_pull(grad_hidden)[0].astype(jnp.bfloat16)
    grad_w_out = jnp.einsum(
        "secf,secd->efd", hidden, grad_results, preferred_element_type=jnp.float32
    )
    grad_w_in = jnp.einsum("secd,secf->edf", arrived, grad_pre, preferred_element_type=jnp.float32)
    grad_arrived = jnp.einsum("secf,edf->secd", grad_pre, w_in, preferred_element_type=jnp.float32)
    grad_arrived = grad_arrived.astype(jnp.bfloat16)
    grad_sent = lax.all_to_all(
        grad_arrived.reshape(-1, width), "ea", split_axis=0, concat_axis=0, tiled=True
    )
    grad_normed_two = jnp.sum(
        grad_sent[slots].astype(jnp.float32).reshape(tokens_dev, 2, width), axis=1
    )
    grad_router = jnp.sum((onehot * grad_gate[:, None]).reshape(tokens_dev, 2, experts), axis=1)
    grad_logit = router * (grad_router - jnp.sum(grad_router * router, axis=-1, keepdims=True))
    router_float = router_w.astype(jnp.float32)
    grad_normed_two = grad_normed_two + jnp.dot(grad_logit, router_float.T, precision=HIGH)
    grad_router_w = jnp.dot(normed_two.astype(jnp.float32).T, grad_logit, precision=HIGH)
    pull_two = jax.vjp(layer_norm, after_attn, gains[1], biases[1])[1]
    part_two, gain_two, bias_two = pull_two(grad_normed_two)
    grad_after = grad_out + part_two
    grad_attn = grad_after.astype(jnp.bfloat16)
    grad_out_w = jnp.einsum("td,te->de", mixed, grad_attn, preferred_element_type=jnp.float32)
    grad_mixed = jnp.einsum(
        "te,de->td", grad_attn, out_w, preferred_element_type=jnp.float32
    ).astype(jnp.bfloat16)
    grad_mixed = head_split(grad_mixed, images)
    query = head_split(projected[:, :width], images)
    key_part = head_split(projected[:, width : 2 * width], images)
    value_part = head_split(projected[:, 2 * width :], images)
    scaled = jnp.einsum(
        "bqhd,bkhd->bhqk", query, key_part, preferred_element_type=jnp.float32
    ) * HEAD ** (-0.5)
    shares = jnp.exp(scaled - log_total)
    grad_value = jnp.einsum(
        "bhqk,bqhd->bkhd",
        shares.astype(jnp.bfloat16),
        grad_mixed,
        preferred_element_type=jnp.float32,
    )
    grad_shares = jnp.einsum(
        "bqhd,bkhd->bhqk", grad_mixed, value_part, preferred_element_type=jnp.float32
    )
    grad_scores = shares * (grad_shares - jnp.sum(grad_shares * shares, axis=-1, keepdims=True))
    grad_raw = (grad_scores * HEAD ** (-0.5)).astype(jnp.bfloat16)
    grad_query = jnp.einsum(
        "bhqk,bkhd->bqhd", grad_raw, key_part, preferred_element_type=jnp.float32
    )
    grad_key = jnp.einsum("bhqk,bqhd->bkhd", grad_raw, query, preferred_element_type=jnp.float32)
    grad_projected = jnp.concatenate(
        [
            grad_query.reshape(tokens_dev, width),
            grad_key.reshape(tokens_dev, width),
            grad_value.reshape(tokens_dev, width),
        ],
        axis=1,
    ).astype(jnp.bfloat16)
    grad_qkv = jnp.einsum("td,te->de", normed, grad_projected, preferred_element_type=jnp.float32)
    grad_normed = jnp.einsum("te,de->td", grad_projected, qkv_w, preferred_element_type=jnp.float32)
    pull_one = jax.vjp(layer_norm, state, gains[0], biases[0])[1]
    part_one, gain_one, bias_one = pull_one(grad_normed)
    grad_input = grad_after + part_one
    dense_grad = (
        grad_qkv,
        grad_out_w,
        grad_router_w,
        jnp.stack([gain_one, gain_two]),
        jnp.stack([bias_one, bias_two]),
    )
    return (grad_input, dense_grad, (grad_w_in, grad_w_out))


def per_device(
    image_tokens,
    cotangent,
    routes,
    norm_gains,
    norm_biases,
    qkv_weight,
    out_weight,
    router_weight,
    expert_in,
    expert_out,
):
    tokens_dev = image_tokens.shape[0]
    experts = expert_in.shape[1] * lax.axis_size("ea")
    capacity = max((2 * tokens_dev + experts - 1) // experts, 2)
    state = image_tokens.astype(jnp.float32)
    saved = []
    for depth in range(LAYERS):
        dense = (
            lax.all_gather(qkv_weight[depth], "ea", axis=0, tiled=True),
            lax.all_gather(out_weight[depth], "ea", axis=0, tiled=True),
            lax.all_gather(router_weight[depth], "ea", axis=0, tiled=True),
            lax.all_gather(norm_gains[depth], "ea", axis=1, tiled=True),
            lax.all_gather(norm_biases[depth], "ea", axis=1, tiled=True),
        )
        expert_w = (
            lax.all_gather(expert_in[depth], "row", axis=2, tiled=True),
            lax.all_gather(expert_out[depth], "row", axis=1, tiled=True),
        )
        state, kept = forward_block(state, dense, expert_w, routes[depth], experts, capacity)
        saved.append((kept, dense, expert_w))
    block_out = state.astype(jnp.bfloat16)
    grad_state = cotangent.astype(jnp.float32)
    dense_terms = [None] * LAYERS
    expert_terms = [None] * LAYERS
    for depth in reversed(range(LAYERS)):
        kept, dense, expert_w = saved[depth]
        dense = (
            lax.all_gather(qkv_weight[depth], "ea", axis=0, tiled=True),
            lax.all_gather(out_weight[depth], "ea", axis=0, tiled=True),
            lax.all_gather(router_weight[depth], "ea", axis=0, tiled=True),
            lax.all_gather(norm_gains[depth], "ea", axis=1, tiled=True),
            lax.all_gather(norm_biases[depth], "ea", axis=1, tiled=True),
        )
        expert_w = (
            lax.all_gather(expert_in[depth], "row", axis=2, tiled=True),
            lax.all_gather(expert_out[depth], "row", axis=1, tiled=True),
        )
        grad_state, dense_grad, expert_grad = backward_block(
            grad_state, kept, dense, expert_w, experts, capacity
        )
        expert_terms[depth] = (
            lax.psum_scatter(
                expert_grad[0].astype(jnp.bfloat16), "row", scatter_dimension=2, tiled=True
            ).astype(jnp.float32),
            lax.psum_scatter(
                expert_grad[1].astype(jnp.bfloat16), "row", scatter_dimension=1, tiled=True
            ).astype(jnp.float32),
        )
        group_shares = (
            lax.psum_scatter(
                dense_grad[0].astype(jnp.bfloat16), "ea", scatter_dimension=0, tiled=True
            ).astype(jnp.float32),
            lax.psum_scatter(
                dense_grad[1].astype(jnp.bfloat16), "ea", scatter_dimension=0, tiled=True
            ).astype(jnp.float32),
            lax.psum_scatter(
                dense_grad[2].astype(jnp.bfloat16), "ea", scatter_dimension=0, tiled=True
            ).astype(jnp.float32),
            lax.psum_scatter(
                dense_grad[3].astype(jnp.bfloat16), "ea", scatter_dimension=1, tiled=True
            ).astype(jnp.float32),
            lax.psum_scatter(
                dense_grad[4].astype(jnp.bfloat16), "ea", scatter_dimension=1, tiled=True
            ).astype(jnp.float32),
        )
        dense_terms[depth] = (
            lax.psum(group_shares[0].astype(jnp.bfloat16), "row").astype(jnp.float32),
            lax.psum(group_shares[1].astype(jnp.bfloat16), "row").astype(jnp.float32),
            lax.psum(group_shares[2].astype(jnp.bfloat16), "row").astype(jnp.float32),
            lax.psum(group_shares[3].astype(jnp.bfloat16), "row").astype(jnp.float32),
            lax.psum(group_shares[4].astype(jnp.bfloat16), "row").astype(jnp.float32),
        )
    totals = [jnp.stack([layer_term[member] for layer_term in dense_terms]) for member in range(5)]
    grad_in_stack = jnp.stack([layer_term[0] for layer_term in expert_terms])
    grad_out_stack = jnp.stack([layer_term[1] for layer_term in expert_terms])
    return (
        block_out,
        grad_state,
        totals[3],
        totals[4],
        totals[0],
        totals[1],
        totals[2],
        grad_in_stack,
        grad_out_stack,
    )


def solution(mesh):
    in_specs = (
        P(("ea", "row"), None),
        P(("ea", "row"), None),
        P(None, ("ea", "row"), None),
        P(None, None, "ea"),
        P(None, None, "ea"),
        P(None, "ea", None),
        P(None, "ea", None),
        P(None, "ea", None),
        P(None, "ea", None, "row"),
        P(None, "ea", "row", None),
    )
    out_specs = (
        P(("ea", "row"), None),
        P(("ea", "row"), None),
        P(None, None, "ea"),
        P(None, None, "ea"),
        P(None, "ea", None),
        P(None, "ea", None),
        P(None, "ea", None),
        P(None, "ea", None, "row"),
        P(None, "ea", "row", None),
    )
    return jax.shard_map(
        per_device, mesh=mesh, in_specs=in_specs, out_specs=out_specs, check_vma=False
    )
```

profile of v0, /device:TPU:1, one launch (start us, length us, event | category | flops | bytes accessed | tf_op | source)
XLA Modules:
  0.0 2287.8 jit_solution(2501022368404337579)
XLA Ops:
  24.8 72.8 %all-gather.4 = bf16[1,768,32]{2,1,0:T(8,128)(2,1)S(1)} all-gather(bf16[1,24,32]{2,1,0:T(8,128)(2,1)S(1)} %get-tuple-element.70), channel_id=6, replica_groups=mesh['ea'=32,'row'=4] {'ea'}, dimensions={1}, use_global_device_ids=true | all-gather | bytes 50688 | tf_op jit(solution)/shard_map/all_gather | solution.py:232
  97.5 66.4 %all-gather = bf16[1,2,768]{1,0,2:T(2,128)(2,1)S(1)} all-gather(bf16[1,2,24]{1,0,2:T(2,128)(2,1)S(1)} %copy.233), channel_id=2, replica_groups=mesh['ea'=32,'row'=4] {'ea'}, dimensions={2}, use_global_device_ids=true | all-gather | bytes 3168 | tf_op jit(solution)/shard_map/all_gather | solution.py:233
  169.0 66.1 %all-gather.1 = bf16[1,2,768]{1,0,2:T(2,128)(2,1)S(1)} all-gather(bf16[1,2,24]{1,0,2:T(2,128)(2,1)S(1)} %copy.234), channel_id=3, replica_groups=mesh['ea'=32,'row'=4] {'ea'}, dimensions={2}, use_global_device_ids=true | all-gather | bytes 3168 | tf_op jit(solution)/shard_map/all_gather | solution.py:234
  240.1 65.2 %all-gather.7 = bf16[1,2,768]{1,0,2:T(2,128)(2,1)S(1)} all-gather(bf16[1,2,24]{1,0,2:T(2,128)(2,1)S(1)} %copy.235), channel_id=9, replica_groups=mesh['ea'=32,'row'=4] {'ea'}, dimensions={2}, use_global_device_ids=true | all-gather | bytes 3168 | tf_op jit(solution)/shard_map/all_gather | solution.py:233
  305.6 67.3 %all-gather.8 = bf16[1,2,768]{1,0,2:T(2,128)(2,1)S(1)} all-gather(bf16[1,2,24]{1,0,2:T(2,128)(2,1)S(1)} %copy.236), channel_id=10, replica_groups=mesh['ea'=32,'row'=4] {'ea'}, dimensions={2}, use_global_device_ids=true | all-gather | bytes 3168 | tf_op jit(solution)/shard_map/all_gather | solution.py:234
  401.7 8.7 all-to-all-done
  417.5 15.0 fusion.102
  441.8 9.3 all-to-all-done.1
  458.6 98.3 %all-gather.31.cloned.1.call-done = bf16[1,768,2304]{2,1,0:T(8,128)(2,1)} async-done(((bf16[1,24,2304]{2,1,0:T(8,128)(2,1)}), bf16[1,768,2304]{2,1,0:T(8,128)(2,1)}) %all-gather.31.cloned.1.call-update) | async-done | bytes 3538960 | tf_op jit(solution)/shard_map/all_gather | solution.py:230
  566.9 142.2 %all-gather.33.cloned.1.call-done = bf16[1,768,768]{2,1,0:T(8,128)(2,1)} async-done(((bf16[1,24,768]{2,1,0:T(8,128)(2,1)}), bf16[1,768,768]{2,1,0:T(8,128)(2,1)}) %all-gather.33.cloned.1.call-update) | async-done | bytes 1179664 | tf_op jit(solution)/shard_map/all_gather | solution.py:231
  728.7 49.7 %all-gather.35.cloned.1.call-done = bf16[1,1,768,3072]{3,2,1,0:T(8,128)(2,1)} async-done(((bf16[1,1,768,768]{3,2,1,0:T(8,128)(2,1)}), bf16[1,1,768,3072]{3,2,1,0:T(8,128)(2,1)}) %all-gather.35.cloned.1.call-update) | async-done | bytes 4718608 | tf_op jit(solution)/shard_map/all_gather | solution.py:237
  785.5 35.6 %all-gather.37.cloned.1.call-done = bf16[1,1,3072,768]{3,2,1,0:T(8,128)(2,1)} async-done(((bf16[1,1,768,768]{3,2,1,0:T(8,128)(2,1)}), bf16[1,1,3072,768]{3,2,1,0:T(8,128)(2,1)}) %all-gather.37.cloned.1.call-update) | async-done | bytes 4718608 | tf_op jit(solution)/shard_map/all_gather | solution.py:238
  821.1 14.9 fusion.96
  849.3 67.9 %all-gather.11 = bf16[1,768,32]{2,1,0:T(8,128)(2,1)S(1)} all-gather(bf16[1,24,32]{2,1,0:T(8,128)(2,1)S(1)} %copy-done.63), channel_id=13, replica_groups=mesh['ea'=32,'row'=4] {'ea'}, dimensions={1}, use_global_device_ids=true | all-gather | bytes 50688 | tf_op jit(solution)/shard_map/all_gather | solution.py:232
  936.9 9.1 all-to-all-done.4
  946.0 15.4 fusion.66
  1048.4 15.5 fusion.71
  1069.8 14.8 all_to_all.72
  1129.3 128.8 %all-reduce.8 = (bf16[2,768]{1,0:T(2,128)(2,1)S(1)}, bf16[2,768]{1,0:T(2,128)(2,1)S(1)}, bf16[2,768]{1,0:T(2,128)(2,1)S(1)}, bf16[2,768]{1,0:T(2,128)(2,1)S(1)}) all-reduce(bf16[2,768]{1,0:T(2,128)(2,1)S(1)} %pad_maximum_fusion.7, bf16[2,768]{1,0:T(2,128)(2,1)S(1)} %pad_maximum_fusion.6, ...), channel_id=17, replica_groups=mesh['ea'=32,'row'=4] {'ea'}, use_global_device_ids=true, to_apply=%region_54.55.clone | all-reduce | flops 6144 | bytes 24576
  1259.2 29.2 %reduce-scatter.37.cloned.1.call-done = bf16[24,32]{1,0:T(8,128)(2,1)} async-done(((bf16[768,32]{1,0:T(8,128)(2,1)}), bf16[24,32]{1,0:T(8,128)(2,1)}) %reduce-scatter.37.cloned.1.call-update) | async-done | bytes 1552
  1288.4 161.1 %reduce-scatter.27.cloned.1.call-done = bf16[24,768]{1,0:T(8,128)(2,1)} async-done(((bf16[768,768]{1,0:T(8,128)(2,1)}), bf16[24,768]{1,0:T(8,128)(2,1)}) %reduce-scatter.27.cloned.1.call-update) | async-done | bytes 36880 | tf_op jit(solution)/shard_map/reduce_scatter | solution.py:274
  1449.5 159.7 %reduce-scatter.25.cloned.1.call-done = bf16[24,768]{1,0:T(8,128)(2,1)} async-done(((bf16[768,768]{1,0:T(8,128)(2,1)}), bf16[24,768]{1,0:T(8,128)(2,1)}) %reduce-scatter.25.cloned.1.call-update) | async-done | bytes 36880 | tf_op jit(solution)/shard_map/reduce_scatter | solution.py:274
  1609.2 168.1 %reduce-scatter.23.cloned.1.call-done = bf16[24,2304]{1,0:T(8,128)(2,1)} async-done(((bf16[768,2304]{1,0:T(8,128)(2,1)}), bf16[24,2304]{1,0:T(8,128)(2,1)}) %reduce-scatter.23.cloned.1.call-update) | async-done | bytes 110608 | tf_op jit(solution)/shard_map/reduce_scatter | solution.py:271
  1777.3 166.3 %reduce-scatter.21.cloned.1.call-done = bf16[24,2304]{1,0:T(8,128)(2,1)} async-done(((bf16[768,2304]{1,0:T(8,128)(2,1)}), bf16[24,2304]{1,0:T(8,128)(2,1)}) %reduce-scatter.21.cloned.1.call-update) | async-done | bytes 110608 | tf_op jit(solution)/shard_map/reduce_scatter | solution.py:271
  1956.8 16.6 fusion.57
  1973.7 16.6 fusion.56
  1992.4 13.8 all-reduce.14.cloned.1.call-done
  2011.4 37.3 %all-reduce.16.cloned.1.call-done = (bf16[1,24,2304]{2,1,0:T(8,128)(2,1)}, bf16[1,24,2304]{2,1,0:T(8,128)(2,1)}) async-done(((bf16[1,24,2304]{2,1,0:T(8,128)(2,1)}, bf16[1,24,2304]{2,1,0:T(8,128)(2,1)}), (bf16[1,24,2304]{2,1,0:T(8,128)(2,1)}, bf16[1,24,2304]{2,1,0:T(8,128)(2,1)})) %all-reduce.16.cloned.1.call-update) | async-done | bytes 221200 | tf_op jit(solution)/shard_map/psum | solution.py:288
  2050.4 55.0 %reduce-scatter.31.cloned.1.call-done = bf16[1,768,768]{2,1,0:T(8,128)(2,1)} async-done(((bf16[1,768,3072]{2,1,0:T(8,128)(2,1)}), bf16[1,768,768]{2,1,0:T(8,128)(2,1)}) %reduce-scatter.31.cloned.1.call-update) | async-done | bytes 1179664 | tf_op jit(solution)/shard_map/reduce_scatter | solution.py:263
  2105.5 57.5 %reduce-scatter.29.cloned.1.call-done = bf16[1,768,768]{2,1,0:T(8,128)(2,1)} async-done(((bf16[1,768,3072]{2,1,0:T(8,128)(2,1)}), bf16[1,768,768]{2,1,0:T(8,128)(2,1)}) %reduce-scatter.29.cloned.1.call-update) | async-done | bytes 1179664 | tf_op jit(solution)/shard_map/reduce_scatter | solution.py:263
  2167.0 52.7 %reduce-scatter.35.cloned.1.call-done = bf16[1,768,768]{2,1,0:T(8,128)(2,1)} async-done(((bf16[1,3072,768]{2,1,0:T(8,128)(2,1)}), bf16[1,768,768]{2,1,0:T(8,128)(2,1)}) %reduce-scatter.35.cloned.1.call-update) | async-done | bytes 1179664 | tf_op jit(solution)/shard_map/reduce_scatter | solution.py:266
  2219.8 56.9 %reduce-scatter.33.cloned.1.call-done = bf16[1,768,768]{2,1,0:T(8,128)(2,1)} async-done(((bf16[1,3072,768]{2,1,0:T(8,128)(2,1)}), bf16[1,768,768]{2,1,0:T(8,128)(2,1)}) %reduce-scatter.33.cloned.1.call-update) | async-done | bytes 1179664 | tf_op jit(solution)/shard_map/reduce_scatter | solution.py:266
  (500 shorter events, 317.0 us)
Async XLA Ops:
  7.2 366.2 %all-gather.23.cloned.1.call-start = ((), (), s32[]{:S(2)}) async-start(), calls=%async_computation.26 | async-start | bytes 3649536 | tf_op jit(solution)/shard_map/all_gather | solution.py:230
  9.1 370.7 %all-gather.25.cloned.1.call-start = ((), (), s32[]{:S(2)}) async-start(), calls=%async_computation.27 | async-start | bytes 1216512 | tf_op jit(solution)/shard_map/all_gather | solution.py:231
  10.6 391.1 %all-gather.27.cloned.1.call-start = ((), (), s32[]{:S(2)}) async-start(), calls=%async_computation.28 | async-start | bytes 5898240 | tf_op jit(solution)/shard_map/all_gather | solution.py:237
  13.9 403.6 %all-gather.29.cloned.1.call-start = ((), (), s32[]{:S(2)}) async-start(), calls=%async_computation.29 | async-start | bytes 5898240 | tf_op jit(solution)/shard_map/all_gather | solution.py:238
  15.5 541.3 %all-gather.31.cloned.1.call-start = ((), (), s32[]{:S(2)}) async-start(), calls=%async_computation.30 | async-start | bytes 3649536 | tf_op jit(solution)/shard_map/all_gather | solution.py:230
  16.1 693.1 %all-gather.33.cloned.1.call-start = ((), (), s32[]{:S(2)}) async-start(), calls=%async_computation.31 | async-start | bytes 1216512 | tf_op jit(solution)/shard_map/all_gather | solution.py:231
  16.7 761.8 %all-gather.35.cloned.1.call-start = ((), (), s32[]{:S(2)}) async-start(), calls=%async_computation.32 | async-start | bytes 5898240 | tf_op jit(solution)/shard_map/all_gather | solution.py:237
  17.4 803.6 %all-gather.37.cloned.1.call-start = ((), (), s32[]{:S(2)}) async-start(), calls=%async_computation.33 | async-start | bytes 5898240 | tf_op jit(solution)/shard_map/all_gather | solution.py:238
  18.3 358.0 %copy-start.75 = (f32[197]{0:T(256)}, f32[197]{0:T(256)S(1)}, u32[]{:S(2)}) copy-start(f32[197]{0:T(256)S(1)} %broadcast_multiply_fusion.5) | copy-start | bytes 2368
  19.8 421.3 %copy-start.64 = (s32[197,2]{0,1:T(2,128)}, s32[197,2]{0,1:T(2,128)S(1)}, u32[]{:S(2)}) copy-start(s32[197,2]{0,1:T(2,128)S(1)} %get-tuple-element.72) | copy-start | bytes 4732
  24.7 359.6 %copy-start.101 = (s32[394,1]{0,1:T(1,128)}, s32[394,1]{0,1:T(1,128)S(1)}, u32[]{:S(2)}) copy-start(s32[394,1]{0,1:T(1,128)S(1)} %compare_select_fusion.1) | copy-start | bytes 4732
  24.8 426.5 %copy-start.66 = (s32[1024]{0:T(1024)}, s32[1024]{0:T(1024)S(1)}, u32[]{:S(2)}) copy-start(s32[1024]{0:T(1024)S(1)} %pad_clamp_fusion.1) | copy-start | bytes 12292
  388.3 22.1 all-to-all-start
  401.6 442.8 %copy-start.102 = (s32[394,1]{0,1:T(1,128)}, s32[394,1]{0,1:T(1,128)S(1)}, u32[]{:S(2)}) copy-start(s32[394,1]{0,1:T(1,128)S(1)} %compare_select_fusion) | copy-start | bytes 4732
  433.7 17.4 all-to-all-start.1
  721.6 56.9 %all-to-all-start.2 = ((bf16[32,13,768]{2,1,0:T(8,128)(2,1)}), bf16[32,13,768]{2,1,0:T(8,128)(2,1)}, u32[]{:S(2)}, u32[]{:S(2)}) async-start(bf16[32,13,768]{2,1,0:T(8,128)(2,1)} %all_to_all.52), calls=%async_computation.2 | async-start | bytes 1572864 | tf_op jit(solution)/shard_map/all_to_all | solution.py:72
  837.3 80.9 %all-to-all-start.3 = ((bf16[32,13,768]{2,1,0:T(8,128)(2,1)}), bf16[32,13,768]{2,1,0:T(8,128)(2,1)}, u32[]{:S(2)}, u32[]{:S(2)}) async-start(bf16[32,13,768]{2,1,0:T(8,128)(2,1)} %copy.196), calls=%async_computation.3 | async-start | bytes 1572864 | tf_op jit(solution)/shard_map/all_to_all | solution.py:79
  931.3 14.7 all-to-all-start.4
  968.3 14.8 all-to-all-start.5
  973.2 286.0 %reduce-scatter.39.cloned.1.call-start = ((), (), s32[]{:S(2)}) async-start(), calls=%async_computation.35 | async-start | bytes 202752
  1031.4 17.0 all-to-all-start.6
  1038.5 249.9 %reduce-scatter.37.cloned.1.call-start = ((), (), s32[]{:S(2)}) async-start(), calls=%async_computation.34 | async-start | bytes 202752
  1039.8 409.6 %reduce-scatter.27.cloned.1.call-start = ((), (), s32[]{:S(2)}) async-start(), calls=%async_computation.21 | async-start | bytes 1216512 | tf_op jit(solution)/shard_map/reduce_scatter | solution.py:274
  1042.6 566.6 %reduce-scatter.25.cloned.1.call-start = ((), (), s32[]{:S(2)}) async-start(), calls=%async_computation.20 | async-start | bytes 1216512 | tf_op jit(solution)/shard_map/reduce_scatter | solution.py:274
  1098.4 678.9 %reduce-scatter.23.cloned.1.call-start = ((), (), s32[]{:S(2)}) async-start(), calls=%async_computation.19 | async-start | bytes 3649536 | tf_op jit(solution)/shard_map/reduce_scatter | solution.py:271
  1102.6 841.0 %reduce-scatter.21.cloned.1.call-start = ((), (), s32[]{:S(2)}) async-start(), calls=%async_computation.18 | async-start | bytes 3649536 | tf_op jit(solution)/shard_map/reduce_scatter | solution.py:271
  1123.4 882.7 %all-reduce.14.cloned.1.call-start = ((), (), s32[]{:S(2)}) async-start(), calls=%async_computation.36 | async-start | bytes 176128 | tf_op jit(solution)/shard_map/psum | solution.py:291
  1609.2 439.5 %all-reduce.16.cloned.1.call-start = ((), (), s32[]{:S(2)}) async-start(), calls=%async_computation.37 | async-start | bytes 442368 | tf_op jit(solution)/shard_map/psum | solution.py:288
  1943.7 161.8 %reduce-scatter.31.cloned.1.call-start = ((), (), s32[]{:S(2)}) async-start(), calls=%async_computation.23 | async-start | bytes 5898240 | tf_op jit(solution)/shard_map/reduce_scatter | solution.py:263
  1950.6 212.3 %reduce-scatter.29.cloned.1.call-start = ((), (), s32[]{:S(2)}) async-start(), calls=%async_computation.22 | async-start | bytes 5898240 | tf_op jit(solution)/shard_map/reduce_scatter | solution.py:263
  1956.8 263.0 %reduce-scatter.35.cloned.1.call-start = ((), (), s32[]{:S(2)}) async-start(), calls=%async_computation.25 | async-start | bytes 5898240 | tf_op jit(solution)/shard_map/reduce_scatter | solution.py:266
  1973.5 303.2 %reduce-scatter.33.cloned.1.call-start = ((), (), s32[]{:S(2)}) async-start(), calls=%async_computation.24 | async-start | bytes 5898240 | tf_op jit(solution)/shard_map/reduce_scatter | solution.py:266
  (114 other events, 3892.2 us)
Sparse Core Ops, SparseCore 0:
  10.2 140.1 all-gather.22
  152.6 150.9 all-gather.24
  305.3 64.3 all-gather.26
  371.7 45.6 all-gather.28
  419.5 137.2 all-gather.30
  558.3 150.7 all-gather.32
  710.8 67.5 all-gather.34
  780.1 40.9 all-gather.36
  978.9 151.7 reduce-scatter.38
  1133.0 155.3 reduce-scatter.36
  1290.8 158.6 reduce-scatter.26
  1451.8 157.3 reduce-scatter.24
  1612.1 165.1 reduce-scatter.22
  1780.3 163.2 reduce-scatter.20
  1947.1 59.0 all-reduce.13
  2008.8 39.8 all-reduce.15
  2051.8 53.6 reduce-scatter.30
  2108.7 54.1 reduce-scatter.28
  2165.6 54.1 reduce-scatter.34
  2222.5 54.1 reduce-scatter.32
where the time goes:
time: 2300 us; the launch traced here: 2290 us
  waiting for transfers between devices  1320 us (57%)
  blocking collectives  549 us (24%)
  matrix products  206 us (9%)
  local copies, waits for them, and re-layouts  98 us (4%)
  other arithmetic  53.8 us (2%)
  starting transfers between devices  43.6 us (2%)
    reduce_scatter x2, waiting for transfers between devices, per_device(): lax.psum_scatter(dense_grad[0].astype(jnp.bfloat16), 'ea', scatter_dimens...  334 us
    reduce_scatter x2, waiting for transfers between devices, per_device(): lax.psum_scatter(dense_grad[1].astype(jnp.bfloat16), 'ea', scatter_dimens...  321 us
    all_gather x2, waiting for transfers between devices, per_device(): lax.all_gather(out_weight[depth], 'ea', axis=0, tiled=True)  142 us
    all_gather x2, blocking collectives, per_device(): lax.all_gather(router_weight[depth], 'ea', axis=0, tiled=True)  141 us
    all_gather x2, blocking collectives, per_device(): lax.all_gather(norm_biases[depth], 'ea', axis=1, tiled=True)  133 us
    all_gather x2, blocking collectives, per_device(): lax.all_gather(norm_gains[depth], 'ea', axis=1, tiled=True)  132 us
    unnamed x1, blocking collectives  129 us
    reduce_scatter x2, waiting for transfers between devices, per_device(): lax.psum_scatter(expert_grad[0].astype(jnp.bfloat16), 'row', scatter_dime...  112 us
  transfers between devices with their start and end apart: 27, of which 20 were waited for; matrix products, arithmetic and copies ran while one was open for 13% of the time, Pallas kernels for 0%

commit v1 on v0

v1 whole, which is shorter than its diff:
```python
import jax
import jax.numpy as jnp
from jax import lax
from jax.sharding import Mesh
from jax.sharding import PartitionSpec as P

HEADS = 12
HEAD = 64
SEQ = 197
LAYERS = 2
EPS = 1e-06
HIGH = lax.Precision.HIGHEST
BF = jnp.bfloat16
F32 = jnp.float32
SLOTS = 16
SCALE = HEAD ** (-0.5)
GROUP = ("ea", "half")


def dot(a, b, dims=((1,), (0,))):
    return lax.dot_general(a, b, (dims, ((), ())), preferred_element_type=F32)


def dot_nt(a, b):
    return dot(a, b, ((1,), (1,)))


def dot_tn(a, b):
    return dot(a, b, ((0,), (0,)))


def swap_core(value):
    return lax.ppermute(value, "core", [(0, 1), (1, 0)])


def swap_half(value):
    return lax.ppermute(value, "half", [(0, 1), (1, 0)])


def exchange(rows):
    return lax.all_to_all(rows, GROUP, split_axis=0, concat_axis=0, tiled=True)


def gelu_parts(x):
    mag = jnp.abs(x)
    t = 1.0 / (1.0 + (0.3275911 * 0.7071067811865476) * mag)
    bell = jnp.exp(-0.5 * x * x)
    poly = 0.5 * t * (
        0.254829592
        + t * (-0.284496736 + t * (1.421413741 + t * (-1.453152027 + t * 1.061405429)))
    )
    tail = poly * bell
    cdf = jnp.where(x < 0, tail, 1.0 - tail)
    return cdf, cdf + x * bell * 0.3989422804014327


def normalize(x, gain, bias):
    center = jnp.mean(x, axis=-1, keepdims=True)
    shifted = x - center
    spread = jnp.mean(shifted * shifted, axis=-1, keepdims=True)
    inv = lax.rsqrt(spread + EPS)
    unit = shifted * inv
    return unit * gain + bias, unit, inv


def normalize_back(grad, unit, inv, gain):
    scaled = grad * gain
    mean_a = jnp.mean(scaled, axis=-1, keepdims=True)
    mean_b = jnp.mean(scaled * unit, axis=-1, keepdims=True)
    return (
        inv * (scaled - mean_a - unit * mean_b),
        jnp.sum(grad * unit, axis=0),
        jnp.sum(grad, axis=0),
    )


def heads_of(matrix):
    return matrix.reshape(SEQ, HEADS, HEAD)


def gather_cols(mine):
    n = mine.shape[1]
    groups = lax.axis_size("ea")
    sent = jnp.broadcast_to(mine[None], (groups,) + mine.shape)
    got = lax.all_to_all(sent, "ea", split_axis=0, concat_axis=0).reshape(-1, n)
    other = swap_core(got)
    first = lax.axis_index("core") == 0
    return jnp.where(first, got, other), jnp.where(first, other, got)


def core_cols(packed):
    n = packed.shape[1] // 2
    return lax.dynamic_slice_in_dim(packed, lax.axis_index("core") * n, n, 1)


def sum_cols(packed):
    n = packed.shape[1] // 2
    packed = packed.astype(BF)
    core = lax.axis_index("core")
    own = lax.dynamic_slice_in_dim(packed, core * n, n, 1)
    give = lax.dynamic_slice_in_dim(packed, (1 - core) * n, n, 1)
    pair = (own.astype(F32) + swap_core(give).astype(F32)).astype(BF)
    groups = lax.axis_size("ea")
    parts = lax.all_to_all(
        pair.reshape(groups, -1, n), "ea", split_axis=0, concat_axis=0
    )
    part = jnp.sum(parts.astype(F32), axis=0)
    full = part + swap_half(part)
    other = swap_core(full)
    first = core == 0
    return jnp.concatenate(
        [jnp.where(first, full, other), jnp.where(first, other, full)], axis=1
    )


def pad_cols(value, cols):
    return jnp.pad(value, ((0, 0), (0, cols - value.shape[1])))


def attention(state, dense):
    qkv_w, out_w, _, gains, biases = dense
    normed, unit, inv = normalize(state, gains[0], biases[0])
    normed = normed.astype(BF)
    projected = dot(normed, qkv_w).astype(BF)
    query, key_part, value_part = (
        heads_of(projected[:, i * 768 : (i + 1) * 768]) for i in range(3)
    )
    scaled = jnp.einsum("qhd,khd->hqk", query, key_part, preferred_element_type=F32) * SCALE
    peak = jnp.max(scaled, axis=-1, keepdims=True)
    expo = jnp.exp(scaled - peak)
    total = jnp.sum(expo, axis=-1, keepdims=True)
    log_total = peak + jnp.log(total)
    shares = (expo / total).astype(BF)
    mixed = jnp.einsum("hqk,khd->qhd", shares, value_part, preferred_element_type=F32)
    mixed = mixed.reshape(state.shape).astype(BF)
    after = state + dot(mixed, out_w)
    return after, (unit, inv, normed, projected, log_total, mixed)


def attention_back(grad_after, kept, dense):
    unit, inv, normed, projected, log_total, mixed = kept
    qkv_w, out_w, _, gains, _ = dense
    tokens, width = grad_after.shape
    grad_attn = grad_after.astype(BF)
    grad_out_w = dot_tn(mixed, grad_attn)
    grad_mixed = heads_of(dot_nt(grad_attn, out_w).astype(BF))
    query, key_part, value_part = (
        heads_of(projected[:, i * width : (i + 1) * width]) for i in range(3)
    )
    scaled = jnp.einsum("qhd,khd->hqk", query, key_part, preferred_element_type=F32) * SCALE
    shares = jnp.exp(scaled - log_total)
    grad_value = jnp.einsum(
        "hqk,qhd->khd", shares.astype(BF), grad_mixed, preferred_element_type=F32
    )
    grad_shares = jnp.einsum("qhd,khd->hqk", grad_mixed, value_part, preferred_element_type=F32)
    grad_scores = shares * (grad_shares - jnp.sum(grad_shares * shares, axis=-1, keepdims=True))
    grad_raw = (grad_scores * SCALE).astype(BF)
    grad_query = jnp.einsum("hqk,khd->qhd", grad_raw, key_part, preferred_element_type=F32)
    grad_key = jnp.einsum("hqk,qhd->khd", grad_raw, query, preferred_element_type=F32)
    grad_projected = jnp.concatenate(
        [part.reshape(tokens, width) for part in (grad_query, grad_key, grad_value)], axis=1
    ).astype(BF)
    grad_qkv = dot_tn(normed, grad_projected)
    grad_normed = dot_nt(grad_projected, qkv_w)
    part_one, gain_one, bias_one = normalize_back(grad_normed, unit, inv, gains[0])
    return grad_after + part_one, grad_qkv, grad_out_w, gain_one, bias_one


def routing(chosen, experts):
    tokens = chosen.shape[0]
    flat = jnp.concatenate([chosen[:, 0], chosen[:, 1]])
    onehot = flat[:, None] == jnp.arange(experts, dtype=jnp.int32)[None, :]
    pairs = 2 * tokens
    earlier = (
        lax.broadcasted_iota(jnp.int32, (pairs, pairs), 1)
        < lax.broadcasted_iota(jnp.int32, (pairs, pairs), 0)
    ).astype(BF)
    onehot = onehot.astype(F32)
    before = dot(earlier, onehot.astype(BF))
    position = jnp.sum(before * onehot, axis=1).astype(jnp.int32)
    code = flat * (2 * SLOTS) + position
    slots = experts * 2 * SLOTS
    row_code = lax.broadcasted_iota(jnp.int32, (slots, pairs), 0)
    row_code = row_code - (row_code & SLOTS)
    send = (row_code == code[None, :]).astype(BF)
    col_code = lax.broadcasted_iota(jnp.int32, (pairs, slots), 1)
    col_code = col_code - (col_code & SLOTS)
    fetch = (col_code == code[:, None]).astype(BF)
    return onehot, send, fetch


def router_forward(normed_two, router_w, onehot):
    router = jax.nn.softmax(dot(normed_two, router_w), axis=-1)
    tokens = router.shape[0]
    gate = [
        jnp.sum(onehot[j * tokens : (j + 1) * tokens] * router, axis=1, keepdims=True)
        for j in range(2)
    ]
    return router, gate


def router_back(grad, picked, router, onehot, normed_two, router_w):
    tokens = router.shape[0]
    grad_router = 0.0
    for j in range(2):
        part = jnp.sum(grad * picked[j], axis=1, keepdims=True)
        grad_router = grad_router + onehot[j * tokens : (j + 1) * tokens] * part
    grad_logit = router * (grad_router - jnp.sum(grad_router * router, axis=-1, keepdims=True))
    grad_normed = jnp.dot(grad_logit, router_w.astype(F32).T, precision=HIGH)
    grad_router_w = jnp.dot(normed_two.astype(F32).T, grad_logit, precision=HIGH)
    return grad_normed, grad_router_w


def pack_grads(grad_qkv, grad_out_w, grad_router_w, gain_grads, bias_grads):
    small = jnp.concatenate([grad_router_w, jnp.stack(gain_grads + bias_grads, axis=1)], axis=1)
    return jnp.concatenate([grad_qkv, grad_out_w, pad_cols(small, 256)], axis=1)


def per_device(
    image_tokens,
    cotangent,
    routes,
    norm_gains,
    norm_biases,
    qkv_weight,
    out_weight,
    router_weight,
    expert_in,
    expert_out,
):
    tokens, width = image_tokens.shape
    experts = lax.axis_size("ea")
    dense = []
    small = [
        pad_cols(
            jnp.concatenate([router_weight[b], norm_gains[b].T, norm_biases[b].T], axis=1), 256
        )
        for b in range(LAYERS)
    ]
    for b in range(LAYERS):
        packed = jnp.concatenate([qkv_weight[b], out_weight[b], small[b]], axis=1)
        whole = jnp.concatenate(gather_cols(core_cols(packed)), axis=1)
        rest = whole[:, 3072:]
        gains = rest[:, experts : experts + 2].astype(F32).T
        biases = rest[:, experts + 2 : experts + 4].astype(F32).T
        dense.append((whole[:, :2304], whole[:, 2304:3072], rest[:, :experts], gains, biases))
    routed = [routing(routes[b], experts) for b in range(LAYERS)]
    w_in = [expert_in[b, 0] for b in range(LAYERS)]
    w_out = [expert_out[b, 0] for b in range(LAYERS)]

    state = image_tokens.astype(F32)
    after0, kept0 = attention(state, dense[0])
    onehot, send, fetch = routed[0]
    wide, unit0, inv0 = normalize(after0, dense[0][3][1], dense[0][4][1])
    normed0 = wide.astype(BF)
    router0, gate0 = router_forward(normed0, dense[0][2], onehot)
    arrived = exchange(dot(send[:, :tokens] + send[:, tokens:], normed0).astype(BF))
    rows0 = jnp.concatenate([arrived, swap_core(arrived)], axis=0)
    pre = dot(rows0, w_in[0])
    cdf, slope0 = gelu_parts(pre)
    hidden0 = (pre * cdf).astype(BF)
    part = dot(hidden0, w_out[0])
    half_rows = part.shape[0] // 2
    back = part[:half_rows] + swap_core(part[half_rows:].astype(BF)).astype(F32)
    returned = exchange(back.astype(BF))
    picked = dot(fetch, returned)
    picked0 = (picked[:tokens], picked[tokens:])
    state1 = after0 + gate0[0] * picked0[0] + gate0[1] * picked0[1]

    grad = cotangent.astype(F32)
    after1, kept1 = attention(state1, dense[1])
    onehot1, send1, fetch1 = routed[1]
    wide, unit1, inv1 = normalize(after1, dense[1][3][1], dense[1][4][1])
    normed1 = wide.astype(BF)
    router1, gate1 = router_forward(normed1, dense[1][2], onehot1)
    rows = dot(send1[:, :tokens] + send1[:, tokens:], normed1).astype(BF)
    grad_rows = jnp.concatenate([(g * grad).astype(BF) for g in gate1], axis=0)
    grad_rows = dot(send1, grad_rows).astype(BF)
    arrived = exchange(jnp.concatenate([rows, grad_rows], axis=1))
    both = jnp.concatenate([arrived, swap_core(arrived)], axis=0)
    rows1, grows1 = both[:, :width], both[:, width:]
    pre = dot(rows1, w_in[1])
    cdf, slope = gelu_parts(pre)
    hidden1 = (pre * cdf).astype(BF)
    grad_pre1 = (dot_nt(grows1, w_out[1]) * slope).astype(BF)
    part = jnp.concatenate([dot(hidden1, w_out[1]), dot_nt(grad_pre1, w_in[1])], axis=1)
    back = part[:half_rows] + swap_core(part[half_rows:].astype(BF)).astype(F32)
    returned = exchange(back.astype(BF))
    picked = dot(fetch1, returned)
    picked1 = (picked[:tokens, :width], picked[tokens:, :width])
    grad_sent = picked[:tokens, width:] + picked[tokens:, width:]
    block_out = (after1 + gate1[0] * picked1[0] + gate1[1] * picked1[1]).astype(BF)
    grad_w_out1 = dot_tn(hidden1, grows1)
    grad_w_in1 = dot_tn(rows1, grad_pre1)

    extra, grad_router_w1 = router_back(grad, picked1, router1, onehot1, normed1, dense[1][2])
    part_two, gain_two, bias_two = normalize_back(
        grad_sent + extra, unit1, inv1, dense[1][3][1]
    )
    grad, grad_qkv, grad_out_w, gain_one, bias_one = attention_back(
        grad + part_two, kept1, dense[1]
    )
    sums1 = sum_cols(
        pack_grads(grad_qkv, grad_out_w, grad_router_w1, [gain_one, gain_two], [bias_one, bias_two])
    )

    grad_rows = jnp.concatenate([(g * grad).astype(BF) for g in gate0], axis=0)
    arrived = exchange(dot(send, grad_rows).astype(BF))
    grows0 = jnp.concatenate([arrived, swap_core(arrived)], axis=0)
    grad_pre0 = (dot_nt(grows0, w_out[0]) * slope0).astype(BF)
    part = dot_nt(grad_pre0, w_in[0])
    back = part[:half_rows] + swap_core(part[half_rows:].astype(BF)).astype(F32)
    returned = exchange(back.astype(BF))
    picked = dot(fetch, returned)
    grad_sent = picked[:tokens] + picked[tokens:]
    grad_w_out0 = dot_tn(hidden0, grows0)
    grad_w_in0 = dot_tn(rows0, grad_pre0)
    extra, grad_router_w0 = router_back(grad, picked0, router0, onehot, normed0, dense[0][2])
    part_two, gain_two, bias_two = normalize_back(
        grad_sent + extra, unit0, inv0, dense[0][3][1]
    )
    grad, grad_qkv, grad_out_w, gain_one, bias_one = attention_back(
        grad + part_two, kept0, dense[0]
    )
    sums0 = sum_cols(
        pack_grads(grad_qkv, grad_out_w, grad_router_w0, [gain_one, gain_two], [bias_one, bias_two])
    )

    sums = jnp.stack([sums0, sums1])
    rest = sums[:, :, 3072:]
    return (
        block_out,
        grad,
        rest[:, :, experts : experts + 2].transpose(0, 2, 1),
        rest[:, :, experts + 2 : experts + 4].transpose(0, 2, 1),
        sums[:, :, :2304],
        sums[:, :, 2304:3072],
        rest[:, :, :experts],
        jnp.stack([grad_w_in0, grad_w_in1])[:, None],
        jnp.stack([grad_w_out0, grad_w_out1])[:, None],
    )


def solution(mesh):
    fine = Mesh(
        mesh.devices.reshape(mesh.shape["ea"], mesh.shape["row"] // 2, 2), ("ea", "half", "core")
    )
    row = ("half", "core")
    every = ("ea",) + row
    in_specs = (
        P(every, None),
        P(every, None),
        P(None, every, None),
        P(None, None, "ea"),
        P(None, None, "ea"),
        P(None, "ea", None),
        P(None, "ea", None),
        P(None, "ea", None),
        P(None, "ea", None, row),
        P(None, "ea", row, None),
    )
    out_specs = (
        P(every, None),
        P(every, None),
        P(None, None, "ea"),
        P(None, None, "ea"),
        P(None, "ea", None),
        P(None, "ea", None),
        P(None, "ea", None),
        P(None, "ea", None, row),
        P(None, "ea", row, None),
    )
    return jax.shard_map(
        per_device, mesh=fine, in_specs=in_specs, out_specs=out_specs, check_vma=False
    )
```

time: 2300 us -> 604 us (0.26)
  waiting for transfers between devices: 1320 us -> 185 us
  blocking collectives: 549 us -> 113 us
  matrix products: 206 us -> 137 us
  local copies, waits for them, and re-layouts: 98 us -> 44.2 us
  starting transfers between devices: 43.6 us -> 67.2 us
    reduce_scatter x8 -> x0, waiting for transfers between devices: 877 us -> none  [the longest x2 334 us: per_device(): lax.psum_scatter(dense_grad[0].astype(jnp.bfloat16), 'ea', scatter_dimens...]
    all_gather x6 -> x0, blocking collectives: 406 us -> none  [the longest x2 141 us: per_device(): lax.all_gather(router_weight[depth], 'ea', axis=0, tiled=True)]
    all_gather x8 -> x0, waiting for transfers between devices: 326 us -> none  [the longest x2 142 us: per_device(): lax.all_gather(out_weight[depth], 'ea', axis=0, tiled=True)]
    unnamed x1 -> x0, blocking collectives: 129 us -> none
    all_to_all x7, waiting for transfers between devices: 33.5 us -> 144 us  [the longest x4 94.5 us: exchange(): return lax.all_to_all(rows, GROUP, split_axis=0, concat_axis=0, tiled=True)]
    all_to_all x1 -> x3, blocking collectives: 14.8 us -> 113 us  [the longest x2 71.9 us: exchange(): return lax.all_to_all(rows, GROUP, split_axis=0, concat_axis=0, tiled=True)]
    dot_general x42 -> x51, matrix products: 206 us -> 137 us  [the longest x35 105 us: dot(): return lax.dot_general(a, b, (dims, ((), ())), preferred_element_type=F32)]
    psum x2 -> x0, waiting for transfers between devices: 51.1 us -> none  [the longest x1 37.3 us: per_device(): lax.psum(group_shares[0].astype(jnp.bfloat16), 'row').astype(jnp.float32)]
  transfers between devices with their start and end apart: 27 -> 21, of which waited for: 20 -> 13; matrix products, arithmetic and copies ran while one was open for 13% -> 16% of each run, Pallas kernels for 0% -> 0%
where the time goes in v1:
time: 604 us; the launch traced here: 594 us
  waiting for transfers between devices  185 us (31%)
  matrix products  137 us (23%)
  blocking collectives  113 us (19%)
  starting transfers between devices  67.2 us (11%)
  other arithmetic  44.9 us (7%)
  local copies, waits for them, and re-layouts  44.2 us (7%)
    dot_general x35, matrix products, dot(): return lax.dot_general(a, b, (dims, ((), ())), preferred_element_type=F32)  105 us
    all_to_all x4, waiting for transfers between devices, exchange(): return lax.all_to_all(rows, GROUP, split_axis=0, concat_axis=0, tiled=True)  94.5 us
    all_to_all x2, blocking collectives, exchange(): return lax.all_to_all(rows, GROUP, split_axis=0, concat_axis=0, tiled=True)  71.9 us
    all_to_all x1, blocking collectives, gather_cols(): got = lax.all_to_all(sent, 'ea', split_axis=0, concat_axis=0).reshape(-1, n)  41.4 us
    all_to_all x1, waiting for transfers between devices, gather_cols(): got = lax.all_to_all(sent, 'ea', split_axis=0, concat_axis=0).reshape(-1, n)  28.8 us
    all_to_all x4, starting transfers between devices, exchange(): return lax.all_to_all(rows, GROUP, split_axis=0, concat_axis=0, tiled=True)  24.6 us
    ppermute x2, waiting for transfers between devices, swap_half(): return lax.ppermute(value, 'half', [(0, 1), (1, 0)])  23.8 us
    ppermute x12, starting transfers between devices, swap_core(): return lax.ppermute(value, 'core', [(0, 1), (1, 0)])  23.8 us
  transfers between devices with their start and end apart: 21, of which 13 were waited for; matrix products, arithmetic and copies ran while one was open for 16% of the time, Pallas kernels for 0%

profile of v1, /device:TPU:1, one launch (start us, length us, event | category | flops | bytes accessed | tf_op | source)
XLA Modules:
  0.0 594.2 jit_solution(13578609946168380594)
XLA Ops:
  6.0 41.4 %all_to_all.92 = bf16[32,24,1664]{2,1,0:T(8,128)(2,1)S(1)} all-to-all(bf16[32,24,1664]{2,1,0:T(8,128)(2,1)S(1)} %broadcast_in_dim.8), channel_id=1, replica_groups=mesh['ea'=32,'half'=2,'core'=2] {'ea'}, dimensions={0} | all-to-all | bytes 5111808 | tf_op jit(solution)/shard_map/all_to_all | solution.py:85
  66.0 6.3 %all-to-all-start.1 = ((bf16[64,16,768]{2,1,0:T(8,128)(2,1)}), bf16[64,16,768]{2,1,0:T(8,128)(2,1)S(1)}, u32[]{:S(2)}, u32[]{:S(2)}) async-start(bf16[64,16,768]{2,1,0:T(8,128)(2,1)} %bitcast.18), calls=%async_computation.1 | async-start | bytes 3145728 | tf_op jit(solution)/shard_map/all_to_all | solution.py:41
  72.5 22.9 %all-to-all-done.1 = bf16[64,16,768]{2,1,0:T(8,128)(2,1)S(1)} async-done(((bf16[64,16,768]{2,1,0:T(8,128)(2,1)}), bf16[64,16,768]{2,1,0:T(8,128)(2,1)S(1)}, u32[]{:S(2)}, u32[]{:S(2)}) %all-to-all-start.1) | async-done | bytes 1572896 | tf_op jit(solution)/shard_map/all_to_all | solution.py:41
  103.4 28.8 %all-to-all-done.3 = bf16[32,24,1664]{2,1,0:T(8,128)(2,1)S(1)} async-done(((bf16[32,24,1664]{2,1,0:T(8,128)(2,1)}), bf16[32,24,1664]{2,1,0:T(8,128)(2,1)S(1)}, u32[]{:S(2)}, u32[]{:S(2)}) %all-to-all-start.3) | async-done | bytes 2555936 | tf_op jit(solution)/shard_map/all_to_all | solution.py:85
  132.3 5.1 collective-permute-start.3
  137.3 10.5 %multiply_convert_fusion.1 = (bf16[2048,768]{1,0:T(8,128)(2,1)S(1)}, f32[2048,768]{1,0:T(8,128)}) fusion(bf16[2,1,768,768]{3,2,1,0:T(8,128)(2,1)} %param.18, bf16[1024,768]{1,0:T(8,128)(2,1)} %collective-permute-done.1, bf16[1024,768]{1,0:T(8,128)(2,1)} %bitcast.201), kind=kOutput, calls=%fused_computation.33 | convolution fusion | flops 2456813568 | bytes 13762560 | tf_op jit(solution)/shard_map/dot_general | solution.py:21
  156.4 7.6 %all-to-all-start.2 = ((bf16[64,16,768]{2,1,0:T(8,128)(2,1)}), bf16[64,16,768]{2,1,0:T(8,128)(2,1)}, u32[]{:S(2)}, u32[]{:S(2)}) async-start(bf16[64,16,768]{2,1,0:T(8,128)(2,1)} %bitcast.190), calls=%async_computation.2 | async-start | bytes 3145728 | tf_op jit(solution)/shard_map/all_to_all | solution.py:41
  165.8 4.4 broadcast_select_fusion
  171.3 15.7 %all-to-all-done.2 = bf16[64,16,768]{2,1,0:T(8,128)(2,1)} async-done(((bf16[64,16,768]{2,1,0:T(8,128)(2,1)}), bf16[64,16,768]{2,1,0:T(8,128)(2,1)}, u32[]{:S(2)}, u32[]{:S(2)}) %all-to-all-start.2) | async-done | bytes 1572896 | tf_op jit(solution)/shard_map/all_to_all | solution.py:41
  203.1 4.6 copy.145
  207.8 43.7 %all_to_all.93 = bf16[64,16,1536]{2,1,0:T(8,128)(2,1)S(1)} all-to-all(bf16[64,16,1536]{2,1,0:T(8,128)(2,1)} %bitcast.186), channel_id=1, replica_groups=mesh['ea'=32,'half'=2,'core'=2] {'ea','half'}, dimensions={0} | all-to-all | bytes 6291456 | tf_op jit(solution)/shard_map/all_to_all | solution.py:41
  255.3 5.3 collective-permute-done.4
  260.6 9.6 %multiply_convert_fusion = (bf16[2048,768]{1,0:T(8,128)(2,1)S(1)}, f32[2048,768]{1,0:T(8,128)}) fusion(bf16[2,1,768,768]{3,2,1,0:T(8,128)(2,1)S(1)} %copy-done.118, bf16[1024,1536]{1,0:T(8,128)(2,1)S(1)} %bitcast.196, bf16[1024,1536]{1,0:T(8,128)(2,1)S(1)} %collective-permute-done.4), kind=kOutput, calls=%fused_computation.32 | convolution fusion | flops 2456813568 | bytes 16908288 | tf_op jit(solution)/shard_map/dot_general | solution.py:21
  272.9 10.1 %fusion.17 = bf16[2048,768]{1,0:T(8,128)(2,1)S(1)} fusion(f32[2048,768]{1,0:T(8,128)} %get-tuple-element.142, bf16[2,1,768,768]{3,2,1,0:T(8,128)(2,1)S(1)} %copy-done.116, bf16[1024,1536]{1,0:T(8,128)(2,1)S(1)} %collective-permute-done.4, bf16[1024,1536]{1,0:T(8,128)(2,1)S(1)} %bitcast.197), kind=kOutput, calls=%fused_computation.24 | convolution fusion | flops 2461532160 | bytes 16908288 | tf_op jit(solution)/shard_map/dot_general | solution.py:21
  288.7 5.3 collective-permute-done.5
  296.4 4.6 copy.146
  301.0 5.6 all-to-all-start.5
  306.7 39.9 %all-to-all-done.5 = bf16[64,16,1536]{2,1,0:T(8,128)(2,1)} async-done(((bf16[64,16,1536]{2,1,0:T(8,128)(2,1)}), bf16[64,16,1536]{2,1,0:T(8,128)(2,1)}, u32[]{:S(2)}, u32[]{:S(2)}) %all-to-all-start.5) | async-done | bytes 3145760 | tf_op jit(solution)/shard_map/all_to_all | solution.py:41
  363.2 4.6 fusion.79
  373.9 28.2 %all_to_all.94 = bf16[64,16,768]{2,1,0:T(8,128)(2,1)S(1)} all-to-all(bf16[64,16,768]{2,1,0:T(8,128)(2,1)S(1)} %bitcast.207), channel_id=1, replica_groups=mesh['ea'=32,'half'=2,'core'=2] {'ea','half'}, dimensions={0} | all-to-all | bytes 3145728 | tf_op jit(solution)/shard_map/all_to_all | solution.py:41
  408.2 8.6 %fusion.10 = bf16[2048,768]{1,0:T(8,128)(2,1)S(1)} fusion(f32[2048,768]{1,0:T(8,128)S(1)} %bitcast.245, bf16[1024,768]{1,0:T(8,128)(2,1)S(1)} %collective-permute-done.6, bf16[1024,768]{1,0:T(8,128)(2,1)S(1)} %bitcast.204, bf16[2,1,768,768]{3,2,1,0:T(8,128)(2,1)S(1)} %copy-done.117), kind=kOutput, calls=%fused_computation.17 | convolution fusion | flops 2461532160 | bytes 13762560 | tf_op jit(solution)/shard_map/dot_general | solution.py:21
  431.7 5.2 all-to-all-start.7
  444.3 15.9 %all-to-all-done.7 = bf16[64,16,768]{2,1,0:T(8,128)(2,1)S(1)} async-done(((bf16[64,16,768]{2,1,0:T(8,128)(2,1)}), bf16[64,16,768]{2,1,0:T(8,128)(2,1)S(1)}, u32[]{:S(2)}, u32[]{:S(2)}) %all-to-all-start.7) | async-done | bytes 1572896 | tf_op jit(solution)/shard_map/all_to_all | solution.py:41
  467.9 4.6 fusion.70
  472.5 4.6 fusion.73
  479.1 4.7 fusion.137
  495.5 4.5 all-to-all-start.9
  500.0 7.1 %convolution_bitcast_fusion = f32[1,768,768]{2,1,0:T(8,128)} fusion(bf16[2048,768]{1,0:T(8,128)(2,1)} %copy-done.128, bf16[1024,1536]{1,0:T(8,128)(2,1)} %copy-done.113, bf16[1024,1536]{1,0:T(8,128)(2,1)} %bitcast.198), kind=kOutput, calls=%fused_computation.96 | convolution fusion | flops 2422210560 | bytes 11796480 | tf_op jit(solution)/shard_map/dot_general | solution.py:21
  515.2 20.3 %all-to-all-done.9 = bf16[32,24,1664]{2,1,0:T(8,128)(2,1)S(1)} async-done(((bf16[32,24,1664]{2,1,0:T(8,128)(2,1)}), bf16[32,24,1664]{2,1,0:T(8,128)(2,1)S(1)}, u32[]{:S(2)}, u32[]{:S(2)}) %all-to-all-start.9) | async-done | bytes 2555936 | tf_op jit(solution)/shard_map/all_to_all | solution.py:104
  537.0 5.5 all-to-all-start.8
  542.5 5.6 fusion.59
  557.1 19.5 %collective-permute-done.12 = f32[24,1664]{1,0:T(8,128)S(1)} collective-permute-done((f32[24,1664]{1,0:T(8,128)S(1)}, f32[24,1664]{1,0:T(8,128)S(1)}, u32[]{:S(2)}, u32[]{:S(2)}) %collective-permute-start.12) | collective-permute-done | bytes 159776 | tf_op jit(solution)/shard_map/ppermute | solution.py:37
  (467 shorter events, 181.0 us)
Async XLA Ops:
  5.9 44.2 %copy-start.110 = (s32[2,197,2]{1,2,0:T(2,128)S(1)}, s32[2,197,2]{1,2,0:T(2,128)}, u32[]{:S(2)}) copy-start(s32[2,197,2]{1,2,0:T(2,128)} %param.12) | copy-start | bytes 9460
  5.9 44.8 %copy-start.31 = (bf16[197,768]{1,0:T(8,128)(2,1)S(1)}, bf16[197,768]{1,0:T(8,128)(2,1)}, u32[]{:S(2)}) copy-start(bf16[197,768]{1,0:T(8,128)(2,1)} %param.10) | copy-start | bytes 907780
  47.4 7.3 %collective-permute-start = (bf16[768,1664]{1,0:T(8,128)(2,1)S(1)}, bf16[768,1664]{1,0:T(8,128)(2,1)}, u32[]{:S(2)}, u32[]{:S(2)}) collective-permute-start(bf16[768,1664]{1,0:T(8,128)(2,1)S(1)} %bitcast.188), channel_id=1, source_target_pairs={{0,1},{1,0},{2,3},{3,2},{4,5},{5,4},{6,7},{7,6},{8,9},{9,8},{10,11... | collective-permute-start | bytes 7667720 | tf_op jit(solution)/shard_map/ppermute | solution.py:33
  50.3 136.7 %copy-start.78 = (s32[1024]{0:T(1024)}, s32[1024]{0:T(1024)S(1)}, u32[]{:S(2)}) copy-start(s32[1024]{0:T(1024)S(1)} %and_subtract_fusion) | copy-start | bytes 12292
  63.7 125.5 %copy-start.15 = (f32[197,768]{1,0:T(8,128)}, f32[197,768]{1,0:T(8,128)S(1)}, u32[]{:S(2)}) copy-start(f32[197,768]{1,0:T(8,128)S(1)} %get-tuple-element.130) | copy-start | bytes 1815556
  64.2 99.8 %copy-start.22 = (bf16[197,768]{1,0:T(8,128)(2,1)}, bf16[197,768]{1,0:T(8,128)(2,1)S(1)}, u32[]{:S(2)}) copy-start(bf16[197,768]{1,0:T(8,128)(2,1)S(1)} %add_convert_fusion.5) | copy-start | bytes 907780
  66.0 29.4 %all-to-all-start.1 = ((bf16[64,16,768]{2,1,0:T(8,128)(2,1)}), bf16[64,16,768]{2,1,0:T(8,128)(2,1)S(1)}, u32[]{:S(2)}, u32[]{:S(2)}) async-start(bf16[64,16,768]{2,1,0:T(8,128)(2,1)} %bitcast.18), calls=%async_computation.1 | async-start | bytes 3145728 | tf_op jit(solution)/shard_map/all_to_all | solution.py:41
  97.4 34.9 %all-to-all-start.3 = ((bf16[32,24,1664]{2,1,0:T(8,128)(2,1)}), bf16[32,24,1664]{2,1,0:T(8,128)(2,1)S(1)}, u32[]{:S(2)}, u32[]{:S(2)}) async-start(bf16[32,24,1664]{2,1,0:T(8,128)(2,1)} %broadcast_in_dim.9), calls=%async_computation.3 | async-start | bytes 5111808 | tf_op jit(solution)/shard_map/all_to_all | solution.py:85
  101.4 35.9 %collective-permute-start.1 = (bf16[1024,768]{1,0:T(8,128)(2,1)}, bf16[1024,768]{1,0:T(8,128)(2,1)}, u32[]{:S(2)}, u32[]{:S(2)}) collective-permute-start(bf16[1024,768]{1,0:T(8,128)(2,1)} %bitcast.200), channel_id=1, source_target_pairs={{0,1},{1,0},{2,3},{3,2},{4,5},{5,4},{6,7},{7,6},{8,9},{9,8},{10,11... | collective-permute-start | bytes 4718600 | tf_op jit(solution)/shard_map/ppermute | solution.py:33
  132.3 33.6 %collective-permute-start.3 = (bf16[768,1664]{1,0:T(8,128)(2,1)S(1)}, bf16[768,1664]{1,0:T(8,128)(2,1)}, u32[]{:S(2)}, u32[]{:S(2)}) collective-permute-start(bf16[768,1664]{1,0:T(8,128)(2,1)S(1)} %bitcast.187), channel_id=1, source_target_pairs={{0,1},{1,0},{2,3},{3,2},{4,5},{5,4},{6,7},{7,6},{8,9},{9,8},{10,11... | collective-permute-start | bytes 7667720 | tf_op jit(solution)/shard_map/ppermute | solution.py:33
  150.6 4.2 collective-permute-start.2
  156.4 30.6 %all-to-all-start.2 = ((bf16[64,16,768]{2,1,0:T(8,128)(2,1)}), bf16[64,16,768]{2,1,0:T(8,128)(2,1)}, u32[]{:S(2)}, u32[]{:S(2)}) async-start(bf16[64,16,768]{2,1,0:T(8,128)(2,1)} %bitcast.190), calls=%async_computation.2 | async-start | bytes 3145728 | tf_op jit(solution)/shard_map/all_to_all | solution.py:41
  165.8 23.5 %copy-start.87 = (f32[197]{0:T(256)}, f32[197]{0:T(256)S(1)}, u32[]{:S(2)}) copy-start(f32[197]{0:T(256)S(1)} %get-tuple-element.76) | copy-start | bytes 2368
  207.8 52.8 %copy-start.118 = (bf16[2,1,768,768]{3,2,1,0:T(8,128)(2,1)S(1)}, bf16[2,1,768,768]{3,2,1,0:T(8,128)(2,1)}, u32[]{:S(2)}) copy-start(bf16[2,1,768,768]{3,2,1,0:T(8,128)(2,1)} %param.18) | copy-start | bytes 7077892
  251.4 9.1 %collective-permute-start.4 = (bf16[1024,1536]{1,0:T(8,128)(2,1)S(1)}, bf16[1024,1536]{1,0:T(8,128)(2,1)S(1)}, u32[]{:S(2)}, u32[]{:S(2)}) collective-permute-start(bf16[1024,1536]{1,0:T(8,128)(2,1)S(1)} %bitcast.195), channel_id=1, source_target_pairs={{0,1},{1,0},{2,3},{3,2},{4,5},{5,4},{6,7},{7,6},{8,9},{9,8},{10,11... | collective-permute-start | bytes 9437192 | tf_op jit(solution)/shard_map/ppermute | solution.py:33
  287.8 6.1 %collective-permute-start.5 = (bf16[1024,1536]{0,1:T(8,128)(2,1)S(1)}, bf16[1024,1536]{0,1:T(8,128)(2,1)S(1)}, u32[]{:S(2)}, u32[]{:S(2)}) collective-permute-start(bf16[1024,1536]{0,1:T(8,128)(2,1)S(1)} %fusion.21), channel_id=1, source_target_pairs={{0,1},{1,0},{2,3},{3,2},{4,5},{5,4},{6,7},{7,6},{8,9},{9,8},{10,11... | collective-permute-start | bytes 9437192 | tf_op jit(solution)/shard_map/ppermute | solution.py:33
  301.0 45.5 %all-to-all-start.5 = ((bf16[64,16,1536]{2,1,0:T(8,128)(2,1)}), bf16[64,16,1536]{2,1,0:T(8,128)(2,1)}, u32[]{:S(2)}, u32[]{:S(2)}) async-start(bf16[64,16,1536]{2,1,0:T(8,128)(2,1)} %bitcast.185), calls=%async_computation.5 | async-start | bytes 6291456 | tf_op jit(solution)/shard_map/all_to_all | solution.py:41
  367.9 40.3 %slice-start.4 = ((s8[6291456]{0:T(1024)(128)(4,1)}), s8[4194304]{0:T(1024)(128)(4,1)S(1)}, s32[]{:S(2)}) async-start(s8[6291456]{0:T(1024)(128)(4,1)} %bitcast.244), calls=%async_computation.14 | async-start | bytes 8388608
  372.0 36.1 %slice-start.5 = ((s8[6291456]{0:T(1024)(128)(4,1)}), s8[2097152]{0:T(1024)(128)(4,1)S(1)}, s32[]{:S(2)}) async-start(s8[6291456]{0:T(1024)(128)(4,1)} %bitcast.244), calls=%async_computation.15 | async-start | bytes 4194304
  373.8 34.3 %copy-start.117 = (bf16[2,1,768,768]{3,2,1,0:T(8,128)(2,1)S(1)}, bf16[2,1,768,768]{3,2,1,0:T(8,128)(2,1)}, u32[]{:S(2)}) copy-start(bf16[2,1,768,768]{3,2,1,0:T(8,128)(2,1)} %param.19) | copy-start | bytes 7077892
  402.1 6.0 %collective-permute-start.6 = (bf16[1024,768]{1,0:T(8,128)(2,1)S(1)}, bf16[1024,768]{1,0:T(8,128)(2,1)S(1)}, u32[]{:S(2)}, u32[]{:S(2)}) collective-permute-start(bf16[1024,768]{1,0:T(8,128)(2,1)S(1)} %bitcast.203), channel_id=1, source_target_pairs={{0,1},{1,0},{2,3},{3,2},{4,5},{5,4},{6,7},{7,6},{8,9},{9,8},{10,11... | collective-permute-start | bytes 4718600 | tf_op jit(solution)/shard_map/ppermute | solution.py:33
  423.6 5.2 collective-permute-start.7
  431.7 28.5 %all-to-all-start.7 = ((bf16[64,16,768]{2,1,0:T(8,128)(2,1)}), bf16[64,16,768]{2,1,0:T(8,128)(2,1)S(1)}, u32[]{:S(2)}, u32[]{:S(2)}) async-start(bf16[64,16,768]{2,1,0:T(8,128)(2,1)} %bitcast.57), calls=%async_computation.7 | async-start | bytes 3145728 | tf_op jit(solution)/shard_map/all_to_all | solution.py:41
  443.3 48.2 %collective-permute-start.11 = (bf16[768,1664]{1,0:T(8,128)(2,1)}, bf16[768,1664]{1,0:T(8,128)(2,1)}, u32[]{:S(2)}, u32[]{:S(2)}) collective-permute-start(bf16[768,1664]{1,0:T(8,128)(2,1)} %constant_dynamic-slice_fusion), channel_id=1, source_target_pairs={{0,1},{1,0},{2,3},{3,2},{4,5},{5,4},{6,7},{7,6},{8,9},{9,8},{10,11... | collective-permute-start | bytes 7667720 | tf_op jit(solution)/shard_map/ppermute | solution.py:33
  489.9 21.5 %collective-permute-start.8 = (bf16[768,1664]{1,0:T(8,128)(2,1)}, bf16[768,1664]{1,0:T(8,128)(2,1)}, u32[]{:S(2)}, u32[]{:S(2)}) collective-permute-start(bf16[768,1664]{1,0:T(8,128)(2,1)} %constant_dynamic-slice_fusion.1), channel_id=1, source_target_pairs={{0,1},{1,0},{2,3},{3,2},{4,5},{5,4},{6,7},{7,6},{8,9},{9,8},{10,11... | collective-permute-start | bytes 7667720 | tf_op jit(solution)/shard_map/ppermute | solution.py:33
  495.5 40.0 %all-to-all-start.9 = ((bf16[32,24,1664]{2,1,0:T(8,128)(2,1)}), bf16[32,24,1664]{2,1,0:T(8,128)(2,1)S(1)}, u32[]{:S(2)}, u32[]{:S(2)}) async-start(bf16[32,24,1664]{2,1,0:T(8,128)(2,1)} %bitcast.189), calls=%async_computation.9 | async-start | bytes 5111808 | tf_op jit(solution)/shard_map/all_to_all | solution.py:104
  537.0 43.8 %all-to-all-start.8 = ((bf16[32,24,1664]{2,1,0:T(8,128)(2,1)}), bf16[32,24,1664]{2,1,0:T(8,128)(2,1)S(1)}, u32[]{:S(2)}, u32[]{:S(2)}) async-start(bf16[32,24,1664]{2,1,0:T(8,128)(2,1)} %bitcast.67), calls=%async_computation.8 | async-start | bytes 5111808 | tf_op jit(solution)/shard_map/all_to_all | solution.py:104
  552.8 25.4 %copy-start.38 = (f32[1,768,768]{2,1,0:T(8,128)S(1)}, f32[1,768,768]{2,1,0:T(8,128)}, u32[]{:S(2)}) copy-start(f32[1,768,768]{2,1,0:T(8,128)} %convolution_bitcast_fusion) | copy-start | bytes 7077892
  552.8 23.8 %collective-permute-start.12 = (f32[24,1664]{1,0:T(8,128)S(1)}, f32[24,1664]{1,0:T(8,128)S(1)}, u32[]{:S(2)}, u32[]{:S(2)}) collective-permute-start(f32[24,1664]{1,0:T(8,128)S(1)} %convert_reduce_fusion), channel_id=1, source_target_pairs={{0,2},{2,0},{1,3},{3,1},{4,6},{6,4},{5,7},{7,5},{8,10},{10,8},{9,1... | collective-permute-start | bytes 479240 | tf_op jit(solution)/shard_map/ppermute | solution.py:37
  576.6 4.1 collective-permute-start.13
  581.1 7.3 %collective-permute-start.9 = (f32[24,1664]{1,0:T(8,128)S(1)}, f32[24,1664]{1,0:T(8,128)S(1)}, u32[]{:S(2)}, u32[]{:S(2)}) collective-permute-start(f32[24,1664]{1,0:T(8,128)S(1)} %convert_reduce_fusion.1), channel_id=1, source_target_pairs={{0,2},{2,0},{1,3},{3,1},{4,6},{6,4},{5,7},{7,5},{8,10},{10,8},{9,1... | collective-permute-start | bytes 479240 | tf_op jit(solution)/shard_map/ppermute | solution.py:37
  588.5 2.0 collective-permute-start.10
  (126 other events, 569.5 us)

commit v2 on v1

v2 whole, which is shorter than its diff:
```python
import jax
import jax.numpy as jnp
from jax import lax
from jax.experimental import pallas as pl
from jax.experimental.pallas import tpu as pltpu
from jax.sharding import Mesh
from jax.sharding import PartitionSpec as P

HEADS = 12
HEAD = 64
SEQ = 197
LAYERS = 2
EPS = 1e-06
HIGH = lax.Precision.HIGHEST
BF = jnp.bfloat16
F32 = jnp.float32
SLOTS = 16
SCALE = HEAD ** (-0.5)
GROUP = ("ea", "half")


def dot(a, b, dims=((1,), (0,))):
    return lax.dot_general(a, b, (dims, ((), ())), preferred_element_type=F32)


def dot_nt(a, b):
    return dot(a, b, ((1,), (1,)))


def dot_tn(a, b):
    return dot(a, b, ((0,), (0,)))


def swap_core(value):
    return lax.ppermute(value, "core", [(0, 1), (1, 0)])


def swap_half(value):
    return lax.ppermute(value, "half", [(0, 1), (1, 0)])


def exchange(rows):
    return lax.all_to_all(rows, GROUP, split_axis=0, concat_axis=0, tiled=True)


def gelu_parts(x):
    mag = jnp.abs(x)
    t = 1.0 / (1.0 + (0.3275911 * 0.7071067811865476) * mag)
    bell = jnp.exp(-0.5 * x * x)
    poly = 0.5 * t * (
        0.254829592
        + t * (-0.284496736 + t * (1.421413741 + t * (-1.453152027 + t * 1.061405429)))
    )
    tail = poly * bell
    cdf = jnp.where(x < 0, tail, 1.0 - tail)
    return cdf, cdf + x * bell * 0.3989422804014327


def normalize(x, gain, bias):
    center = jnp.mean(x, axis=-1, keepdims=True)
    shifted = x - center
    spread = jnp.mean(shifted * shifted, axis=-1, keepdims=True)
    inv = lax.rsqrt(spread + EPS)
    unit = shifted * inv
    return unit * gain + bias, unit, inv


def normalize_back(grad, unit, inv, gain):
    scaled = grad * gain
    mean_a = jnp.mean(scaled, axis=-1, keepdims=True)
    mean_b = jnp.mean(scaled * unit, axis=-1, keepdims=True)
    return (
        inv * (scaled - mean_a - unit * mean_b),
        jnp.sum(grad * unit, axis=0),
        jnp.sum(grad, axis=0),
    )


def heads_of(matrix):
    return matrix.reshape(SEQ, HEADS, HEAD)


def gather_cols(mine, after=None):
    groups = lax.axis_size("ea")
    if after is not None:
        mine, _ = lax.optimization_barrier((mine, after))
    sent = jnp.broadcast_to(mine[None], (groups,) + mine.shape)
    got = lax.all_to_all(sent, "ea", split_axis=0, concat_axis=0)
    return got.reshape(-1, mine.shape[1])


def core_half(value, which=0):
    n = value.shape[1] // 2
    core = lax.axis_index("core")
    return lax.dynamic_slice_in_dim(value, (core if which == 0 else 1 - core) * n, n, 1)


def in_order(own, other):
    first = lax.axis_index("core") == 0
    return jnp.concatenate(
        [jnp.where(first, own, other), jnp.where(first, other, own)], axis=1
    )


def thirds(value):
    n = value.shape[1] // 3
    return [value[:, i * n : (i + 1) * n] for i in range(3)]


def core_dense(qkv, out, small):
    return jnp.concatenate([core_half(part) for part in thirds(qkv)] + [core_half(out), small], axis=1)


def split_dense(own, experts):
    other = swap_core(own[:, :1536])
    small = own[:, 1536:]
    norms = small[:, experts : experts + 4].astype(F32).T
    return (
        (own[:, :1152], other[:, :1152]),
        (own[:, 1152:1536], other[:, 1152:]),
        small,
        norms,
    )


def sum_send(grad_qkv, grad_out, small):
    give = [grad_qkv[1].astype(BF), grad_out[1].astype(BF), small.astype(BF)]
    own = [grad_qkv[0], grad_out[0], small]
    return jnp.concatenate(
        [(o + swap_core(g).astype(F32)).astype(BF) for o, g in zip(own, give)], axis=1
    )


def sum_exchange(pair, after=None):
    groups = lax.axis_size("ea")
    if after is not None:
        pair, _ = lax.optimization_barrier((pair, after))
    return lax.all_to_all(
        pair.reshape(groups, -1, pair.shape[1]), "ea", split_axis=0, concat_axis=0
    )


def sum_finish(parts):
    part = jnp.sum(parts.astype(F32), axis=0)
    full = part + swap_half(part)
    other = swap_core(full[:, :1536])
    qkv = [
        in_order(own, more) for own, more in zip(thirds(full[:, :1152]), thirds(other[:, :1152]))
    ]
    return (
        jnp.concatenate(qkv, axis=1),
        in_order(full[:, 1152:1536], other[:, 1152:]),
        full[:, 1536:],
    )


def pad_cols(value, cols):
    return jnp.pad(value, ((0, 0), (0, cols - value.shape[1])))


def softmax_rows(scores):
    expo = jnp.exp(scores - jnp.max(scores, axis=-1, keepdims=True))
    return expo * (1.0 / jnp.sum(expo, axis=-1, keepdims=True))


def place(core, side, start, size):
    half = core if side == 0 else 1 - core
    return pl.ds(pl.multiple_of(half * 384 + start, 128), size)


def masked(pair, j):
    lane = lax.broadcasted_iota(jnp.int32, pair.shape, 1)
    return jnp.where((lane < HEAD) == (j == 0), pair, jnp.zeros_like(pair))


def merge(first, second):
    lane = lax.broadcasted_iota(jnp.int32, first.shape, 1)
    return jnp.where(lane < HEAD, first, second)


def attend_kernel(
    core_ref, state, norms, qkv_o, qkv_x, out_o, out_x, small, normed, proj_o, proj_x, mixed, after,
    normed_two, logits,
):
    core = core_ref[0]
    wide, _, _ = normalize(state[...], norms[0:1, :], norms[2:3, :])
    normed[...] = wide.astype(BF)
    for side, weight, proj in ((0, qkv_o, proj_o), (1, qkv_x, proj_x)):
        proj[...] = dot(normed[...], weight[...]).astype(BF)
        for at in range(0, 384, 128):
            query, key_part, value_part = (proj[:, i * 384 + at : i * 384 + at + 128] for i in range(3))
            found = []
            for j in range(2):
                shares = softmax_rows(dot_nt(masked(query, j), key_part) * SCALE)
                found.append(dot(shares.astype(BF), value_part))
            mixed[:, place(core, side, at, 128)] = merge(*found).astype(BF)
    for side, weight in ((0, out_o), (1, out_x)):
        cols = place(core, side, 0, 384)
        after[:, cols] = state[:, cols] + dot(mixed[...], weight[...])
    wide, _, _ = normalize(after[...], norms[1:2, :], norms[3:4, :])
    normed_two[...] = wide.astype(BF)
    logits[...] = dot(normed_two[...], small[...])


def attend_back_kernel(
    core_ref, grad, grad_two, state, after, norms, proj_o, proj_x, qkv_o, qkv_x, out_o, out_x,
    grad_in, grad_attn, gp_o, gp_x, stats, grad_mixed,
):
    core = core_ref[0]
    _, unit, inv = normalize(after[...], norms[1:2, :], norms[3:4, :])
    part, gain_two, bias_two = normalize_back(grad_two[...], unit, inv, norms[1:2, :])
    grad_in[...] = grad[...] + part
    grad_attn[...] = grad_in[...].astype(BF)
    grad_mixed[...] = sum(
        dot_nt(grad_attn[:, place(core, side, 0, 384)], weight[...])
        for side, weight in ((0, out_o), (1, out_x))
    ).astype(BF)
    for side, proj, gp in ((0, proj_o, gp_o), (1, proj_x, gp_x)):
        for at in range(0, 384, 128):
            query, key_part, value_part = (proj[:, i * 384 + at : i * 384 + at + 128] for i in range(3))
            outer = grad_mixed[:, place(core, side, at, 128)]
            found = []
            for j in range(2):
                shares = softmax_rows(dot_nt(masked(query, j), key_part) * SCALE)
                grad_shares = dot_nt(masked(outer, j), value_part)
                inner = jnp.sum(grad_shares * shares, axis=-1, keepdims=True)
                raw = (shares * (grad_shares - inner) * SCALE).astype(BF)
                found.append(
                    (dot(raw, key_part), dot_tn(raw, query), dot_tn(shares.astype(BF), outer))
                )
            for i in range(3):
                gp[:, i * 384 + at : i * 384 + at + 128] = merge(found[0][i], found[1][i]).astype(BF)
    grad_normed = dot_nt(gp_o[...], qkv_o[...]) + dot_nt(gp_x[...], qkv_x[...])
    _, unit, inv = normalize(state[...], norms[0:1, :], norms[2:3, :])
    part, gain_one, bias_one = normalize_back(grad_normed, unit, inv, norms[0:1, :])
    grad_in[...] = grad_in[...] + part
    for i, row in enumerate((gain_one, gain_two, bias_one, bias_two)):
        stats[i : i + 1, :] = row[None, :]


def whole_call(kernel, args, outs, flops, scratch=()):
    core = lax.axis_index("core").astype(jnp.int32).reshape(1)
    vmem = pl.BlockSpec(memory_space=pltpu.VMEM)
    return pl.pallas_call(
        kernel,
        in_specs=[pl.BlockSpec(memory_space=pltpu.SMEM)] + [vmem] * len(args),
        out_specs=[vmem] * len(outs),
        out_shape=[jax.ShapeDtypeStruct(shape, kind) for shape, kind in outs],
        scratch_shapes=list(scratch),
        compiler_params=pltpu.CompilerParams(vmem_limit_bytes=48 * 1024 * 1024),
        cost_estimate=pl.CostEstimate(flops=flops, bytes_accessed=8 << 20, transcendentals=0),
    )(core, *args)


def attention(state, dense):
    qkv_w, out_w, small, norms = dense
    tokens, width = state.shape
    rows = lambda n, kind: ((tokens, n), kind)
    normed, proj_o, proj_x, mixed, after, normed_two, logits = whole_call(
        attend_kernel,
        [state, norms, *qkv_w, *out_w, small],
        [
            rows(width, BF), rows(1152, BF), rows(1152, BF), rows(width, BF), rows(width, F32),
            rows(width, BF), rows(128, F32),
        ],
        4 * tokens * width * (4 * width + 4 * tokens),
    )
    return after, normed_two, logits, (state, normed, proj_o, proj_x, mixed, after)


def attention_back(grad, grad_two, kept, dense):
    state, normed, proj_o, proj_x, mixed, after = kept
    qkv_w, out_w, _, norms = dense
    tokens, width = grad.shape
    rows = lambda n, kind: ((tokens, n), kind)
    grad_in, grad_attn, gp_o, gp_x, stats = whole_call(
        attend_back_kernel,
        [grad, grad_two, state, after, norms, proj_o, proj_x, *qkv_w, *out_w],
        [rows(width, F32), rows(width, BF), rows(1152, BF), rows(1152, BF), ((4, width), F32)],
        8 * tokens * width * (4 * width + 8 * tokens),
        [pltpu.VMEM((tokens, width), BF)],
    )
    return grad_in, stats, (normed, gp_o, gp_x, mixed, grad_attn)


def dense_grads(normed, gp_o, gp_x, mixed, grad_attn):
    grad_out = [dot_tn(mixed, core_half(grad_attn, which)) for which in (0, 1)]
    return [dot_tn(normed, gp_o), dot_tn(normed, gp_x)], grad_out


def forward_kernel(rows, w_in, w_out, hidden, slope, part):
    pre = dot(rows[...], w_in[...])
    cdf, steep = gelu_parts(pre)
    hidden[...] = (pre * cdf).astype(BF)
    slope[...] = steep.astype(BF)
    part[...] = dot(hidden[...], w_out[...]).astype(BF)


def backward_kernel(grows, slope, w_in, w_out, grad_pre, part):
    grad_hidden = dot_nt(grows[...], w_out[...])
    grad_pre[...] = (grad_hidden * slope[...].astype(F32)).astype(BF)
    part[...] = dot_nt(grad_pre[...], w_in[...]).astype(BF)


def both_kernel(rows, w_in, w_out, hidden, grad_pre, part):
    width = w_in.shape[0]
    pre = dot(rows[:, :width], w_in[...])
    cdf, steep = gelu_parts(pre)
    hidden[...] = (pre * cdf).astype(BF)
    part[:, :width] = dot(hidden[...], w_out[...]).astype(BF)
    grad_hidden = dot_nt(rows[:, width:], w_out[...])
    grad_pre[...] = (grad_hidden * steep).astype(BF)
    part[:, width:] = dot_nt(grad_pre[...], w_in[...]).astype(BF)


BLOCK = 512


def expert_call(kernel, row_args, weights, out_widths, products):
    count = row_args[0].shape[0]

    def rows_spec(width):
        return pl.BlockSpec((BLOCK, width), lambda i: (i, 0))

    moved = sum(a.size for a in row_args) + sum(w.size for w in weights) + count * sum(out_widths)
    return pl.pallas_call(
        kernel,
        grid=(count // BLOCK,),
        in_specs=[rows_spec(a.shape[1]) for a in row_args]
        + [pl.BlockSpec(w.shape, lambda i: (0, 0)) for w in weights],
        out_specs=[rows_spec(width) for width in out_widths],
        out_shape=[jax.ShapeDtypeStruct((count, width), BF) for width in out_widths],
        compiler_params=pltpu.CompilerParams(vmem_limit_bytes=48 * 1024 * 1024),
        cost_estimate=pl.CostEstimate(
            flops=2 * count * 768 * 768 * products, bytes_accessed=2 * moved, transcendentals=0
        ),
    )(*row_args, *weights)


def join_cores(part_own, part_other):
    return (part_own.astype(F32) + swap_core(part_other).astype(F32)).astype(BF)


def routing(chosen, experts):
    tokens = chosen.shape[0]
    flat = jnp.concatenate([chosen[:, 0], chosen[:, 1]])
    onehot = flat[:, None] == jnp.arange(experts, dtype=jnp.int32)[None, :]
    pairs = 2 * tokens
    earlier = (
        lax.broadcasted_iota(jnp.int32, (pairs, pairs), 1)
        < lax.broadcasted_iota(jnp.int32, (pairs, pairs), 0)
    ).astype(BF)
    onehot = onehot.astype(F32)
    before = dot(earlier, onehot.astype(BF))
    position = jnp.sum(before * onehot, axis=1).astype(jnp.int32)
    code = flat * (2 * SLOTS) + position
    slots = experts * 2 * SLOTS
    row_code = lax.broadcasted_iota(jnp.int32, (slots, pairs), 0)
    row_code = row_code - jnp.where(lax.rem(row_code, 2 * SLOTS) >= SLOTS, SLOTS, 0)
    send = (row_code == code[None, :]).astype(BF)
    col_code = lax.broadcasted_iota(jnp.int32, (pairs, slots), 1)
    col_code = col_code - jnp.where(lax.rem(col_code, 2 * SLOTS) >= SLOTS, SLOTS, 0)
    fetch = (col_code == code[:, None]).astype(BF)
    return onehot, send, fetch


def router_forward(logits, onehot):
    router = jax.nn.softmax(logits, axis=-1)
    tokens = router.shape[0]
    gate = [
        jnp.sum(onehot[j * tokens : (j + 1) * tokens] * router, axis=1, keepdims=True)
        for j in range(2)
    ]
    return router, gate


def router_back(grad, picked, router, onehot, normed_two, router_w):
    tokens = router.shape[0]
    grad_router = 0.0
    for j in range(2):
        part = jnp.sum(grad * picked[j], axis=1, keepdims=True)
        grad_router = grad_router + onehot[j * tokens : (j + 1) * tokens] * part
    grad_logit = router * (grad_router - jnp.sum(grad_router * router, axis=-1, keepdims=True))
    grad_normed = jnp.dot(grad_logit, router_w.astype(F32).T, precision=HIGH)
    grad_router_w = jnp.dot(normed_two.astype(F32).T, grad_logit, precision=HIGH)
    return grad_normed, grad_router_w


def small_grads(grad_router_w, stats):
    return pad_cols(jnp.concatenate([grad_router_w, stats.T], axis=1), 128)


def per_device(
    image_tokens,
    cotangent,
    routes,
    norm_gains,
    norm_biases,
    qkv_weight,
    out_weight,
    router_weight,
    expert_in,
    expert_out,
):
    tokens, width = image_tokens.shape
    experts = lax.axis_size("ea")
    mine = []
    for b in range(LAYERS):
        small = jnp.concatenate([router_weight[b], norm_gains[b].T, norm_biases[b].T], axis=1)
        mine.append(core_dense(qkv_weight[b], out_weight[b], pad_cols(small, 128)))
    dense0 = split_dense(gather_cols(mine[0]), experts)
    routed = [routing(routes[b], experts) for b in range(LAYERS)]
    w_in = [expert_in[b, 0] for b in range(LAYERS)]
    w_out = [expert_out[b, 0] for b in range(LAYERS)]

    state = image_tokens.astype(F32)
    after0, normed0, logits, kept0 = attention(state, dense0)
    onehot, send, fetch = routed[0]
    router0, gate0 = router_forward(logits[:, :experts], onehot)
    arrived = exchange(dot(send[:, :tokens] + send[:, tokens:], normed0).astype(BF))
    gathered1 = gather_cols(mine[1], after=arrived)
    rows0 = (arrived, swap_core(arrived))
    first = [
        expert_call(forward_kernel, [r], [w_in[0], w_out[0]], [width] * 3, 2) for r in rows0
    ]
    hidden0, slope0, part = zip(*first)
    returned = exchange(join_cores(*part))
    dense1 = split_dense(gathered1, experts)
    picked = dot(fetch, returned)
    picked0 = (picked[:tokens], picked[tokens:])
    state1 = after0 + gate0[0] * picked0[0] + gate0[1] * picked0[1]

    grad = cotangent.astype(F32)
    after1, normed1, logits, kept1 = attention(state1, dense1)
    onehot1, send1, fetch1 = routed[1]
    router1, gate1 = router_forward(logits[:, :experts], onehot1)
    rows = dot(send1[:, :tokens] + send1[:, tokens:], normed1).astype(BF)
    grad_rows = jnp.concatenate([(g * grad).astype(BF) for g in gate1], axis=0)
    grad_rows = dot(send1, grad_rows).astype(BF)
    arrived = exchange(jnp.concatenate([rows, grad_rows], axis=1))
    both = (arrived, swap_core(arrived))
    second = [
        expert_call(both_kernel, [r], [w_in[1], w_out[1]], [width, width, 2 * width], 4)
        for r in both
    ]
    hidden1, grad_pre1, part = zip(*second)
    returned = exchange(join_cores(*part))
    picked = dot(fetch1, returned)
    picked1 = (picked[:tokens, :width], picked[tokens:, :width])
    grad_sent = picked[:tokens, width:] + picked[tokens:, width:]
    block_out = (after1 + gate1[0] * picked1[0] + gate1[1] * picked1[1]).astype(BF)
    grad_w_out1 = sum(dot_tn(h, r[:, width:]) for h, r in zip(hidden1, both))
    grad_w_in1 = sum(dot_tn(r[:, :width], g) for r, g in zip(both, grad_pre1))

    extra, grad_router_w1 = router_back(
        grad, picked1, router1, onehot1, normed1, dense1[2][:, :experts]
    )
    grad, stats1, terms1 = attention_back(grad, grad_sent + extra, kept1, dense1)

    grad_rows = jnp.concatenate([(g * grad).astype(BF) for g in gate0], axis=0)
    arrived = exchange(dot(send, grad_rows).astype(BF))
    grows0 = (arrived, swap_core(arrived))
    third = [
        expert_call(backward_kernel, [r, s], [w_in[0], w_out[0]], [width] * 2, 2)
        for r, s in zip(grows0, slope0)
    ]
    grad_pre0, part = zip(*third)
    pair1 = sum_send(*dense_grads(*terms1), small_grads(grad_router_w1, stats1))
    returned = exchange(join_cores(*part))
    parts1 = sum_exchange(pair1, after=returned)
    picked = dot(fetch, returned)
    grad_sent = picked[:tokens] + picked[tokens:]
    grad_w_out0 = sum(dot_tn(h, g) for h, g in zip(hidden0, grows0))
    grad_w_in0 = sum(dot_tn(r, g) for r, g in zip(rows0, grad_pre0))
    extra, grad_router_w0 = router_back(
        grad, picked0, router0, onehot, normed0, dense0[2][:, :experts]
    )
    grad, stats0, terms0 = attention_back(grad, grad_sent + extra, kept0, dense0)
    terms0, parts1 = lax.optimization_barrier((terms0, parts1))
    pair0 = sum_send(*dense_grads(*terms0), small_grads(grad_router_w0, stats0))
    parts0 = sum_exchange(pair0)
    sums1 = sum_finish(parts1)
    sums0 = sum_finish(parts0)

    qkv_sum, out_sum, small = (jnp.stack(pair) for pair in zip(sums0, sums1))
    return (
        block_out,
        grad,
        small[:, :, experts : experts + 2].transpose(0, 2, 1),
        small[:, :, experts + 2 : experts + 4].transpose(0, 2, 1),
        qkv_sum,
        out_sum,
        small[:, :, :experts],
        jnp.stack([grad_w_in0, grad_w_in1])[:, None],
        jnp.stack([grad_w_out0, grad_w_out1])[:, None],
    )


def solution(mesh):
    fine = Mesh(
        mesh.devices.reshape(mesh.shape["ea"], mesh.shape["row"] // 2, 2), ("ea", "half", "core")
    )
    row = ("half", "core")
    every = ("ea",) + row
    in_specs = (
        P(every, None),
        P(every, None),
        P(None, every, None),
        P(None, None, "ea"),
        P(None, None, "ea"),
        P(None, "ea", None),
        P(None, "ea", None),
        P(None, "ea", None),
        P(None, "ea", None, row),
        P(None, "ea", row, None),
    )
    out_specs = (
        P(every, None),
        P(every, None),
        P(None, None, "ea"),
        P(None, None, "ea"),
        P(None, "ea", None),
        P(None, "ea", None),
        P(None, "ea", None),
        P(None, "ea", None, row),
        P(None, "ea", row, None),
    )
    return jax.shard_map(
        per_device, mesh=fine, in_specs=in_specs, out_specs=out_specs, check_vma=False
    )
```

time: 604 us -> 573 us (0.949)
  Pallas kernels: 0 us -> 80.8 us
  matrix products: 137 us -> 61 us
  waiting for transfers between devices: 185 us -> 118 us
  blocking collectives: 113 us -> 142 us
  local copies, waits for them, and re-layouts: 44.2 us -> 56.5 us
  starting transfers between devices: 67.2 us -> 58.3 us
    pallas_call x0 -> x10, Pallas kernels: none -> 80.8 us  [the longest x6 44.8 us: expert_call(): pl.pallas_call(kernel, grid=(count // BLOCK,), in_specs=[rows_spec(a.shap...]
    dot_general x35 -> x25, matrix products: 105 us -> 57 us  [dot(): return lax.dot_general(a, b, (dims, ((), ())), preferred_element_type=F32)]
    all_to_all x3, waiting for transfers between devices: 49.1 us -> 14.4 us  [the longest x1 11.4 us: gather_cols(): got = lax.all_to_all(sent, 'ea', split_axis=0, concat_axis=0)]
    dot_general x12 -> x0, matrix products: 29.8 us -> none  [the longest x2 9.17 us: attention_back(): jnp.einsum('hqk,qhd->khd', grad_raw, query, preferred_element_type=F32)]
    all_to_all x4 -> x3, waiting for transfers between devices: 94.5 us -> 65.4 us  [exchange(): return lax.all_to_all(rows, GROUP, split_axis=0, concat_axis=0, tiled=True)]
    all_to_all x2 -> x3, blocking collectives: 71.9 us -> 100 us  [exchange(): return lax.all_to_all(rows, GROUP, split_axis=0, concat_axis=0, tiled=True)]
    slice x14 -> x16, local copies, waits for them, and re-layouts: 4.93 us -> 23 us  [the longest x2 5.91 us: split_dense(): other[:, :1152]]
    ppermute x12 -> x16, waiting for transfers between devices: 17.7 us -> 9.36 us  [swap_core(): return lax.ppermute(value, 'core', [(0, 1), (1, 0)])]
  transfers between devices with their start and end apart: 21 -> 24, of which waited for: 13 -> 10; matrix products, arithmetic and copies ran while one was open for 16% -> 17% of each run, Pallas kernels for 0% -> 7%
where the time goes in v2:
time: 573 us; the launch traced here: 562 us
  blocking collectives  142 us (25%)
  waiting for transfers between devices  118 us (21%)
  Pallas kernels  80.8 us (14%)
  matrix products  61 us (11%)
  starting transfers between devices  58.3 us (10%)
  local copies, waits for them, and re-layouts  56.5 us (10%)
  other arithmetic  43.7 us (8%)
    all_to_all x3, blocking collectives, exchange(): return lax.all_to_all(rows, GROUP, split_axis=0, concat_axis=0, tiled=True)  100 us
    all_to_all x3, waiting for transfers between devices, exchange(): return lax.all_to_all(rows, GROUP, split_axis=0, concat_axis=0, tiled=True)  65.4 us
    dot_general x25, matrix products, dot(): return lax.dot_general(a, b, (dims, ((), ())), preferred_element_type=F32)  57 us
    pallas_call x6, Pallas kernels, expert_call(): pl.pallas_call(kernel, grid=(count // BLOCK,), in_specs=[rows_spec(a.shap...  44.8 us
    all_to_all x1, blocking collectives, gather_cols(): got = lax.all_to_all(sent, 'ea', split_axis=0, concat_axis=0)  41.3 us
    pallas_call x4, Pallas kernels, whole_call(): pl.pallas_call(kernel, in_specs=[pl.BlockSpec(memory_space=pltpu.SMEM)] +...  35.9 us
    ppermute x2, waiting for transfers between devices, swap_half(): return lax.ppermute(value, 'half', [(0, 1), (1, 0)])  28.5 us
    ppermute x16, starting transfers between devices, swap_core(): return lax.ppermute(value, 'core', [(0, 1), (1, 0)])  21.4 us
  transfers between devices with their start and end apart: 24, of which 10 were waited for; matrix products, arithmetic and copies ran while one was open for 17% of the time, Pallas kernels for 7%

profile of v2, /device:TPU:1, one launch (start us, length us, event | category | flops | bytes accessed | tf_op | source)
XLA Modules:
  0.0 562.2 jit_solution(4227569873563306023)
XLA Ops:
  7.3 41.3 %all_to_all.89 = bf16[32,24,1664]{2,1,0:T(8,128)(2,1)S(1)} all-to-all(bf16[32,24,1664]{2,1,0:T(8,128)(2,1)S(1)} %broadcast_in_dim.22), channel_id=1, replica_groups=mesh['ea'=32,'half'=2,'core'=2] {'ea'}, dimensions={0} | all-to-all | bytes 5111808 | tf_op jit(solution)/shard_map/all_to_all | solution.py:88
  61.4 6.2 %shard_map.169 = (bf16[197,768]{1,0:T(8,128)(2,1)S(1)}, bf16[197,1152]{1,0:T(8,128)(2,1)S(1)}, bf16[197,1152]{1,0:T(8,128)(2,1)S(1)}, bf16[197,768]{1,0:T(8,128)...) custom-call(s32[1]{0:T(128)} %bitcast.core_ref, ...), custom_call_target="tpu_custom_call" | custom-call | flops 2336010240 | bytes 8388608 | tf_op jit(solution)/shard_map/pallas_call | solution.py:244
  68.3 29.4 %all_to_all.90 = bf16[64,16,768]{2,1,0:T(8,128)(2,1)} all-to-all(bf16[64,16,768]{2,1,0:T(8,128)(2,1)S(1)} %bitcast.140), channel_id=1, replica_groups=mesh['ea'=32,'half'=2,'core'=2] {'ea','half'}, dimensions={0} | all-to-all | bytes 3145728 | tf_op jit(solution)/shard_map/all_to_all | solution.py:43
  101.8 4.8 all-to-all-start.3
  110.7 7.7 %shard_map.171 = (bf16[1024,768]{1,0:T(8,128)(2,1)S(1)}, bf16[1024,768]{1,0:T(8,128)(2,1)S(1)}, bf16[1024,768]{1,0:T(8,128)(2,1)}) custom-call(bf16[1024,768]{1,0:T(8,128)(2,1)} %collective-permute-done.1.rows, bf16[768,768]{1,0:T(8,128)(2,1)S(1)} %get-tuple-element.190.w_in, bf16[768,768]{1,0:T(8,128)(2,1)S(1)} %get-tuple-element.146.w_out), custom_call_target="tpu_custom_call" | custom-call | flops 2415919104 | bytes 8650752 | tf_op jit(solution)/shard_map/pallas_call | solution.py:326
  121.0 7.2 %shard_map.170 = (bf16[1024,768]{1,0:T(8,128)(2,1)S(1)}, bf16[1024,768]{1,0:T(8,128)(2,1)S(1)}, bf16[1024,768]{1,0:T(8,128)(2,1)}) custom-call(bf16[1024,768]{1,0:T(8,128)(2,1)} %bitcast.14.rows, bf16[768,768]{1,0:T(8,128)(2,1)S(1)} %get-tuple-element.190.w_in, bf16[768,768]{1,0:T(8,128)(2,1)S(1)} %get-tuple-element.146.w_out), custom_call_target="tpu_custom_call" | custom-call | flops 2415919104 | bytes 8650752 | tf_op jit(solution)/shard_map/pallas_call | solution.py:326
  130.6 11.4 %all-to-all-done.3 = bf16[32,24,1664]{2,1,0:T(8,128)(2,1)} async-done(((bf16[32,24,1664]{2,1,0:T(8,128)(2,1)}), bf16[32,24,1664]{2,1,0:T(8,128)(2,1)}, u32[]{:S(2)}, u32[]{:S(2)}) %all-to-all-start.3) | async-done | bytes 2555936 | tf_op jit(solution)/shard_map/all_to_all | solution.py:88
  149.1 7.1 %all-to-all-start.2 = ((bf16[64,16,768]{2,1,0:T(8,128)(2,1)}), bf16[64,16,768]{2,1,0:T(8,128)(2,1)}, u32[]{:S(2)}, u32[]{:S(2)}) async-start(bf16[64,16,768]{2,1,0:T(8,128)(2,1)} %bitcast.142), calls=%async_computation.2 | async-start | bytes 3145728 | tf_op jit(solution)/shard_map/all_to_all | solution.py:43
  166.2 13.3 %all-to-all-done.2 = bf16[64,16,768]{2,1,0:T(8,128)(2,1)} async-done(((bf16[64,16,768]{2,1,0:T(8,128)(2,1)}), bf16[64,16,768]{2,1,0:T(8,128)(2,1)}, u32[]{:S(2)}, u32[]{:S(2)}) %all-to-all-start.2) | async-done | bytes 1572896 | tf_op jit(solution)/shard_map/all_to_all | solution.py:43
  187.5 6.3 %shard_map.172 = (bf16[197,768]{1,0:T(8,128)(2,1)S(1)}, bf16[197,1152]{1,0:T(8,128)(2,1)S(1)}, bf16[197,1152]{1,0:T(8,128)(2,1)S(1)}, bf16[197,768]{1,0:T(8,128)...) custom-call(s32[1]{0:T(128)} %bitcast.core_ref, ...), custom_call_target="tpu_custom_call" | custom-call | flops 2336010240 | bytes 8388608 | tf_op jit(solution)/shard_map/pallas_call | solution.py:244
  203.9 43.3 %all_to_all.91 = bf16[64,16,1536]{2,1,0:T(8,128)(2,1)S(1)} all-to-all(bf16[64,16,1536]{2,1,0:T(8,128)(2,1)} %bitcast.136), channel_id=1, replica_groups=mesh['ea'=32,'half'=2,'core'=2] {'ea','half'}, dimensions={0} | all-to-all | bytes 6291456 | tf_op jit(solution)/shard_map/all_to_all | solution.py:43
  251.1 5.3 collective-permute-done.4.rows
  258.0 10.0 %shard_map.174 = (bf16[1024,768]{1,0:T(8,128)(2,1)S(1)}, bf16[1024,768]{1,0:T(8,128)(2,1)S(1)}, bf16[1024,1536]{1,0:T(8,128)(2,1)}) custom-call(bf16[1024,1536]{1,0:T(8,128)(2,1)} %copy-done.109, bf16[768,768]{1,0:T(8,128)(2,1)S(1)} %copy-done.4, bf16[768,768]{1,0:T(8,128)(2,1)S(1)} %copy-done.3), custom_call_target="tpu_custom_call" | custom-call | flops 4831838208 | bytes 11796480 | tf_op jit(solution)/shard_map/pallas_call | solution.py:326
  270.7 10.0 %shard_map.173 = (bf16[1024,768]{1,0:T(8,128)(2,1)S(1)}, bf16[1024,768]{1,0:T(8,128)(2,1)S(1)}, bf16[1024,1536]{1,0:T(8,128)(2,1)}) custom-call(bf16[1024,1536]{1,0:T(8,128)(2,1)} %bitcast.144, bf16[768,768]{1,0:T(8,128)(2,1)S(1)} %copy-done.4, bf16[768,768]{1,0:T(8,128)(2,1)S(1)} %copy-done.3), custom_call_target="tpu_custom_call" | custom-call | flops 4831838208 | bytes 11796480 | tf_op jit(solution)/shard_map/pallas_call | solution.py:326
  280.7 5.7 %add_convert_fusion = bf16[1024,1536]{1,0:T(8,128)(2,1)} fusion(bf16[1024,1536]{1,0:T(8,128)(2,1)S(1)} %collective-permute-done.5, bf16[1024,1536]{1,0:T(8,128)(2,1)} %get-tuple-element.66), kind=kLoop, calls=%fused_computation | loop fusion | flops 6291456 | bytes 9437184 | tf_op jit(solution)/shard_map/convert_element_type | solution.py:341
  286.5 5.8 %all-to-all-start.5 = ((bf16[64,16,1536]{2,1,0:T(8,128)(2,1)}), bf16[64,16,1536]{2,1,0:T(8,128)(2,1)}, u32[]{:S(2)}, u32[]{:S(2)}) async-start(bf16[64,16,1536]{2,1,0:T(8,128)(2,1)} %bitcast.137), calls=%async_computation.5 | async-start | bytes 6291456 | tf_op jit(solution)/shard_map/all_to_all | solution.py:43
  294.1 39.5 %all-to-all-done.5 = bf16[64,16,1536]{2,1,0:T(8,128)(2,1)} async-done(((bf16[64,16,1536]{2,1,0:T(8,128)(2,1)}), bf16[64,16,1536]{2,1,0:T(8,128)(2,1)}, u32[]{:S(2)}, u32[]{:S(2)}) %all-to-all-start.5) | async-done | bytes 3145760 | tf_op jit(solution)/shard_map/all_to_all | solution.py:43
  340.3 11.4 %shard_map.175 = (f32[197,768]{1,0:T(8,128)S(1)}, bf16[197,768]{1,0:T(8,128)(2,1)S(1)}, bf16[197,1152]{1,0:T(8,128)(2,1)S(1)}, bf16[197,1152]{1,0:T(8,128)(2,1)S(1)}, f32[4,768]{1,0:T(4,128)S(1)}) custom-call(s32[1]{0:T(128)} %bitcast.core_ref, f32[197,768]{1,0:T(8,128)S(1)} %copy-done.5, f32[197,768]{1,0:T(8,128)S(1)} %convolution_add_fusion.3.grad_two, ...), custom_call_target="tpu_custom_call" | custom-call | flops 5625790464 | bytes 8388608 | tf_op jit(solution)/shard_map/pallas_call | solution.py:244
  354.1 27.9 %all_to_all.92 = bf16[64,16,768]{2,1,0:T(8,128)(2,1)S(1)} all-to-all(bf16[64,16,768]{2,1,0:T(8,128)(2,1)S(1)} %bitcast.150), channel_id=1, replica_groups=mesh['ea'=32,'half'=2,'core'=2] {'ea','half'}, dimensions={0} | all-to-all | bytes 3145728 | tf_op jit(solution)/shard_map/all_to_all | solution.py:43
  389.6 5.4 shard_map.177
  396.6 4.8 fusion.29
  416.7 5.6 %all-to-all-start.7 = ((bf16[64,16,768]{2,1,0:T(8,128)(2,1)}), bf16[64,16,768]{2,1,0:T(8,128)(2,1)}, u32[]{:S(2)}, u32[]{:S(2)}) async-start(bf16[64,16,768]{2,1,0:T(8,128)(2,1)} %bitcast.141), calls=%async_computation.7 | async-start | bytes 3145728 | tf_op jit(solution)/shard_map/all_to_all | solution.py:43
  423.0 4.8 fusion.25
  433.2 12.5 %all-to-all-done.7 = bf16[64,16,768]{2,1,0:T(8,128)(2,1)} async-done(((bf16[64,16,768]{2,1,0:T(8,128)(2,1)}), bf16[64,16,768]{2,1,0:T(8,128)(2,1)}, u32[]{:S(2)}, u32[]{:S(2)}) %all-to-all-start.7) | async-done | bytes 1572896 | tf_op jit(solution)/shard_map/all_to_all | solution.py:43
  445.8 5.3 all-to-all-start.8
  451.2 5.1 add_bitcast_fusion.2
  468.4 12.1 %shard_map.178 = (f32[197,768]{1,0:T(8,128)}, bf16[197,768]{1,0:T(8,128)(2,1)S(1)}, bf16[197,1152]{1,0:T(8,128)(2,1)S(1)}, bf16[197,1152]{1,0:T(8,128)(2,1)S(1)}, f32[4,768]{1,0:T(4,128)S(1)}) custom-call(s32[1]{0:T(128)} %bitcast.core_ref, f32[197,768]{1,0:T(8,128)S(1)} %copy-done.10, f32[197,768]{1,0:T(8,128)S(1)} %convolution_add_fusion.2.grad_two, ...), custom_call_target="tpu_custom_call" | custom-call | flops 5625790464 | bytes 8388608 | tf_op jit(solution)/shard_map/pallas_call | solution.py:244
  495.0 5.5 add_bitcast_fusion.3
  504.9 5.2 all-to-all-start.9
  510.1 5.0 maximum_bitcast_fusion
  522.9 23.3 %collective-permute-done.15 = f32[24,1664]{1,0:T(8,128)S(1)} collective-permute-done((f32[24,1664]{1,0:T(8,128)S(1)}, f32[24,1664]{1,0:T(8,128)S(1)}, u32[]{:S(2)}, u32[]{:S(2)}) %collective-permute-start.15) | collective-permute-done | bytes 159776 | tf_op jit(solution)/shard_map/ppermute | solution.py:39
  551.8 5.3 collective-permute-done.14
  (397 shorter events, 166.4 us)
Async XLA Ops:
  50.1 7.2 %collective-permute-start = (bf16[768,1536]{1,0:T(8,128)(2,1)}, bf16[768,1536]{1,0:T(8,128)(2,1)}, u32[]{:S(2)}, u32[]{:S(2)}) collective-permute-start(bf16[768,1536]{1,0:T(8,128)(2,1)} %slice.377), channel_id=1, source_target_pairs={{0,1},{1,0},{2,3},{3,2},{4,5},{5,4},{6,7},{7,6},{8,9},{9,8},{10,11... | collective-permute-start | bytes 7077896 | tf_op jit(solution)/shard_map/ppermute | solution.py:35
  53.1 126.4 %copy-start.80 = (s32[1024]{0:T(1024)}, s32[1024]{0:T(1024)S(1)}, u32[]{:S(2)}) copy-start(s32[1024]{0:T(1024)S(1)} %fusion.91) | copy-start | bytes 12292
  54.2 125.3 %copy-start.97 = (s32[394]{0:T(512)}, s32[394]{0:T(512)S(1)}, u32[]{:S(2)}) copy-start(s32[394]{0:T(512)S(1)} %convert_add_fusion.1) | copy-start | bytes 4732
  68.3 31.6 %copy-start.78 = (bf16[24,768]{1,0:T(8,128)(2,1)S(1)}, bf16[24,768]{1,0:T(8,128)(2,1)}, u32[]{:S(2)}) copy-start(bf16[24,768]{1,0:T(8,128)(2,1)} %get-tuple-element.163) | copy-start | bytes 110596
  68.3 31.6 %copy-start.77 = (bf16[24,768]{1,0:T(8,128)(2,1)S(1)}, bf16[24,768]{1,0:T(8,128)(2,1)}, u32[]{:S(2)}) copy-start(bf16[24,768]{1,0:T(8,128)(2,1)} %get-tuple-element.162) | copy-start | bytes 110596
  68.3 31.7 %copy-start.79 = (bf16[1,24,768]{2,1,0:T(8,128)(2,1)S(1)}, bf16[1,24,768]{2,1,0:T(8,128)(2,1)}, u32[]{:S(2)}) copy-start(bf16[1,24,768]{2,1,0:T(8,128)(2,1)} %get-tuple-element.167) | copy-start | bytes 110596
  97.7 12.9 %collective-permute-start.1 = (bf16[1024,768]{1,0:T(8,128)(2,1)}, bf16[1024,768]{1,0:T(8,128)(2,1)}, u32[]{:S(2)}, u32[]{:S(2)}) collective-permute-start(bf16[1024,768]{1,0:T(8,128)(2,1)} %bitcast.14.rows), channel_id=1, source_target_pairs={{0,1},{1,0},{2,3},{3,2},{4,5},{5,4},{6,7},{7,6},{8,9},{9,8},{10,11... | collective-permute-start | bytes 4718600 | tf_op jit(solution)/shard_map/ppermute | solution.py:35
  101.8 40.2 %all-to-all-start.3 = ((bf16[32,24,1664]{2,1,0:T(8,128)(2,1)}), bf16[32,24,1664]{2,1,0:T(8,128)(2,1)}, u32[]{:S(2)}, u32[]{:S(2)}) async-start(bf16[32,24,1664]{2,1,0:T(8,128)(2,1)} %broadcast_in_dim.24), calls=%async_computation.3 | async-start | bytes 5111808 | tf_op jit(solution)/shard_map/all_to_all | solution.py:88
  120.8 25.4 %collective-permute-start.2 = (bf16[1024,768]{1,0:T(8,128)(2,1)}, bf16[1024,768]{1,0:T(8,128)(2,1)}, u32[]{:S(2)}, u32[]{:S(2)}) collective-permute-start(bf16[1024,768]{1,0:T(8,128)(2,1)} %get-tuple-element.61), channel_id=1, source_target_pairs={{0,1},{1,0},{2,3},{3,2},{4,5},{5,4},{6,7},{7,6},{8,9},{9,8},{10,11... | collective-permute-start | bytes 4718600 | tf_op jit(solution)/shard_map/ppermute | solution.py:35
  145.3 37.8 %collective-permute-start.3 = (bf16[768,1536]{1,0:T(8,128)(2,1)}, bf16[768,1536]{1,0:T(8,128)(2,1)}, u32[]{:S(2)}, u32[]{:S(2)}) collective-permute-start(bf16[768,1536]{1,0:T(8,128)(2,1)} %slice.395), channel_id=1, source_target_pairs={{0,1},{1,0},{2,3},{3,2},{4,5},{5,4},{6,7},{7,6},{8,9},{9,8},{10,11... | collective-permute-start | bytes 7077896 | tf_op jit(solution)/shard_map/ppermute | solution.py:35
  149.1 30.5 %all-to-all-start.2 = ((bf16[64,16,768]{2,1,0:T(8,128)(2,1)}), bf16[64,16,768]{2,1,0:T(8,128)(2,1)}, u32[]{:S(2)}, u32[]{:S(2)}) async-start(bf16[64,16,768]{2,1,0:T(8,128)(2,1)} %bitcast.142), calls=%async_computation.2 | async-start | bytes 3145728 | tf_op jit(solution)/shard_map/all_to_all | solution.py:43
  203.9 54.1 %copy-start.3 = (bf16[768,768]{1,0:T(8,128)(2,1)S(1)}, bf16[768,768]{1,0:T(8,128)(2,1)}, u32[]{:S(2)}) copy-start(bf16[768,768]{1,0:T(8,128)(2,1)} %get-tuple-element.145.w_out) | copy-start | bytes 3538948
  203.9 54.1 %copy-start.4 = (bf16[768,768]{1,0:T(8,128)(2,1)S(1)}, bf16[768,768]{1,0:T(8,128)(2,1)}, u32[]{:S(2)}) copy-start(bf16[768,768]{1,0:T(8,128)(2,1)} %get-tuple-element.191.w_in) | copy-start | bytes 3538948
  247.2 9.2 %collective-permute-start.4 = (bf16[1024,1536]{1,0:T(8,128)(2,1)S(1)}, bf16[1024,1536]{1,0:T(8,128)(2,1)S(1)}, u32[]{:S(2)}, u32[]{:S(2)}) collective-permute-start(bf16[1024,1536]{1,0:T(8,128)(2,1)S(1)} %bitcast.143), channel_id=1, source_target_pairs={{0,1},{1,0},{2,3},{3,2},{4,5},{5,4},{6,7},{7,6},{8,9},{9,8},{10,11... | collective-permute-start | bytes 9437192 | tf_op jit(solution)/shard_map/ppermute | solution.py:35
  270.3 10.4 %collective-permute-start.5 = (bf16[1024,1536]{1,0:T(8,128)(2,1)}, bf16[1024,1536]{1,0:T(8,128)(2,1)S(1)}, u32[]{:S(2)}, u32[]{:S(2)}) collective-permute-start(bf16[1024,1536]{1,0:T(8,128)(2,1)} %get-tuple-element.67), channel_id=1, source_target_pairs={{0,1},{1,0},{2,3},{3,2},{4,5},{5,4},{6,7},{7,6},{8,9},{9,8},{10,11... | collective-permute-start | bytes 9437192 | tf_op jit(solution)/shard_map/ppermute | solution.py:35
  286.5 47.1 %all-to-all-start.5 = ((bf16[64,16,1536]{2,1,0:T(8,128)(2,1)}), bf16[64,16,1536]{2,1,0:T(8,128)(2,1)}, u32[]{:S(2)}, u32[]{:S(2)}) async-start(bf16[64,16,1536]{2,1,0:T(8,128)(2,1)} %bitcast.137), calls=%async_computation.5 | async-start | bytes 6291456 | tf_op jit(solution)/shard_map/all_to_all | solution.py:43
  354.0 35.5 %copy-start.1 = (bf16[768,768]{1,0:T(8,128)(2,1)S(1)}, bf16[768,768]{1,0:T(8,128)(2,1)}, u32[]{:S(2)}) copy-start(bf16[768,768]{1,0:T(8,128)(2,1)} %copy-done) | copy-start | bytes 3538948
  381.9 6.5 %collective-permute-start.6 = (bf16[1024,768]{1,0:T(8,128)(2,1)S(1)}, bf16[1024,768]{1,0:T(8,128)(2,1)S(1)}, u32[]{:S(2)}, u32[]{:S(2)}) collective-permute-start(bf16[1024,768]{1,0:T(8,128)(2,1)S(1)} %bitcast.147), channel_id=1, source_target_pairs={{0,1},{1,0},{2,3},{3,2},{4,5},{5,4},{6,7},{7,6},{8,9},{9,8},{10,11... | collective-permute-start | bytes 4718600 | tf_op jit(solution)/shard_map/ppermute | solution.py:35
  396.2 16.9 %collective-permute-start.7 = (bf16[1024,768]{1,0:T(8,128)(2,1)}, bf16[1024,768]{1,0:T(8,128)(2,1)}, u32[]{:S(2)}, u32[]{:S(2)}) collective-permute-start(bf16[1024,768]{1,0:T(8,128)(2,1)} %get-tuple-element.74), channel_id=1, source_target_pairs={{0,1},{1,0},{2,3},{3,2},{4,5},{5,4},{6,7},{7,6},{8,9},{9,8},{10,11... | collective-permute-start | bytes 4718600 | tf_op jit(solution)/shard_map/ppermute | solution.py:35
  407.4 21.9 %collective-permute-start.8 = (bf16[768,1152]{1,0:T(8,128)(2,1)}, bf16[768,1152]{1,0:T(8,128)(2,1)}, u32[]{:S(2)}, u32[]{:S(2)}) collective-permute-start(bf16[768,1152]{1,0:T(8,128)(2,1)} %convolution_convert_fusion.1), channel_id=1, source_target_pairs={{0,1},{1,0},{2,3},{3,2},{4,5},{5,4},{6,7},{7,6},{8,9},{9,8},{10,11... | collective-permute-start | bytes 5308424 | tf_op jit(solution)/shard_map/ppermute | solution.py:35
  408.2 19.6 %collective-permute-start.10 = (bf16[768,128]{1,0:T(8,128)(2,1)}, bf16[768,128]{1,0:T(8,128)(2,1)}, u32[]{:S(2)}, u32[]{:S(2)}) collective-permute-start(bf16[768,128]{1,0:T(8,128)(2,1)} %pad_convert_fusion.1), channel_id=1, source_target_pairs={{0,1},{1,0},{2,3},{3,2},{4,5},{5,4},{6,7},{7,6},{8,9},{9,8},{10,11... | collective-permute-start | bytes 589832 | tf_op jit(solution)/shard_map/ppermute | solution.py:35
  416.7 29.1 %all-to-all-start.7 = ((bf16[64,16,768]{2,1,0:T(8,128)(2,1)}), bf16[64,16,768]{2,1,0:T(8,128)(2,1)}, u32[]{:S(2)}, u32[]{:S(2)}) async-start(bf16[64,16,768]{2,1,0:T(8,128)(2,1)} %bitcast.141), calls=%async_computation.7 | async-start | bytes 3145728 | tf_op jit(solution)/shard_map/all_to_all | solution.py:43
  422.7 6.1 %collective-permute-start.9 = (bf16[768,384]{1,0:T(8,128)(2,1)S(1)}, bf16[768,384]{1,0:T(8,128)(2,1)S(1)}, u32[]{:S(2)}, u32[]{:S(2)}) collective-permute-start(bf16[768,384]{1,0:T(8,128)(2,1)S(1)} %convolution_convert_fusion.5), channel_id=1, source_target_pairs={{0,1},{1,0},{2,3},{3,2},{4,5},{5,4},{6,7},{7,6},{8,9},{9,8},{10,11... | collective-permute-start | bytes 1769480 | tf_op jit(solution)/shard_map/ppermute | solution.py:35
  445.8 37.7 %all-to-all-start.8 = ((bf16[32,24,1664]{2,1,0:T(8,128)(2,1)}), bf16[32,24,1664]{2,1,0:T(8,128)(2,1)}, u32[]{:S(2)}, u32[]{:S(2)}) async-start(bf16[32,24,1664]{2,1,0:T(8,128)(2,1)} %bitcast.138), calls=%async_computation.8 | async-start | bytes 5111808 | tf_op jit(solution)/shard_map/all_to_all | solution.py:138
  485.4 15.6 %collective-permute-start.11 = (bf16[768,1152]{1,0:T(8,128)(2,1)}, bf16[768,1152]{1,0:T(8,128)(2,1)}, u32[]{:S(2)}, u32[]{:S(2)}) collective-permute-start(bf16[768,1152]{1,0:T(8,128)(2,1)} %convolution_convert_fusion), channel_id=1, source_target_pairs={{0,1},{1,0},{2,3},{3,2},{4,5},{5,4},{6,7},{7,6},{8,9},{9,8},{10,11... | collective-permute-start | bytes 5308424 | tf_op jit(solution)/shard_map/ppermute | solution.py:35
  493.9 6.5 %collective-permute-start.13 = (bf16[768,128]{1,0:T(8,128)(2,1)S(1)}, bf16[768,128]{1,0:T(8,128)(2,1)S(1)}, u32[]{:S(2)}, u32[]{:S(2)}) collective-permute-start(bf16[768,128]{1,0:T(8,128)(2,1)S(1)} %pad_convert_fusion), channel_id=1, source_target_pairs={{0,1},{1,0},{2,3},{3,2},{4,5},{5,4},{6,7},{7,6},{8,9},{9,8},{10,11... | collective-permute-start | bytes 589832 | tf_op jit(solution)/shard_map/ppermute | solution.py:35
  494.4 6.1 %collective-permute-start.12 = (bf16[768,384]{1,0:T(8,128)(2,1)S(1)}, bf16[768,384]{1,0:T(8,128)(2,1)S(1)}, u32[]{:S(2)}, u32[]{:S(2)}) collective-permute-start(bf16[768,384]{1,0:T(8,128)(2,1)S(1)} %convolution_convert_fusion.4), channel_id=1, source_target_pairs={{0,1},{1,0},{2,3},{3,2},{4,5},{5,4},{6,7},{7,6},{8,9},{9,8},{10,11... | collective-permute-start | bytes 1769480 | tf_op jit(solution)/shard_map/ppermute | solution.py:35
  504.9 43.1 %all-to-all-start.9 = ((bf16[32,24,1664]{2,1,0:T(8,128)(2,1)}), bf16[32,24,1664]{2,1,0:T(8,128)(2,1)}, u32[]{:S(2)}, u32[]{:S(2)}) async-start(bf16[32,24,1664]{2,1,0:T(8,128)(2,1)} %bitcast.139), calls=%async_computation.9 | async-start | bytes 5111808 | tf_op jit(solution)/shard_map/all_to_all | solution.py:138
  518.9 27.2 %collective-permute-start.15 = (f32[24,1664]{1,0:T(8,128)S(1)}, f32[24,1664]{1,0:T(8,128)S(1)}, u32[]{:S(2)}, u32[]{:S(2)}) collective-permute-start(f32[24,1664]{1,0:T(8,128)S(1)} %convert_reduce_fusion), channel_id=1, source_target_pairs={{0,2},{2,0},{1,3},{3,1},{4,6},{6,4},{5,7},{7,5},{8,10},{10,8},{9,1... | collective-permute-start | bytes 479240 | tf_op jit(solution)/shard_map/ppermute | solution.py:39
  546.2 1.8 collective-permute-start.17
  550.1 6.9 %collective-permute-start.14 = (f32[24,1664]{1,0:T(8,128)S(1)}, f32[24,1664]{1,0:T(8,128)S(1)}, u32[]{:S(2)}, u32[]{:S(2)}) collective-permute-start(f32[24,1664]{1,0:T(8,128)S(1)} %convert_reduce_fusion.1), channel_id=1, source_target_pairs={{0,2},{2,0},{1,3},{3,1},{4,6},{6,4},{5,7},{7,5},{8,10},{10,8},{9,1... | collective-permute-start | bytes 479240 | tf_op jit(solution)/shard_map/ppermute | solution.py:39
  557.1 3.3 collective-permute-start.16
  (107 other events, 591.0 us)

commit v3 on v2

--- a/solution.py
+++ b/solution.py
@@ -1,3 +1,5 @@
+import functools
+
 import jax
 import jax.numpy as jnp
 from jax import lax
@@ -17,6 +19,7 @@
 SLOTS = 16
 SCALE = HEAD ** (-0.5)
 GROUP = ("ea", "half")
+VMEM = 28 * 1024 * 1024
 
 
 def dot(a, b, dims=((1,), (0,))):
@@ -35,25 +38,26 @@
     return lax.ppermute(value, "core", [(0, 1), (1, 0)])
 
 
-def swap_half(value):
-    return lax.ppermute(value, "half", [(0, 1), (1, 0)])
-
-
 def exchange(rows):
     return lax.all_to_all(rows, GROUP, split_axis=0, concat_axis=0, tiled=True)
 
 
 def gelu_parts(x):
-    mag = jnp.abs(x)
-    t = 1.0 / (1.0 + (0.3275911 * 0.7071067811865476) * mag)
-    bell = jnp.exp(-0.5 * x * x)
-    poly = 0.5 * t * (
-        0.254829592
-        + t * (-0.284496736 + t * (1.421413741 + t * (-1.453152027 + t * 1.061405429)))
+    base = 1.0 + (0.3275911 * 0.7071067811865476) * jnp.abs(x)
+    t = pl.reciprocal(base, approx=True)
+    t = t * (2.0 - base * t)
+    bell = jnp.exp2((x * x) * (-0.5 * 1.4426950408889634))
+    poly = t * (
+        0.5 * 0.254829592
+        + t
+        * (
+            0.5 * -0.284496736
+            + t * (0.5 * 1.421413741 + t * (0.5 * -1.453152027 + t * (0.5 * 1.061405429)))
+        )
     )
     tail = poly * bell
     cdf = jnp.where(x < 0, tail, 1.0 - tail)
-    return cdf, cdf + x * bell * 0.3989422804014327
+    return cdf, cdf + x * (bell * 0.3989422804014327)
 
 
 def normalize(x, gain, bias):
@@ -111,16 +115,8 @@
     return jnp.concatenate([core_half(part) for part in thirds(qkv)] + [core_half(out), small], axis=1)
 
 
-def split_dense(own, experts):
-    other = swap_core(own[:, :1536])
-    small = own[:, 1536:]
-    norms = small[:, experts : experts + 4].astype(F32).T
-    return (
-        (own[:, :1152], other[:, :1152]),
-        (own[:, 1152:1536], other[:, 1152:]),
-        small,
-        norms,
-    )
+def split_dense(own):
+    return own, swap_core(own)
 
 
 def sum_send(grad_qkv, grad_out, small):
@@ -140,10 +136,15 @@
     )
 
 
+def swap_row(value, flip):
+    return lax.ppermute(value, ("half", "core"), [(i, i ^ flip) for i in range(4)])
+
+
 def sum_finish(parts):
     part = jnp.sum(parts.astype(F32), axis=0)
-    full = part + swap_half(part)
-    other = swap_core(full[:, :1536])
+    full = part + swap_row(part, 2)
+    dense = part[:, :1536]
+    other = swap_row(dense, 1) + swap_row(dense, 3)
     qkv = [
         in_order(own, more) for own, more in zip(thirds(full[:, :1152]), thirds(other[:, :1152]))
     ]
@@ -178,15 +179,24 @@
     return jnp.where(lane < HEAD, first, second)
 
 
+QKV = slice(0, 1152)
+OUT = slice(1152, 1536)
+SMALL = slice(1536, 1664)
+
+
+def norms_of(own, experts):
+    return own[:, SMALL].astype(F32).T[experts : experts + 4]
+
+
 def attend_kernel(
-    core_ref, state, norms, qkv_o, qkv_x, out_o, out_x, small, normed, proj_o, proj_x, mixed, after,
-    normed_two, logits,
+    experts, core_ref, state, own, other, normed, proj_o, proj_x, mixed, after, normed_two, logits
 ):
     core = core_ref[0]
-    wide, _, _ = normalize(state[...], norms[0:1, :], norms[2:3, :])
+    norms = norms_of(own, experts)
+    wide, _, _ = normalize(state[...], norms[0:1], norms[2:3])
     normed[...] = wide.astype(BF)
-    for side, weight, proj in ((0, qkv_o, proj_o), (1, qkv_x, proj_x)):
-        proj[...] = dot(normed[...], weight[...]).astype(BF)
+    for side, weight, proj in ((0, own, proj_o), (1, other, proj_x)):
+        proj[...] = dot(normed[...], weight[:, QKV]).astype(BF)
         for at in range(0, 384, 128):
             query, key_part, value_part = (proj[:, i * 384 + at : i * 384 + at + 128] for i in range(3))
             found = []
@@ -194,26 +204,27 @@
                 shares = softmax_rows(dot_nt(masked(query, j), key_part) * SCALE)
                 found.append(dot(shares.astype(BF), value_part))
             mixed[:, place(core, side, at, 128)] = merge(*found).astype(BF)
-    for side, weight in ((0, out_o), (1, out_x)):
+    for side, weight in ((0, own), (1, other)):
         cols = place(core, side, 0, 384)
-        after[:, cols] = state[:, cols] + dot(mixed[...], weight[...])
-    wide, _, _ = normalize(after[...], norms[1:2, :], norms[3:4, :])
+        after[:, cols] = state[:, cols] + dot(mixed[...], weight[:, OUT])
+    wide, _, _ = normalize(after[...], norms[1:2], norms[3:4])
     normed_two[...] = wide.astype(BF)
-    logits[...] = dot(normed_two[...], small[...])
+    logits[...] = dot(normed_two[...], own[:, SMALL])
 
 
 def attend_back_kernel(
-    core_ref, grad, grad_two, state, after, norms, proj_o, proj_x, qkv_o, qkv_x, out_o, out_x,
-    grad_in, grad_attn, gp_o, gp_x, stats, grad_mixed,
+    experts, core_ref, grad, grad_two, state, after, proj_o, proj_x, own, other, grad_in, grad_attn,
+    gp_o, gp_x, stats, grad_mixed,
 ):
     core = core_ref[0]
-    _, unit, inv = normalize(after[...], norms[1:2, :], norms[3:4, :])
-    part, gain_two, bias_two = normalize_back(grad_two[...], unit, inv, norms[1:2, :])
+    norms = norms_of(own, experts)
+    _, unit, inv = normalize(after[...], norms[1:2], norms[3:4])
+    part, gain_two, bias_two = normalize_back(grad_two[...], unit, inv, norms[1:2])
     grad_in[...] = grad[...] + part
     grad_attn[...] = grad_in[...].astype(BF)
     grad_mixed[...] = sum(
-        dot_nt(grad_attn[:, place(core, side, 0, 384)], weight[...])
-        for side, weight in ((0, out_o), (1, out_x))
+        dot_nt(grad_attn[:, place(core, side, 0, 384)], weight[:, OUT])
+        for side, weight in ((0, own), (1, other))
     ).astype(BF)
     for side, proj, gp in ((0, proj_o, gp_o), (1, proj_x, gp_x)):
         for at in range(0, 384, 128):
@@ -230,9 +241,9 @@
                 )
             for i in range(3):
                 gp[:, i * 384 + at : i * 384 + at + 128] = merge(found[0][i], found[1][i]).astype(BF)
-    grad_normed = dot_nt(gp_o[...], qkv_o[...]) + dot_nt(gp_x[...], qkv_x[...])
-    _, unit, inv = normalize(state[...], norms[0:1, :], norms[2:3, :])
-    part, gain_one, bias_one = normalize_back(grad_normed, unit, inv, norms[0:1, :])
+    grad_normed = dot_nt(gp_o[...], own[:, QKV]) + dot_nt(gp_x[...], other[:, QKV])
+    _, unit, inv = normalize(state[...], norms[0:1], norms[2:3])
+    part, gain_one, bias_one = normalize_back(grad_normed, unit, inv, norms[0:1])
     grad_in[...] = grad_in[...] + part
     for i, row in enumerate((gain_one, gain_two, bias_one, bias_two)):
         stats[i : i + 1, :] = row[None, :]
@@ -247,18 +258,17 @@
         out_specs=[vmem] * len(outs),
         out_shape=[jax.ShapeDtypeStruct(shape, kind) for shape, kind in outs],
         scratch_shapes=list(scratch),
-        compiler_params=pltpu.CompilerParams(vmem_limit_bytes=48 * 1024 * 1024),
+        compiler_params=pltpu.CompilerParams(vmem_limit_bytes=VMEM),
         cost_estimate=pl.CostEstimate(flops=flops, bytes_accessed=8 << 20, transcendentals=0),
     )(core, *args)
 
 
 def attention(state, dense):
-    qkv_w, out_w, small, norms = dense
     tokens, width = state.shape
     rows = lambda n, kind: ((tokens, n), kind)
     normed, proj_o, proj_x, mixed, after, normed_two, logits = whole_call(
-        attend_kernel,
-        [state, norms, *qkv_w, *out_w, small],
+        functools.partial(attend_kernel, lax.axis_size("ea")),
+        [state, *dense],
         [
             rows(width, BF), rows(1152, BF), rows(1152, BF), rows(width, BF), rows(width, F32),
             rows(width, BF), rows(128, F32),
@@ -270,12 +280,11 @@
 
 def attention_back(grad, grad_two, kept, dense):
     state, normed, proj_o, proj_x, mixed, after = kept
-    qkv_w, out_w, _, norms = dense
     tokens, width = grad.shape
     rows = lambda n, kind: ((tokens, n), kind)
     grad_in, grad_attn, gp_o, gp_x, stats = whole_call(
-        attend_back_kernel,
-        [grad, grad_two, state, after, norms, proj_o, proj_x, *qkv_w, *out_w],
+        functools.partial(attend_back_kernel, lax.axis_size("ea")),
+        [grad, grad_two, state, after, proj_o, proj_x, *dense],
         [rows(width, F32), rows(width, BF), rows(1152, BF), rows(1152, BF), ((4, width), F32)],
         8 * tokens * width * (4 * width + 8 * tokens),
         [pltpu.VMEM((tokens, width), BF)],
@@ -289,50 +298,55 @@
 
 
 def forward_kernel(rows, w_in, w_out, hidden, slope, part):
-    pre = dot(rows[...], w_in[...])
+    pre = dot(rows[...], w_in[0, 0])
     cdf, steep = gelu_parts(pre)
     hidden[...] = (pre * cdf).astype(BF)
     slope[...] = steep.astype(BF)
-    part[...] = dot(hidden[...], w_out[...]).astype(BF)
+    part[...] = dot(hidden[...], w_out[0, 0]).astype(BF)
 
 
 def backward_kernel(grows, slope, w_in, w_out, grad_pre, part):
-    grad_hidden = dot_nt(grows[...], w_out[...])
+    grad_hidden = dot_nt(grows[...], w_out[0, 0])
     grad_pre[...] = (grad_hidden * slope[...].astype(F32)).astype(BF)
-    part[...] = dot_nt(grad_pre[...], w_in[...]).astype(BF)
+    part[...] = dot_nt(grad_pre[...], w_in[0, 0]).astype(BF)
 
 
 def both_kernel(rows, w_in, w_out, hidden, grad_pre, part):
-    width = w_in.shape[0]
-    pre = dot(rows[:, :width], w_in[...])
+    groups, _, slots, width = rows.shape
+    pre = dot(rows[:, 0].reshape(groups * slots, width), w_in[0, 0])
     cdf, steep = gelu_parts(pre)
     hidden[...] = (pre * cdf).astype(BF)
-    part[:, :width] = dot(hidden[...], w_out[...]).astype(BF)
-    grad_hidden = dot_nt(rows[:, width:], w_out[...])
+    out = dot(hidden[...], w_out[0, 0]).astype(BF)
+    part[:, 0] = out.reshape(groups, slots, width)
+    grad_hidden = dot_nt(rows[:, 1].reshape(groups * slots, width), w_out[0, 0])
     grad_pre[...] = (grad_hidden * steep).astype(BF)
-    part[:, width:] = dot_nt(grad_pre[...], w_in[...]).astype(BF)
-
-
-BLOCK = 512
-
-
-def expert_call(kernel, row_args, weights, out_widths, products):
-    count = row_args[0].shape[0]
-
-    def rows_spec(width):
-        return pl.BlockSpec((BLOCK, width), lambda i: (i, 0))
-
-    moved = sum(a.size for a in row_args) + sum(w.size for w in weights) + count * sum(out_widths)
+    out = dot_nt(grad_pre[...], w_in[0, 0]).astype(BF)
+    part[:, 1] = out.reshape(groups, slots, width)
+
+
+GROUPS = 32
+
+
+def expert_call(kernel, depth, row_args, weights, out_dims, products):
+    def spec(shape):
+        block = (GROUPS * SLOTS,) + shape[1:] if len(shape) == 2 else (GROUPS,) + shape[1:]
+        return pl.BlockSpec(block, lambda i: (i,) + (0,) * (len(shape) - 1))
+
+    hidden_units, width = weights[1].shape[2:]
+    count = row_args[-1].shape[0] * (1 if row_args[-1].ndim == 2 else SLOTS)
+    moved = count * width * (len(row_args) + len(out_dims)) + 2 * hidden_units * width
     return pl.pallas_call(
         kernel,
-        grid=(count // BLOCK,),
-        in_specs=[rows_spec(a.shape[1]) for a in row_args]
-        + [pl.BlockSpec(w.shape, lambda i: (0, 0)) for w in weights],
-        out_specs=[rows_spec(width) for width in out_widths],
-        out_shape=[jax.ShapeDtypeStruct((count, width), BF) for width in out_widths],
-        compiler_params=pltpu.CompilerParams(vmem_limit_bytes=48 * 1024 * 1024),
+        grid=(count // (GROUPS * SLOTS),),
+        in_specs=[spec(a.shape) for a in row_args]
+        + [pl.BlockSpec((1,) + w.shape[1:], lambda i: (depth, 0, 0, 0)) for w in weights],
+        out_specs=[spec(shape) for shape in out_dims],
+        out_shape=[jax.ShapeDtypeStruct(shape, BF) for shape in out_dims],
+        compiler_params=pltpu.CompilerParams(vmem_limit_bytes=VMEM),
         cost_estimate=pl.CostEstimate(
-            flops=2 * count * 768 * 768 * products, bytes_accessed=2 * moved, transcendentals=0
+            flops=2 * count * hidden_units * width * products,
+            bytes_accessed=2 * moved,
+            transcendentals=0,
         ),
     )(*row_args, *weights)
 
@@ -342,10 +356,9 @@
 
 
 def routing(chosen, experts):
-    tokens = chosen.shape[0]
     flat = jnp.concatenate([chosen[:, 0], chosen[:, 1]])
     onehot = flat[:, None] == jnp.arange(experts, dtype=jnp.int32)[None, :]
-    pairs = 2 * tokens
+    pairs = flat.shape[0]
     earlier = (
         lax.broadcasted_iota(jnp.int32, (pairs, pairs), 1)
         < lax.broadcasted_iota(jnp.int32, (pairs, pairs), 0)
@@ -353,15 +366,22 @@
     onehot = onehot.astype(F32)
     before = dot(earlier, onehot.astype(BF))
     position = jnp.sum(before * onehot, axis=1).astype(jnp.int32)
-    code = flat * (2 * SLOTS) + position
-    slots = experts * 2 * SLOTS
-    row_code = lax.broadcasted_iota(jnp.int32, (slots, pairs), 0)
-    row_code = row_code - jnp.where(lax.rem(row_code, 2 * SLOTS) >= SLOTS, SLOTS, 0)
-    send = (row_code == code[None, :]).astype(BF)
-    col_code = lax.broadcasted_iota(jnp.int32, (pairs, slots), 1)
-    col_code = col_code - jnp.where(lax.rem(col_code, 2 * SLOTS) >= SLOTS, SLOTS, 0)
-    fetch = (col_code == code[:, None]).astype(BF)
-    return onehot, send, fetch
+    return onehot, flat * SLOTS + position
+
+
+def slot_codes(slots, kinds, dims, axis):
+    row = lax.broadcasted_iota(jnp.int32, dims, axis)
+    run = row // SLOTS
+    return lax.rem(run, kinds), (run // (2 * kinds)) * SLOTS + lax.rem(row, SLOTS)
+
+
+def one_hots(code, slots, kinds, kind):
+    pairs = code.shape[0]
+    found = []
+    for dims, axis, codes in (((slots, pairs), 0, code[None, :]), ((pairs, slots), 1, code[:, None])):
+        kind_of, slot_of = slot_codes(slots, kinds, dims, axis)
+        found.append(((slot_of == codes) & (kind_of == kind)).astype(BF))
+    return found
 
 
 def router_forward(logits, onehot):
@@ -408,77 +428,87 @@
     for b in range(LAYERS):
         small = jnp.concatenate([router_weight[b], norm_gains[b].T, norm_biases[b].T], axis=1)
         mine.append(core_dense(qkv_weight[b], out_weight[b], pad_cols(small, 128)))
-    dense0 = split_dense(gather_cols(mine[0]), experts)
-    routed = [routing(routes[b], experts) for b in range(LAYERS)]
-    w_in = [expert_in[b, 0] for b in range(LAYERS)]
-    w_out = [expert_out[b, 0] for b in range(LAYERS)]
+    dense0 = split_dense(gather_cols(mine[0]))
+    weights = [expert_in, expert_out]
+    onehot0, code = routing(routes[0], experts)
+    send, fetch = one_hots(code, experts * 2 * SLOTS, 1, 0)
+    onehot1, code = routing(routes[1], experts)
+    send_rows, fetch_rows = one_hots(code, experts * 4 * SLOTS, 2, 0)
+    send_grads, fetch_grads = one_hots(code, experts * 4 * SLOTS, 2, 1)
+    send_rows = send_rows[:, :tokens] + send_rows[:, tokens:]
+    fetch_grads = fetch_grads[:tokens] + fetch_grads[tokens:]
+    send1 = jnp.concatenate([send_rows, send_grads], axis=1)
+    fetch1 = jnp.concatenate([fetch_rows, fetch_grads], axis=0)
 
     state = image_tokens.astype(F32)
     after0, normed0, logits, kept0 = attention(state, dense0)
-    onehot, send, fetch = routed[0]
-    router0, gate0 = router_forward(logits[:, :experts], onehot)
+    router0, gate0 = router_forward(logits[:, :experts], onehot0)
     arrived = exchange(dot(send[:, :tokens] + send[:, tokens:], normed0).astype(BF))
     gathered1 = gather_cols(mine[1], after=arrived)
     rows0 = (arrived, swap_core(arrived))
     first = [
-        expert_call(forward_kernel, [r], [w_in[0], w_out[0]], [width] * 3, 2) for r in rows0
+        expert_call(forward_kernel, 0, [r], weights, [r.shape] * 3, 2) for r in rows0
     ]
     hidden0, slope0, part = zip(*first)
     returned = exchange(join_cores(*part))
-    dense1 = split_dense(gathered1, experts)
+    dense1 = split_dense(gathered1)
     picked = dot(fetch, returned)
     picked0 = (picked[:tokens], picked[tokens:])
     state1 = after0 + gate0[0] * picked0[0] + gate0[1] * picked0[1]
 
     grad = cotangent.astype(F32)
     after1, normed1, logits, kept1 = attention(state1, dense1)
-    onehot1, send1, fetch1 = routed[1]
     router1, gate1 = router_forward(logits[:, :experts], onehot1)
-    rows = dot(send1[:, :tokens] + send1[:, tokens:], normed1).astype(BF)
-    grad_rows = jnp.concatenate([(g * grad).astype(BF) for g in gate1], axis=0)
-    grad_rows = dot(send1, grad_rows).astype(BF)
-    arrived = exchange(jnp.concatenate([rows, grad_rows], axis=1))
+    rows = jnp.concatenate([normed1] + [(g * grad).astype(BF) for g in gate1], axis=0)
+    arrived = exchange(dot(send1, rows).astype(BF)).reshape(-1, 2, SLOTS, width)
     both = (arrived, swap_core(arrived))
+    flat = (arrived.shape[0] * SLOTS, width)
     second = [
-        expert_call(both_kernel, [r], [w_in[1], w_out[1]], [width, width, 2 * width], 4)
-        for r in both
+        expert_call(both_kernel, 1, [r], weights, [flat, flat, r.shape], 4) for r in both
     ]
     hidden1, grad_pre1, part = zip(*second)
-    returned = exchange(join_cores(*part))
+    returned = exchange(join_cores(*part).reshape(-1, width))
+    grad_w_out1 = sum(dot_tn(h, r[:, 1].reshape(flat)) for h, r in zip(hidden1, both))
+    grad_w_in1 = sum(dot_tn(r[:, 0].reshape(flat), g) for r, g in zip(both, grad_pre1))
+    returned, grad_w_out1, grad_w_in1 = lax.optimization_barrier(
+        (returned, grad_w_out1, grad_w_in1)
+    )
     picked = dot(fetch1, returned)
-    picked1 = (picked[:tokens, :width], picked[tokens:, :width])
-    grad_sent = picked[:tokens, width:] + picked[tokens:, width:]
+    picked1 = (picked[:tokens], picked[tokens : 2 * tokens])
+    grad_sent = picked[2 * tokens :]
     block_out = (after1 + gate1[0] * picked1[0] + gate1[1] * picked1[1]).astype(BF)
-    grad_w_out1 = sum(dot_tn(h, r[:, width:]) for h, r in zip(hidden1, both))
-    grad_w_in1 = sum(dot_tn(r[:, :width], g) for r, g in zip(both, grad_pre1))
 
     extra, grad_router_w1 = router_back(
-        grad, picked1, router1, onehot1, normed1, dense1[2][:, :experts]
+        grad, picked1, router1, onehot1, normed1, dense1[0][:, 1536 : 1536 + experts]
     )
     grad, stats1, terms1 = attention_back(grad, grad_sent + extra, kept1, dense1)
 
     grad_rows = jnp.concatenate([(g * grad).astype(BF) for g in gate0], axis=0)
     arrived = exchange(dot(send, grad_rows).astype(BF))
+    pair1 = sum_send(*dense_grads(*terms1), small_grads(grad_router_w1, stats1))
+    arrived, pair1 = lax.optimization_barrier((arrived, pair1))
     grows0 = (arrived, swap_core(arrived))
     third = [
-        expert_call(backward_kernel, [r, s], [w_in[0], w_out[0]], [width] * 2, 2)
+        expert_call(backward_kernel, 0, [r, s], weights, [r.shape] * 2, 2)
         for r, s in zip(grows0, slope0)
     ]
     grad_pre0, part = zip(*third)
-    pair1 = sum_send(*dense_grads(*terms1), small_grads(grad_router_w1, stats1))
     returned = exchange(join_cores(*part))
     parts1 = sum_exchange(pair1, after=returned)
     picked = dot(fetch, returned)
     grad_sent = picked[:tokens] + picked[tokens:]
-    grad_w_out0 = sum(dot_tn(h, g) for h, g in zip(hidden0, grows0))
-    grad_w_in0 = sum(dot_tn(r, g) for r, g in zip(rows0, grad_pre0))
     extra, grad_router_w0 = router_back(
-        grad, picked0, router0, onehot, normed0, dense0[2][:, :experts]
+        grad, picked0, router0, onehot0, normed0, dense0[0][:, 1536 : 1536 + experts]
     )
     grad, stats0, terms0 = attention_back(grad, grad_sent + extra, kept0, dense0)
     terms0, parts1 = lax.optimization_barrier((terms0, parts1))
     pair0 = sum_send(*dense_grads(*terms0), small_grads(grad_router_w0, stats0))
     parts0 = sum_exchange(pair0)
+    (hidden0, grows0, rows0, grad_pre0), pair0 = lax.optimization_barrier(
+        ((hidden0, grows0, rows0, grad_pre0), pair0)
+    )
+    grad_w_out0 = sum(dot_tn(h, g) for h, g in zip(hidden0, grows0))
+    grad_w_in0 = sum(dot_tn(r, g) for r, g in zip(rows0, grad_pre0))
     sums1 = sum_finish(parts1)
     sums0 = sum_finish(parts0)
 

time: 573 us -> 525 us (0.916)
  local copies, waits for them, and re-layouts: 56.5 us -> 33.9 us
  Pallas kernels: 80.8 us -> 66.4 us
  matrix products: 61 us -> 49 us
  waiting for transfers between devices: 118 us -> 110 us
    all_to_all x2, waiting for transfers between devices: 2.98 us -> 29.4 us  [sum_exchange(): lax.all_to_all(pair.reshape(groups, -1, pair.shape[1]), 'ea', split_axis=...]
    ppermute x2 -> x6, waiting for transfers between devices: 28.5 us -> 7.96 us  [swap_row(): lax.ppermute(value, ('half', 'core'), [(i, i ^ flip) for i in range(4)])]
    slice x14 -> x4, local copies, waits for them, and re-layouts: 20.9 us -> 0.46 us  [the longest x2 0.44 us: per_device(): r[:, 0].reshape(flat)]
    all_to_all x3, waiting for transfers between devices: 65.4 us -> 48.9 us  [exchange(): return lax.all_to_all(rows, GROUP, split_axis=0, concat_axis=0, tiled=True)]
    dot_general x25 -> x24, matrix products: 57 us -> 46.1 us  [dot(): return lax.dot_general(a, b, (dims, ((), ())), preferred_element_type=F32)]
    unnamed x240 -> x280, local copies, waits for them, and re-layouts: 14.9 us -> 25.2 us
    pallas_call x6, Pallas kernels: 44.8 us -> 35.4 us  [expert_call(): pl.pallas_call(kernel, grid=(count // (GROUPS * SLOTS),), in_specs=[spec(...]
    convert_element_type x2 -> x4, other arithmetic: 1.58 us -> 9.98 us  [the longest x3 9.81 us: one_hots(): found.append(((slot_of == codes) & (kind_of == kind)).astype(BF))]
  transfers between devices with their start and end apart: 24 -> 26, of which waited for: 10 -> 13; matrix products, arithmetic and copies ran while one was open for 17% -> 15% of each run, Pallas kernels for 7% -> 7%
where the time goes in v3:
time: 525 us; the launch traced here: 516 us
  blocking collectives  143 us (27%)
  waiting for transfers between devices  110 us (21%)
  Pallas kernels  66.4 us (13%)
  starting transfers between devices  63.8 us (12%)
  matrix products  49 us (9%)
  other arithmetic  47 us (9%)
  local copies, waits for them, and re-layouts  33.9 us (6%)
    all_to_all x3, blocking collectives, exchange(): return lax.all_to_all(rows, GROUP, split_axis=0, concat_axis=0, tiled=True)  102 us
    all_to_all x3, waiting for transfers between devices, exchange(): return lax.all_to_all(rows, GROUP, split_axis=0, concat_axis=0, tiled=True)  48.9 us
    dot_general x24, matrix products, dot(): return lax.dot_general(a, b, (dims, ((), ())), preferred_element_type=F32)  46.1 us
    all_to_all x1, blocking collectives, gather_cols(): got = lax.all_to_all(sent, 'ea', split_axis=0, concat_axis=0)  41.4 us
    pallas_call x6, Pallas kernels, expert_call(): pl.pallas_call(kernel, grid=(count // (GROUPS * SLOTS),), in_specs=[spec(...  35.4 us
    pallas_call x4, Pallas kernels, whole_call(): pl.pallas_call(kernel, in_specs=[pl.BlockSpec(memory_space=pltpu.SMEM)] +...  31 us
    all_to_all x2, waiting for transfers between devices, sum_exchange(): lax.all_to_all(pair.reshape(groups, -1, pair.shape[1]), 'ea', split_axis=...  29.4 us
    unnamed x280, local copies, waits for them, and re-layouts  25.2 us
  transfers between devices with their start and end apart: 26, of which 13 were waited for; matrix products, arithmetic and copies ran while one was open for 15% of the time, Pallas kernels for 7%

profile of v3, /device:TPU:1, one launch (start us, length us, event | category | flops | bytes accessed | tf_op | source)
XLA Modules:
  0.0 516.1 jit_solution(14896477726953370088)
XLA Ops:
  5.1 41.4 %all_to_all.88 = bf16[32,24,1664]{2,1,0:T(8,128)(2,1)S(1)} all-to-all(bf16[32,24,1664]{2,1,0:T(8,128)(2,1)S(1)} %broadcast_in_dim.8), channel_id=1, replica_groups=mesh['ea'=32,'half'=2,'core'=2] {'ea'}, dimensions={0} | all-to-all | bytes 5111808 | tf_op jit(solution)/shard_map/all_to_all | solution.py:92
  53.7 4.0 shard_map.169
  58.4 29.3 %all_to_all.89 = bf16[64,16,768]{2,1,0:T(8,128)(2,1)} all-to-all(bf16[64,16,768]{2,1,0:T(8,128)(2,1)S(1)} %bitcast.140), channel_id=1, replica_groups=mesh['ea'=32,'half'=2,'core'=2] {'ea','half'}, dimensions={0} | all-to-all | bytes 3145728 | tf_op jit(solution)/shard_map/all_to_all | solution.py:42
  91.8 4.1 all-to-all-start.3
  99.2 7.4 %shard_map.171 = (bf16[1024,768]{1,0:T(8,128)(2,1)S(1)}, bf16[1024,768]{1,0:T(8,128)(2,1)S(1)}, bf16[1024,768]{1,0:T(8,128)(2,1)}) custom-call(bf16[1024,768]{1,0:T(8,128)(2,1)} %collective-permute-done.1.rows, bf16[2,1,768,768]{3,2,1,0:T(8,128)(2,1)S(1)} %copy-done.33, bf16[2,1,768,768]{3,2,1,0:T(8,128)(2,1)S(1)} %copy-done.37), custom_call_target="tpu_custom_call" | custom-call | flops 2415919104 | bytes 8650752 | tf_op jit(solution)/shard_map/pallas_call | solution.py:338
  109.8 6.4 %shard_map.170 = (bf16[1024,768]{1,0:T(8,128)(2,1)S(1)}, bf16[1024,768]{1,0:T(8,128)(2,1)S(1)}, bf16[1024,768]{1,0:T(8,128)(2,1)S(1)}) custom-call(bf16[1024,768]{1,0:T(8,128)(2,1)} %bitcast.13.rows, bf16[2,1,768,768]{3,2,1,0:T(8,128)(2,1)S(1)} %copy-done.34, bf16[2,1,768,768]{3,2,1,0:T(8,128)(2,1)S(1)} %copy-done.38), custom_call_target="tpu_custom_call" | custom-call | flops 2415919104 | bytes 8650752 | tf_op jit(solution)/shard_map/pallas_call | solution.py:338
  119.7 11.6 %all-to-all-done.3 = bf16[32,24,1664]{2,1,0:T(8,128)(2,1)S(1)} async-done(((bf16[32,24,1664]{2,1,0:T(8,128)(2,1)}), bf16[32,24,1664]{2,1,0:T(8,128)(2,1)S(1)}, u32[]{:S(2)}, u32[]{:S(2)}) %all-to-all-start.3) | async-done | bytes 2555936 | tf_op jit(solution)/shard_map/all_to_all | solution.py:92
  135.5 6.9 %all-to-all-start.2 = ((bf16[64,16,768]{2,1,0:T(8,128)(2,1)}), bf16[64,16,768]{2,1,0:T(8,128)(2,1)}, u32[]{:S(2)}, u32[]{:S(2)}) async-start(bf16[64,16,768]{2,1,0:T(8,128)(2,1)} %bitcast.141), calls=%async_computation.2 | async-start | bytes 3145728 | tf_op jit(solution)/shard_map/all_to_all | solution.py:42
  142.5 5.1 and_convert_fusion.1
  149.5 15.5 %all-to-all-done.2 = bf16[64,16,768]{2,1,0:T(8,128)(2,1)} async-done(((bf16[64,16,768]{2,1,0:T(8,128)(2,1)}), bf16[64,16,768]{2,1,0:T(8,128)(2,1)}, u32[]{:S(2)}, u32[]{:S(2)}) %all-to-all-start.2) | async-done | bytes 1572896 | tf_op jit(solution)/shard_map/all_to_all | solution.py:42
  168.5 6.0 %shard_map.172 = (bf16[197,768]{1,0:T(8,128)(2,1)S(1)}, bf16[197,1152]{1,0:T(8,128)(2,1)S(1)}, bf16[197,1152]{1,0:T(8,128)(2,1)S(1)}, bf16[197,768]{1,0:T(8,128)...) custom-call(s32[1]{0:T(128)} %bitcast.core_ref, ...), custom_call_target="tpu_custom_call" | custom-call | flops 2336010240 | bytes 8388608 | tf_op jit(solution)/shard_map/pallas_call | solution.py:255
  178.7 44.2 %all_to_all.90 = bf16[64,32,768]{2,1,0:T(8,128)(2,1)S(1)} all-to-all(bf16[64,32,768]{2,1,0:T(8,128)(2,1)S(1)} %bitcast.143), channel_id=1, replica_groups=mesh['ea'=32,'half'=2,'core'=2] {'ea','half'}, dimensions={0} | all-to-all | bytes 6291456 | tf_op jit(solution)/shard_map/all_to_all | solution.py:42
  222.9 3.6 collective-permute-start.4
  226.5 5.3 %collective-permute-done.4.rows = bf16[64,2,16,768]{3,2,1,0:T(8,128)(2,1)S(1)} collective-permute-done((bf16[64,2,16,768]{3,2,1,0:T(8,128)(2,1)S(1)}, bf16[64,2,16,768]{3,2,1,0:T(8,128)(2,1)S(1)}, u32[]{:S(2)}, u32[]{:S(2)}) %collective-permute-start.4) | collective-permute-done | bytes 3145760 | tf_op jit(solution)/shard_map/ppermute | solution.py:38
  231.8 7.5 %shard_map.174 = (bf16[1024,768]{1,0:T(8,128)(2,1)S(1)}, bf16[1024,768]{1,0:T(8,128)(2,1)S(1)}, bf16[64,2,16,768]{3,2,1,0:T(8,128)(2,1)S(1)}) custom-call(bf16[64,2,16,768]{3,2,1,0:T(8,128)(2,1)S(1)} %collective-permute-done.4.rows, bf16[2,1,768,768]{3,2,1,0:T(8,128)(2,1)S(1)} %copy-done.35, bf16[2,1,768,768]{3,2,1,0:T(8,128)(2,1)S(1)} %copy-done.39), custom_call_target="tpu_custom_call" | custom-call | flops 4831838208 | bytes 8650752 | tf_op jit(solution)/shard_map/pallas_call | solution.py:338
  240.9 7.5 %shard_map.173 = (bf16[1024,768]{1,0:T(8,128)(2,1)S(1)}, bf16[1024,768]{1,0:T(8,128)(2,1)S(1)}, bf16[64,2,16,768]{3,2,1,0:T(8,128)(2,1)S(1)}) custom-call(bf16[64,2,16,768]{3,2,1,0:T(8,128)(2,1)S(1)} %bitcast.122, bf16[2,1,768,768]{3,2,1,0:T(8,128)(2,1)S(1)} %copy-done.35, bf16[2,1,768,768]{3,2,1,0:T(8,128)(2,1)S(1)} %copy-done.39), custom_call_target="tpu_custom_call" | custom-call | flops 4831838208 | bytes 8650752 | tf_op jit(solution)/shard_map/pallas_call | solution.py:338
  251.3 5.6 %all-to-all-start.5 = ((bf16[64,32,768]{2,1,0:T(8,128)(2,1)}), bf16[64,32,768]{2,1,0:T(8,128)(2,1)}, u32[]{:S(2)}, u32[]{:S(2)}) async-start(bf16[64,32,768]{2,1,0:T(8,128)(2,1)} %bitcast.137), calls=%async_computation.5 | async-start | bytes 6291456 | tf_op jit(solution)/shard_map/all_to_all | solution.py:42
  275.8 22.4 %all-to-all-done.5 = bf16[64,32,768]{2,1,0:T(8,128)(2,1)} async-done(((bf16[64,32,768]{2,1,0:T(8,128)(2,1)}), bf16[64,32,768]{2,1,0:T(8,128)(2,1)}, u32[]{:S(2)}, u32[]{:S(2)}) %all-to-all-start.5) | async-done | bytes 3145760 | tf_op jit(solution)/shard_map/all_to_all | solution.py:42
  298.2 4.0 fusion.22
  304.6 11.0 %shard_map.175 = (f32[197,768]{1,0:T(8,128)S(1)}, bf16[197,768]{1,0:T(8,128)(2,1)S(1)}, bf16[197,1152]{1,0:T(8,128)(2,1)S(1)}, bf16[197,1152]{1,0:T(8,128)(2,1)S(1)}, f32[4,768]{1,0:T(4,128)S(1)}) custom-call(s32[1]{0:T(128)} %bitcast.core_ref, f32[197,768]{1,0:T(8,128)S(1)} %copy-done.17, f32[197,768]{1,0:T(8,128)S(1)} %convolution_add_fusion.5.grad_two, ...), custom_call_target="tpu_custom_call" | custom-call | flops 5625790464 | bytes 8388608 | tf_op jit(solution)/shard_map/pallas_call | solution.py:255
  323.8 5.8 %all-to-all-start.6 = ((bf16[64,16,768]{2,1,0:T(8,128)(2,1)}), bf16[64,16,768]{2,1,0:T(8,128)(2,1)S(1)}, u32[]{:S(2)}, u32[]{:S(2)}) async-start(bf16[64,16,768]{2,1,0:T(8,128)(2,1)} %bitcast.146), calls=%async_computation.6 | async-start | bytes 3145728 | tf_op jit(solution)/shard_map/all_to_all | solution.py:42
  341.5 11.0 %all-to-all-done.6 = bf16[64,16,768]{2,1,0:T(8,128)(2,1)S(1)} async-done(((bf16[64,16,768]{2,1,0:T(8,128)(2,1)}), bf16[64,16,768]{2,1,0:T(8,128)(2,1)S(1)}, u32[]{:S(2)}, u32[]{:S(2)}) %all-to-all-start.6) | async-done | bytes 1572896 | tf_op jit(solution)/shard_map/all_to_all | solution.py:42
  372.3 28.3 %all_to_all.91 = bf16[64,16,768]{2,1,0:T(8,128)(2,1)} all-to-all(bf16[64,16,768]{2,1,0:T(8,128)(2,1)S(1)} %bitcast.142), channel_id=1, replica_groups=mesh['ea'=32,'half'=2,'core'=2] {'ea','half'}, dimensions={0} | all-to-all | bytes 3145728 | tf_op jit(solution)/shard_map/all_to_all | solution.py:42
  400.7 5.0 all-to-all-start.8
  409.9 10.0 %shard_map.178 = (f32[197,768]{1,0:T(8,128)}, bf16[197,768]{1,0:T(8,128)(2,1)S(1)}, bf16[197,1152]{1,0:T(8,128)(2,1)S(1)}, bf16[197,1152]{1,0:T(8,128)(2,1)S(1)}, f32[4,768]{1,0:T(4,128)S(1)}) custom-call(s32[1]{0:T(128)} %bitcast.core_ref, f32[197,768]{1,0:T(8,128)S(1)} %get-tuple-element.88.grad, f32[197,768]{1,0:T(8,128)S(1)} %convolution_add_fusion.4.grad_two, ...), custom_call_target="tpu_custom_call" | custom-call | flops 5625790464 | bytes 8388608 | tf_op jit(solution)/shard_map/pallas_call | solution.py:255
  424.7 12.4 %all-to-all-done.8 = bf16[32,24,1664]{2,1,0:T(8,128)(2,1)} async-done(((bf16[32,24,1664]{2,1,0:T(8,128)(2,1)}), bf16[32,24,1664]{2,1,0:T(8,128)(2,1)}, u32[]{:S(2)}, u32[]{:S(2)}) %all-to-all-start.8) | async-done | bytes 2555936 | tf_op jit(solution)/shard_map/all_to_all | solution.py:134
  437.9 5.5 %collective-permute-start.11 = (bf16[768,1152]{1,0:T(8,128)(2,1)S(1)}, bf16[768,1152]{1,0:T(8,128)(2,1)S(1)}, u32[]{:S(2)}, u32[]{:S(2)}) collective-permute-start(bf16[768,1152]{1,0:T(8,128)(2,1)S(1)} %convolution_convert_fusion), channel_id=1, source_target_pairs={{0,1},{1,0},{2,3},{3,2},{4,5},{5,4},{6,7},{7,6},{8,9},{9,8},{10,11... | collective-permute-start | bytes 5308424 | tf_op jit(solution)/shard_map/ppermute | solution.py:38
  449.9 6.2 %collective-permute-done.19 = f32[24,1536]{1,0:T(8,128)S(1)} collective-permute-done((f32[24,1536]{1,0:T(8,128)S(1)}, f32[24,1536]{1,0:T(8,128)S(1)}, u32[]{:S(2)}, u32[]{:S(2)}) %collective-permute-start.19) | collective-permute-done | bytes 147488 | tf_op jit(solution)/shard_map/ppermute | solution.py:140
  459.7 5.2 %all-to-all-start.9 = ((bf16[32,24,1664]{2,1,0:T(8,128)(2,1)}), bf16[32,24,1664]{2,1,0:T(8,128)(2,1)}, u32[]{:S(2)}, u32[]{:S(2)}) async-start(bf16[32,24,1664]{2,1,0:T(8,128)(2,1)} %bitcast.139), calls=%async_computation.9 | async-start | bytes 5111808 | tf_op jit(solution)/shard_map/all_to_all | solution.py:134
  477.1 4.4 add_bitcast_fusion.1
  481.5 17.0 %all-to-all-done.9 = bf16[32,24,1664]{2,1,0:T(8,128)(2,1)} async-done(((bf16[32,24,1664]{2,1,0:T(8,128)(2,1)}), bf16[32,24,1664]{2,1,0:T(8,128)(2,1)}, u32[]{:S(2)}, u32[]{:S(2)}) %all-to-all-start.9) | async-done | bytes 2555936 | tf_op jit(solution)/shard_map/all_to_all | solution.py:134
  506.3 4.2 maximum_bitcast_fusion
  (434 shorter events, 149.7 us)
Async XLA Ops:
  5.0 44.2 %copy-start.85 = (bf16[197,768]{1,0:T(8,128)(2,1)S(1)}, bf16[197,768]{1,0:T(8,128)(2,1)}, u32[]{:S(2)}) copy-start(bf16[197,768]{1,0:T(8,128)(2,1)} %param.10) | copy-start | bytes 907780
  5.1 44.2 %copy-start.128 = (s32[2,197,2]{1,2,0:T(2,128)S(1)}, s32[2,197,2]{1,2,0:T(2,128)}, u32[]{:S(2)}) copy-start(s32[2,197,2]{1,2,0:T(2,128)} %param.12) | copy-start | bytes 9460
  46.5 7.2 %collective-permute-start = (bf16[768,1664]{1,0:T(8,128)(2,1)S(1)}, bf16[768,1664]{1,0:T(8,128)(2,1)S(1)}, u32[]{:S(2)}, u32[]{:S(2)}) collective-permute-start(bf16[768,1664]{1,0:T(8,128)(2,1)S(1)} %bitcast.128), channel_id=1, source_target_pairs={{0,1},{1,0},{2,3},{3,2},{4,5},{5,4},{6,7},{7,6},{8,9},{9,8},{10,11... | collective-permute-start | bytes 7667720 | tf_op jit(solution)/shard_map/ppermute | solution.py:38
  49.4 115.6 %copy-start.97 = (s32[1024]{0:T(1024)}, s32[1024]{0:T(1024)S(1)}, u32[]{:S(2)}) copy-start(s32[1024]{0:T(1024)S(1)} %broadcast_add_fusion.1) | copy-start | bytes 12292
  57.8 109.6 %copy-start.18 = (f32[197,768]{1,0:T(8,128)}, f32[197,768]{1,0:T(8,128)S(1)}, u32[]{:S(2)}) copy-start(f32[197,768]{1,0:T(8,128)S(1)} %get-tuple-element.70.after) | copy-start | bytes 1815556
  87.8 8.0 %collective-permute-start.1 = (bf16[1024,768]{1,0:T(8,128)(2,1)}, bf16[1024,768]{1,0:T(8,128)(2,1)}, u32[]{:S(2)}, u32[]{:S(2)}) collective-permute-start(bf16[1024,768]{1,0:T(8,128)(2,1)} %bitcast.13.rows), channel_id=1, source_target_pairs={{0,1},{1,0},{2,3},{3,2},{4,5},{5,4},{6,7},{7,6},{8,9},{9,8},{10,11... | collective-permute-start | bytes 4718600 | tf_op jit(solution)/shard_map/ppermute | solution.py:38
  91.8 39.5 %all-to-all-start.3 = ((bf16[32,24,1664]{2,1,0:T(8,128)(2,1)}), bf16[32,24,1664]{2,1,0:T(8,128)(2,1)S(1)}, u32[]{:S(2)}, u32[]{:S(2)}) async-start(bf16[32,24,1664]{2,1,0:T(8,128)(2,1)} %broadcast_in_dim.9), calls=%async_computation.3 | async-start | bytes 5111808 | tf_op jit(solution)/shard_map/all_to_all | solution.py:92
  107.8 24.3 %collective-permute-start.2 = (bf16[1024,768]{1,0:T(8,128)(2,1)}, bf16[1024,768]{1,0:T(8,128)(2,1)}, u32[]{:S(2)}, u32[]{:S(2)}) collective-permute-start(bf16[1024,768]{1,0:T(8,128)(2,1)} %get-tuple-element.74), channel_id=1, source_target_pairs={{0,1},{1,0},{2,3},{3,2},{4,5},{5,4},{6,7},{7,6},{8,9},{9,8},{10,11... | collective-permute-start | bytes 4718600 | tf_op jit(solution)/shard_map/ppermute | solution.py:38
  131.3 37.2 %collective-permute-start.3 = (bf16[768,1664]{1,0:T(8,128)(2,1)S(1)}, bf16[768,1664]{1,0:T(8,128)(2,1)}, u32[]{:S(2)}, u32[]{:S(2)}) collective-permute-start(bf16[768,1664]{1,0:T(8,128)(2,1)S(1)} %bitcast.124), channel_id=1, source_target_pairs={{0,1},{1,0},{2,3},{3,2},{4,5},{5,4},{6,7},{7,6},{8,9},{9,8},{10,11... | collective-permute-start | bytes 7667720 | tf_op jit(solution)/shard_map/ppermute | solution.py:38
  135.5 29.5 %all-to-all-start.2 = ((bf16[64,16,768]{2,1,0:T(8,128)(2,1)}), bf16[64,16,768]{2,1,0:T(8,128)(2,1)}, u32[]{:S(2)}, u32[]{:S(2)}) async-start(bf16[64,16,768]{2,1,0:T(8,128)(2,1)} %bitcast.141), calls=%async_computation.2 | async-start | bytes 3145728 | tf_op jit(solution)/shard_map/all_to_all | solution.py:42
  178.7 53.1 %copy-start.35 = (bf16[2,1,768,768]{3,2,1,0:T(8,128)(2,1)S(1)}, bf16[2,1,768,768]{3,2,1,0:T(8,128)(2,1)}, u32[]{:S(2)}) copy-start(bf16[2,1,768,768]{3,2,1,0:T(8,128)(2,1)} %w_in.11) | copy-start | bytes 7077892
  178.7 53.1 %copy-start.39 = (bf16[2,1,768,768]{3,2,1,0:T(8,128)(2,1)S(1)}, bf16[2,1,768,768]{3,2,1,0:T(8,128)(2,1)}, u32[]{:S(2)}) copy-start(bf16[2,1,768,768]{3,2,1,0:T(8,128)(2,1)} %w_out.11) | copy-start | bytes 7077892
  222.9 8.9 %collective-permute-start.4 = (bf16[64,2,16,768]{3,2,1,0:T(8,128)(2,1)S(1)}, bf16[64,2,16,768]{3,2,1,0:T(8,128)(2,1)S(1)}, u32[]{:S(2)}, u32[]{:S(2)}) collective-permute-start(bf16[64,2,16,768]{3,2,1,0:T(8,128)(2,1)S(1)} %bitcast.121), channel_id=1, source_target_pairs={{0,1},{1,0},{2,3},{3,2},{4,5},{5,4},{6,7},{7,6},{8,9},{9,8},{10,11... | collective-permute-start | bytes 9437192 | tf_op jit(solution)/shard_map/ppermute | solution.py:38
  240.5 7.9 %collective-permute-start.5 = (bf16[64,2,16,768]{3,2,1,0:T(8,128)(2,1)S(1)}, bf16[64,2,16,768]{3,2,1,0:T(8,128)(2,1)S(1)}, u32[]{:S(2)}, u32[]{:S(2)}) collective-permute-start(bf16[64,2,16,768]{3,2,1,0:T(8,128)(2,1)S(1)} %get-tuple-element.80), channel_id=1, source_target_pairs={{0,1},{1,0},{2,3},{3,2},{4,5},{5,4},{6,7},{7,6},{8,9},{9,8},{10,11... | collective-permute-start | bytes 9437192 | tf_op jit(solution)/shard_map/ppermute | solution.py:38
  251.3 46.9 %all-to-all-start.5 = ((bf16[64,32,768]{2,1,0:T(8,128)(2,1)}), bf16[64,32,768]{2,1,0:T(8,128)(2,1)}, u32[]{:S(2)}, u32[]{:S(2)}) async-start(bf16[64,32,768]{2,1,0:T(8,128)(2,1)} %bitcast.137), calls=%async_computation.5 | async-start | bytes 6291456 | tf_op jit(solution)/shard_map/all_to_all | solution.py:42
  317.7 19.8 %collective-permute-start.6 = (bf16[768,1152]{1,0:T(8,128)(2,1)}, bf16[768,1152]{1,0:T(8,128)(2,1)}, u32[]{:S(2)}, u32[]{:S(2)}) collective-permute-start(bf16[768,1152]{1,0:T(8,128)(2,1)} %convolution_convert_fusion.1), channel_id=1, source_target_pairs={{0,1},{1,0},{2,3},{3,2},{4,5},{5,4},{6,7},{7,6},{8,9},{9,8},{10,11... | collective-permute-start | bytes 5308424 | tf_op jit(solution)/shard_map/ppermute | solution.py:38
  320.1 15.9 %collective-permute-start.7 = (bf16[768,384]{1,0:T(8,128)(2,1)}, bf16[768,384]{1,0:T(8,128)(2,1)}, u32[]{:S(2)}, u32[]{:S(2)}) collective-permute-start(bf16[768,384]{1,0:T(8,128)(2,1)} %convolution_convert_fusion.6), channel_id=1, source_target_pairs={{0,1},{1,0},{2,3},{3,2},{4,5},{5,4},{6,7},{7,6},{8,9},{9,8},{10,11... | collective-permute-start | bytes 1769480 | tf_op jit(solution)/shard_map/ppermute | solution.py:38
  323.8 28.7 %all-to-all-start.6 = ((bf16[64,16,768]{2,1,0:T(8,128)(2,1)}), bf16[64,16,768]{2,1,0:T(8,128)(2,1)S(1)}, u32[]{:S(2)}, u32[]{:S(2)}) async-start(bf16[64,16,768]{2,1,0:T(8,128)(2,1)} %bitcast.146), calls=%async_computation.6 | async-start | bytes 3145728 | tf_op jit(solution)/shard_map/all_to_all | solution.py:42
  333.0 1.9 collective-permute-start.8
  352.5 5.1 collective-permute-start.9
  367.3 3.9 collective-permute-start.10
  400.7 36.4 %all-to-all-start.8 = ((bf16[32,24,1664]{2,1,0:T(8,128)(2,1)}), bf16[32,24,1664]{2,1,0:T(8,128)(2,1)}, u32[]{:S(2)}, u32[]{:S(2)}) async-start(bf16[32,24,1664]{2,1,0:T(8,128)(2,1)} %bitcast.138), calls=%async_computation.8 | async-start | bytes 5111808 | tf_op jit(solution)/shard_map/all_to_all | solution.py:134
  421.6 3.0 collective-permute-start.13
  437.9 19.4 %collective-permute-start.11 = (bf16[768,1152]{1,0:T(8,128)(2,1)S(1)}, bf16[768,1152]{1,0:T(8,128)(2,1)S(1)}, u32[]{:S(2)}, u32[]{:S(2)}) collective-permute-start(bf16[768,1152]{1,0:T(8,128)(2,1)S(1)} %convolution_convert_fusion), channel_id=1, source_target_pairs={{0,1},{1,0},{2,3},{3,2},{4,5},{5,4},{6,7},{7,6},{8,9},{9,8},{10,11... | collective-permute-start | bytes 5308424 | tf_op jit(solution)/shard_map/ppermute | solution.py:38
  445.5 10.6 %collective-permute-start.15 = (f32[24,1664]{1,0:T(8,128)S(1)}, f32[24,1664]{1,0:T(8,128)S(1)}, u32[]{:S(2)}, u32[]{:S(2)}) collective-permute-start(f32[24,1664]{1,0:T(8,128)S(1)} %convert_reduce_fusion), channel_id=1, source_target_pairs={{0,2},{1,3},{2,0},{3,1},{4,6},{5,7},{6,4},{7,5},{8,10},{9,11},{10,... | collective-permute-start | bytes 479240 | tf_op jit(solution)/shard_map/ppermute | solution.py:140
  446.7 3.2 collective-permute-start.18
  447.1 9.0 %collective-permute-start.19 = (f32[24,1536]{1,0:T(8,128)S(1)}, f32[24,1536]{1,0:T(8,128)S(1)}, u32[]{:S(2)}, u32[]{:S(2)}) collective-permute-start(f32[24,1536]{1,0:T(8,128)S(1)} %slice.347), channel_id=1, source_target_pairs={{0,3},{1,2},{2,1},{3,0},{4,7},{5,6},{6,5},{7,4},{8,11},{9,10},{10,... | collective-permute-start | bytes 442376 | tf_op jit(solution)/shard_map/ppermute | solution.py:140
  449.4 7.4 %collective-permute-start.12 = (bf16[768,384]{1,0:T(8,128)(2,1)S(1)}, bf16[768,384]{1,0:T(8,128)(2,1)S(1)}, u32[]{:S(2)}, u32[]{:S(2)}) collective-permute-start(bf16[768,384]{1,0:T(8,128)(2,1)S(1)} %convolution_convert_fusion.5), channel_id=1, source_target_pairs={{0,1},{1,0},{2,3},{3,2},{4,5},{5,4},{6,7},{7,6},{8,9},{9,8},{10,11... | collective-permute-start | bytes 1769480 | tf_op jit(solution)/shard_map/ppermute | solution.py:38
  459.7 38.8 %all-to-all-start.9 = ((bf16[32,24,1664]{2,1,0:T(8,128)(2,1)}), bf16[32,24,1664]{2,1,0:T(8,128)(2,1)}, u32[]{:S(2)}, u32[]{:S(2)}) async-start(bf16[32,24,1664]{2,1,0:T(8,128)(2,1)} %bitcast.139), calls=%async_computation.9 | async-start | bytes 5111808 | tf_op jit(solution)/shard_map/all_to_all | solution.py:134
  500.6 11.7 %collective-permute-start.14 = (f32[24,1664]{1,0:T(8,128)S(1)}, f32[24,1664]{1,0:T(8,128)S(1)}, u32[]{:S(2)}, u32[]{:S(2)}) collective-permute-start(f32[24,1664]{1,0:T(8,128)S(1)} %convert_reduce_fusion.1), channel_id=1, source_target_pairs={{0,2},{1,3},{2,0},{3,1},{4,6},{5,7},{6,4},{7,5},{8,10},{9,11},{10,... | collective-permute-start | bytes 479240 | tf_op jit(solution)/shard_map/ppermute | solution.py:140
  501.8 8.7 %collective-permute-start.16 = (f32[24,1536]{1,0:T(8,128)S(1)}, f32[24,1536]{1,0:T(8,128)S(1)}, u32[]{:S(2)}, u32[]{:S(2)}) collective-permute-start(f32[24,1536]{1,0:T(8,128)S(1)} %slice.340), channel_id=1, source_target_pairs={{0,1},{1,0},{2,3},{3,2},{4,5},{5,4},{6,7},{7,6},{8,9},{9,8},{10,11... | collective-permute-start | bytes 442376 | tf_op jit(solution)/shard_map/ppermute | solution.py:140
  504.5 7.7 %collective-permute-start.17 = (f32[24,1536]{1,0:T(8,128)S(1)}, f32[24,1536]{1,0:T(8,128)S(1)}, u32[]{:S(2)}, u32[]{:S(2)}) collective-permute-start(f32[24,1536]{1,0:T(8,128)S(1)} %slice.340), channel_id=1, source_target_pairs={{0,3},{1,2},{2,1},{3,0},{4,7},{5,6},{6,5},{7,4},{8,11},{9,10},{10,... | collective-permute-start | bytes 442376 | tf_op jit(solution)/shard_map/ppermute | solution.py:140
  (129 other events, 1077.5 us)

commit v4 on v3

--- a/solution.py
+++ b/solution.py
@@ -119,12 +119,8 @@
     return own, swap_core(own)
 
 
-def sum_send(grad_qkv, grad_out, small):
-    give = [grad_qkv[1].astype(BF), grad_out[1].astype(BF), small.astype(BF)]
-    own = [grad_qkv[0], grad_out[0], small]
-    return jnp.concatenate(
-        [(o + swap_core(g).astype(F32)).astype(BF) for o, g in zip(own, give)], axis=1
-    )
+def sum_send(own, give):
+    return (own.astype(F32) + swap_core(give).astype(F32)).astype(BF)
 
 
 def sum_exchange(pair, after=None):
@@ -259,7 +255,7 @@
         out_shape=[jax.ShapeDtypeStruct(shape, kind) for shape, kind in outs],
         scratch_shapes=list(scratch),
         compiler_params=pltpu.CompilerParams(vmem_limit_bytes=VMEM),
-        cost_estimate=pl.CostEstimate(flops=flops, bytes_accessed=8 << 20, transcendentals=0),
+        cost_estimate=pl.CostEstimate(flops=flops, bytes_accessed=1 << 16, transcendentals=0),
     )(core, *args)
 
 
@@ -273,7 +269,7 @@
             rows(width, BF), rows(1152, BF), rows(1152, BF), rows(width, BF), rows(width, F32),
             rows(width, BF), rows(128, F32),
         ],
-        4 * tokens * width * (4 * width + 4 * tokens),
+        1 << 20,
     )
     return after, normed_two, logits, (state, normed, proj_o, proj_x, mixed, after)
 
@@ -286,15 +282,39 @@
         functools.partial(attend_back_kernel, lax.axis_size("ea")),
         [grad, grad_two, state, after, proj_o, proj_x, *dense],
         [rows(width, F32), rows(width, BF), rows(1152, BF), rows(1152, BF), ((4, width), F32)],
-        8 * tokens * width * (4 * width + 8 * tokens),
+        1 << 20,
         [pltpu.VMEM((tokens, width), BF)],
     )
     return grad_in, stats, (normed, gp_o, gp_x, mixed, grad_attn)
 
 
-def dense_grads(normed, gp_o, gp_x, mixed, grad_attn):
-    grad_out = [dot_tn(mixed, core_half(grad_attn, which)) for which in (0, 1)]
-    return [dot_tn(normed, gp_o), dot_tn(normed, gp_x)], grad_out
+def dense_grad_kernel(core_ref, normed, gp_o, gp_x, mixed, grad_attn, small, own, give):
+    core = core_ref[0]
+    for side, gp, out in ((1, gp_x, give), (0, gp_o, own)):
+        out[:, QKV] = dot_tn(normed[...], gp[...]).astype(BF)
+        out[:, OUT] = dot_tn(mixed[...], grad_attn[:, place(core, side, 0, 384)]).astype(BF)
+        out[:, SMALL] = small[...].astype(BF)
+
+
+def dense_grads(normed, gp_o, gp_x, mixed, grad_attn, small):
+    core = lax.axis_index("core").astype(jnp.int32).reshape(1)
+    tokens, width = normed.shape
+    rows = 256
+    cols = pl.BlockSpec((tokens, rows), lambda i: (0, i))
+    whole = pl.BlockSpec(memory_space=pltpu.VMEM)
+    block = pl.BlockSpec((rows, 1664), lambda i: (i, 0))
+    return pl.pallas_call(
+        dense_grad_kernel,
+        grid=(width // rows,),
+        in_specs=[
+            pl.BlockSpec(memory_space=pltpu.SMEM), cols, whole, whole, cols, whole,
+            pl.BlockSpec((rows, 128), lambda i: (i, 0)),
+        ],
+        out_specs=[block, block],
+        out_shape=[jax.ShapeDtypeStruct((width, 1664), BF)] * 2,
+        compiler_params=pltpu.CompilerParams(vmem_limit_bytes=VMEM),
+        cost_estimate=pl.CostEstimate(flops=1 << 20, bytes_accessed=1 << 16, transcendentals=0),
+    )(core, normed, gp_o, gp_x, mixed, grad_attn, small)
 
 
 def forward_kernel(rows, w_in, w_out, hidden, slope, part):
@@ -485,7 +505,7 @@
 
     grad_rows = jnp.concatenate([(g * grad).astype(BF) for g in gate0], axis=0)
     arrived = exchange(dot(send, grad_rows).astype(BF))
-    pair1 = sum_send(*dense_grads(*terms1), small_grads(grad_router_w1, stats1))
+    pair1 = sum_send(*dense_grads(*terms1, small_grads(grad_router_w1, stats1)))
     arrived, pair1 = lax.optimization_barrier((arrived, pair1))
     grows0 = (arrived, swap_core(arrived))
     third = [
@@ -501,14 +521,17 @@
         grad, picked0, router0, onehot0, normed0, dense0[0][:, 1536 : 1536 + experts]
     )
     grad, stats0, terms0 = attention_back(grad, grad_sent + extra, kept0, dense0)
-    terms0, parts1 = lax.optimization_barrier((terms0, parts1))
-    pair0 = sum_send(*dense_grads(*terms0), small_grads(grad_router_w0, stats0))
+    pair0 = sum_send(*dense_grads(*terms0, small_grads(grad_router_w0, stats0)))
+    pair0, parts1 = lax.optimization_barrier((pair0, parts1))
     parts0 = sum_exchange(pair0)
-    (hidden0, grows0, rows0, grad_pre0), pair0 = lax.optimization_barrier(
+    (hidden0, grows0, rows0, grad_pre0), _ = lax.optimization_barrier(
         ((hidden0, grows0, rows0, grad_pre0), pair0)
     )
     grad_w_out0 = sum(dot_tn(h, g) for h, g in zip(hidden0, grows0))
     grad_w_in0 = sum(dot_tn(r, g) for r, g in zip(rows0, grad_pre0))
+    (grad_w_out0, grad_w_in0), parts1 = lax.optimization_barrier(
+        ((grad_w_out0, grad_w_in0), parts1)
+    )
     sums1 = sum_finish(parts1)
     sums0 = sum_finish(parts0)
 

time: 525 us -> 544 us (1.036)
  waiting for transfers between devices: 110 us -> 159 us
  blocking collectives: 143 us -> 114 us
  matrix products: 49 us -> 36.4 us
  local copies, waits for them, and re-layouts: 33.9 us -> 43.2 us
  Pallas kernels: 66.4 us -> 73 us
    all_to_all x3 -> x4, waiting for transfers between devices: 48.9 us -> 83.2 us  [exchange(): return lax.all_to_all(rows, GROUP, split_axis=0, concat_axis=0, tiled=True)]
    all_to_all x3 -> x2, blocking collectives: 102 us -> 72.5 us  [exchange(): return lax.all_to_all(rows, GROUP, split_axis=0, concat_axis=0, tiled=True)]
    ppermute x6, waiting for transfers between devices: 7.96 us -> 22 us  [swap_row(): lax.ppermute(value, ('half', 'core'), [(i, i ^ flip) for i in range(4)])]
    dot_general x24 -> x16, matrix products: 46.1 us -> 34.6 us  [dot(): return lax.dot_general(a, b, (dims, ((), ())), preferred_element_type=F32)]
    unnamed x280 -> x190, local copies, waits for them, and re-layouts: 25.2 us -> 36.2 us
    ppermute x14 -> x10, starting transfers between devices: 22.1 us -> 14.3 us  [swap_core(): return lax.ppermute(value, 'core', [(0, 1), (1, 0)])]
    convert_element_type x2, other arithmetic: 1.11 us -> 7.68 us  [sum_send(): return (own.astype(F32) + swap_core(give).astype(F32)).astype(BF)]
    pallas_call x0 -> x2, Pallas kernels: none -> 6.13 us  [dense_grads(): pl.pallas_call(dense_grad_kernel, grid=(width // rows,), in_specs=[pl.Blo...]
  transfers between devices with their start and end apart: 26 -> 23, of which waited for: 13 -> 12; matrix products, arithmetic and copies ran while one was open for 15% -> 12% of each run, Pallas kernels for 7% -> 5%
where the time goes in v4:
time: 544 us; the launch traced here: 534 us
  waiting for transfers between devices  159 us (29%)
  blocking collectives  114 us (21%)
  Pallas kernels  73 us (13%)
  starting transfers between devices  61 us (11%)
  other arithmetic  45.4 us (8%)
  local copies, waits for them, and re-layouts  43.2 us (8%)
  matrix products  36.4 us (7%)
    all_to_all x4, waiting for transfers between devices, exchange(): return lax.all_to_all(rows, GROUP, split_axis=0, concat_axis=0, tiled=True)  83.2 us
    all_to_all x2, blocking collectives, exchange(): return lax.all_to_all(rows, GROUP, split_axis=0, concat_axis=0, tiled=True)  72.5 us
    all_to_all x1, blocking collectives, gather_cols(): got = lax.all_to_all(sent, 'ea', split_axis=0, concat_axis=0)  41.4 us
    unnamed x190, local copies, waits for them, and re-layouts  36.2 us
    pallas_call x6, Pallas kernels, expert_call(): pl.pallas_call(kernel, grid=(count // (GROUPS * SLOTS),), in_specs=[spec(...  36 us
    dot_general x16, matrix products, dot(): return lax.dot_general(a, b, (dims, ((), ())), preferred_element_type=F32)  34.6 us
    all_to_all x2, waiting for transfers between devices, sum_exchange(): lax.all_to_all(pair.reshape(groups, -1, pair.shape[1]), 'ea', split_axis=...  31.7 us
    pallas_call x4, Pallas kernels, whole_call(): pl.pallas_call(kernel, in_specs=[pl.BlockSpec(memory_space=pltpu.SMEM)] +...  30.9 us
  transfers between devices with their start and end apart: 23, of which 12 were waited for; matrix products, arithmetic and copies ran while one was open for 12% of the time, Pallas kernels for 5%

profile of v4, /device:TPU:1, one launch (start us, length us, event | category | flops | bytes accessed | tf_op | source)
XLA Modules:
  0.0 533.9 jit_solution(14894039514374409437)
XLA Ops:
  5.1 41.4 %all_to_all.88 = bf16[32,24,1664]{2,1,0:T(8,128)(2,1)S(1)} all-to-all(bf16[32,24,1664]{2,1,0:T(8,128)(2,1)S(1)} %broadcast_in_dim.8), channel_id=1, replica_groups=mesh['ea'=32,'half'=2,'core'=2] {'ea'}, dimensions={0} | all-to-all | bytes 5111808 | tf_op jit(solution)/shard_map/all_to_all | solution.py:92
  53.7 3.9 shard_map.169
  58.3 29.3 %all_to_all.89 = bf16[64,16,768]{2,1,0:T(8,128)(2,1)} all-to-all(bf16[64,16,768]{2,1,0:T(8,128)(2,1)S(1)} %bitcast.123), channel_id=1, replica_groups=mesh['ea'=32,'half'=2,'core'=2] {'ea','half'}, dimensions={0} | all-to-all | bytes 3145728 | tf_op jit(solution)/shard_map/all_to_all | solution.py:42
  91.7 4.1 all-to-all-start.3
  99.1 7.3 %shard_map.171 = (bf16[1024,768]{1,0:T(8,128)(2,1)S(1)}, bf16[1024,768]{1,0:T(8,128)(2,1)S(1)}, bf16[1024,768]{1,0:T(8,128)(2,1)}) custom-call(bf16[1024,768]{1,0:T(8,128)(2,1)} %collective-permute-done.1.rows, bf16[2,1,768,768]{3,2,1,0:T(8,128)(2,1)S(1)} %copy-done.46, bf16[2,1,768,768]{3,2,1,0:T(8,128)(2,1)S(1)} %copy-done.49), custom_call_target="tpu_custom_call" | custom-call | flops 2415919104 | bytes 8650752 | tf_op jit(solution)/shard_map/pallas_call | solution.py:358
  110.5 6.4 %shard_map.170 = (bf16[1024,768]{1,0:T(8,128)(2,1)S(1)}, bf16[1024,768]{1,0:T(8,128)(2,1)S(1)}, bf16[1024,768]{1,0:T(8,128)(2,1)S(1)}) custom-call(bf16[1024,768]{1,0:T(8,128)(2,1)} %bitcast.13.rows, bf16[2,1,768,768]{3,2,1,0:T(8,128)(2,1)S(1)} %copy-done.46, bf16[2,1,768,768]{3,2,1,0:T(8,128)(2,1)S(1)} %copy-done.49), custom_call_target="tpu_custom_call" | custom-call | flops 2415919104 | bytes 8650752 | tf_op jit(solution)/shard_map/pallas_call | solution.py:358
  120.4 10.7 %all-to-all-done.3 = bf16[32,24,1664]{2,1,0:T(8,128)(2,1)S(1)} async-done(((bf16[32,24,1664]{2,1,0:T(8,128)(2,1)}), bf16[32,24,1664]{2,1,0:T(8,128)(2,1)S(1)}, u32[]{:S(2)}, u32[]{:S(2)}) %all-to-all-start.3) | async-done | bytes 2555936 | tf_op jit(solution)/shard_map/all_to_all | solution.py:92
  135.4 6.7 %all-to-all-start.2 = ((bf16[64,16,768]{2,1,0:T(8,128)(2,1)}), bf16[64,16,768]{2,1,0:T(8,128)(2,1)}, u32[]{:S(2)}, u32[]{:S(2)}) async-start(bf16[64,16,768]{2,1,0:T(8,128)(2,1)} %bitcast.124), calls=%async_computation.2 | async-start | bytes 3145728 | tf_op jit(solution)/shard_map/all_to_all | solution.py:42
  142.0 5.1 and_convert_fusion.1
  149.1 16.4 %all-to-all-done.2 = bf16[64,16,768]{2,1,0:T(8,128)(2,1)} async-done(((bf16[64,16,768]{2,1,0:T(8,128)(2,1)}), bf16[64,16,768]{2,1,0:T(8,128)(2,1)}, u32[]{:S(2)}, u32[]{:S(2)}) %all-to-all-start.2) | async-done | bytes 1572896 | tf_op jit(solution)/shard_map/all_to_all | solution.py:42
  168.9 6.0 %shard_map.172 = (bf16[197,768]{1,0:T(8,128)(2,1)S(1)}, bf16[197,1152]{1,0:T(8,128)(2,1)S(1)}, bf16[197,1152]{1,0:T(8,128)(2,1)S(1)}, bf16[197,768]{1,0:T(8,128)...) custom-call(s32[1]{0:T(128)} %bitcast.core_ref, ...), custom_call_target="tpu_custom_call" | custom-call | flops 1048576 | bytes 65536 | tf_op jit(solution)/shard_map/pallas_call | solution.py:251
  179.1 43.2 %all_to_all.90 = bf16[64,32,768]{2,1,0:T(8,128)(2,1)S(1)} all-to-all(bf16[64,32,768]{2,1,0:T(8,128)(2,1)S(1)} %bitcast.125), channel_id=1, replica_groups=mesh['ea'=32,'half'=2,'core'=2] {'ea','half'}, dimensions={0} | all-to-all | bytes 6291456 | tf_op jit(solution)/shard_map/all_to_all | solution.py:42
  225.8 5.3 collective-permute-done.4.rows
  231.1 7.5 %shard_map.174 = (bf16[1024,768]{1,0:T(8,128)(2,1)S(1)}, bf16[1024,768]{1,0:T(8,128)(2,1)S(1)}, bf16[64,2,16,768]{3,2,1,0:T(8,128)(2,1)S(1)}) custom-call(bf16[64,2,16,768]{3,2,1,0:T(8,128)(2,1)S(1)} %collective-permute-done.4.rows, bf16[2,1,768,768]{3,2,1,0:T(8,128)(2,1)S(1)} %copy-done.47, bf16[2,1,768,768]{3,2,1,0:T(8,128)(2,1)S(1)} %copy-done.50), custom_call_target="tpu_custom_call" | custom-call | flops 4831838208 | bytes 8650752 | tf_op jit(solution)/shard_map/pallas_call | solution.py:358
  239.1 7.5 %shard_map.173 = (bf16[1024,768]{1,0:T(8,128)(2,1)S(1)}, bf16[1024,768]{1,0:T(8,128)(2,1)S(1)}, bf16[64,2,16,768]{3,2,1,0:T(8,128)(2,1)S(1)}) custom-call(bf16[64,2,16,768]{3,2,1,0:T(8,128)(2,1)S(1)} %bitcast.116, bf16[2,1,768,768]{3,2,1,0:T(8,128)(2,1)S(1)} %copy-done.47, bf16[2,1,768,768]{3,2,1,0:T(8,128)(2,1)S(1)} %copy-done.50), custom_call_target="tpu_custom_call" | custom-call | flops 4831838208 | bytes 8650752 | tf_op jit(solution)/shard_map/pallas_call | solution.py:358
  250.6 5.6 %all-to-all-start.5 = ((bf16[64,32,768]{2,1,0:T(8,128)(2,1)}), bf16[64,32,768]{2,1,0:T(8,128)(2,1)}, u32[]{:S(2)}, u32[]{:S(2)}) async-start(bf16[64,32,768]{2,1,0:T(8,128)(2,1)} %bitcast.120), calls=%async_computation.5 | async-start | bytes 6291456 | tf_op jit(solution)/shard_map/all_to_all | solution.py:42
  272.8 24.7 %all-to-all-done.5 = bf16[64,32,768]{2,1,0:T(8,128)(2,1)} async-done(((bf16[64,32,768]{2,1,0:T(8,128)(2,1)}), bf16[64,32,768]{2,1,0:T(8,128)(2,1)}, u32[]{:S(2)}, u32[]{:S(2)}) %all-to-all-start.5) | async-done | bytes 3145760 | tf_op jit(solution)/shard_map/all_to_all | solution.py:42
  297.5 4.7 fusion.21
  304.6 11.0 %shard_map.175 = (f32[197,768]{1,0:T(8,128)S(1)}, bf16[197,768]{1,0:T(8,128)(2,1)S(1)}, bf16[197,1152]{1,0:T(8,128)(2,1)S(1)}, bf16[197,1152]{1,0:T(8,128)(2,1)S(1)}, f32[4,768]{1,0:T(4,128)S(1)}) custom-call(s32[1]{0:T(128)} %bitcast.core_ref, f32[197,768]{1,0:T(8,128)S(1)} %copy-done.10, f32[197,768]{1,0:T(8,128)S(1)} %convolution_add_fusion.5.grad_two, ...), custom_call_target="tpu_custom_call" | custom-call | flops 1048576 | bytes 65536 | tf_op jit(solution)/shard_map/pallas_call | solution.py:251
  332.4 5.9 %all-to-all-start.6 = ((bf16[64,16,768]{2,1,0:T(8,128)(2,1)}), bf16[64,16,768]{2,1,0:T(8,128)(2,1)}, u32[]{:S(2)}, u32[]{:S(2)}) async-start(bf16[64,16,768]{2,1,0:T(8,128)(2,1)} %bitcast.131), calls=%async_computation.6 | async-start | bytes 3145728 | tf_op jit(solution)/shard_map/all_to_all | solution.py:42
  338.3 3.9 add_convert_fusion.2
  342.2 19.5 %all-to-all-done.6 = bf16[64,16,768]{2,1,0:T(8,128)(2,1)} async-done(((bf16[64,16,768]{2,1,0:T(8,128)(2,1)}), bf16[64,16,768]{2,1,0:T(8,128)(2,1)}, u32[]{:S(2)}, u32[]{:S(2)}) %all-to-all-start.6) | async-done | bytes 1572896 | tf_op jit(solution)/shard_map/all_to_all | solution.py:42
  376.5 4.2 shard_map.177
  382.4 5.1 all-to-all-start.7
  388.2 22.6 %all-to-all-done.7 = bf16[64,16,768]{2,1,0:T(8,128)(2,1)S(1)} async-done(((bf16[64,16,768]{2,1,0:T(8,128)(2,1)}), bf16[64,16,768]{2,1,0:T(8,128)(2,1)S(1)}, u32[]{:S(2)}, u32[]{:S(2)}) %all-to-all-start.7) | async-done | bytes 1572896 | tf_op jit(solution)/shard_map/all_to_all | solution.py:42
  414.2 9.9 %shard_map.179 = (f32[197,768]{1,0:T(8,128)}, bf16[197,768]{1,0:T(8,128)(2,1)S(1)}, bf16[197,1152]{1,0:T(8,128)(2,1)S(1)}, bf16[197,1152]{1,0:T(8,128)(2,1)S(1)}, f32[4,768]{1,0:T(4,128)S(1)}) custom-call(s32[1]{0:T(128)} %bitcast.core_ref, f32[197,768]{1,0:T(8,128)S(1)} %copy-done.18, f32[197,768]{1,0:T(8,128)S(1)} %convolution_add_fusion.4.grad_two, ...), custom_call_target="tpu_custom_call" | custom-call | flops 1048576 | bytes 65536 | tf_op jit(solution)/shard_map/pallas_call | solution.py:251
  432.7 4.8 all-to-all-start.8
  437.5 3.8 add_convert_fusion.1
  441.3 31.7 %all-to-all-done.8 = bf16[32,24,1664]{2,1,0:T(8,128)(2,1)} async-done(((bf16[32,24,1664]{2,1,0:T(8,128)(2,1)}), bf16[32,24,1664]{2,1,0:T(8,128)(2,1)}, u32[]{:S(2)}, u32[]{:S(2)}) %all-to-all-start.8) | async-done | bytes 2555936 | tf_op jit(solution)/shard_map/all_to_all | solution.py:130
  472.9 6.1 %all-to-all-start.9 = ((bf16[32,24,1664]{2,1,0:T(8,128)(2,1)}), bf16[32,24,1664]{2,1,0:T(8,128)(2,1)}, u32[]{:S(2)}, u32[]{:S(2)}) async-start(bf16[32,24,1664]{2,1,0:T(8,128)(2,1)} %bitcast.122), calls=%async_computation.9 | async-start | bytes 5111808 | tf_op jit(solution)/shard_map/all_to_all | solution.py:130
  501.7 14.9 %collective-permute-done.15 = f32[24,1536]{1,0:T(8,128)S(1)} collective-permute-done((f32[24,1536]{1,0:T(8,128)S(1)}, f32[24,1536]{1,0:T(8,128)S(1)}, u32[]{:S(2)}, u32[]{:S(2)}) %collective-permute-start.15) | collective-permute-done | bytes 147488 | tf_op jit(solution)/shard_map/ppermute | solution.py:136
  523.6 6.1 %collective-permute-done.13 = f32[24,1536]{1,0:T(8,128)S(1)} collective-permute-done((f32[24,1536]{1,0:T(8,128)S(1)}, f32[24,1536]{1,0:T(8,128)S(1)}, u32[]{:S(2)}, u32[]{:S(2)}) %collective-permute-start.13) | collective-permute-done | bytes 147488 | tf_op jit(solution)/shard_map/ppermute | solution.py:136
  (329 shorter events, 146.2 us)
Async XLA Ops:
  5.0 44.2 %copy-start.88 = (bf16[197,768]{1,0:T(8,128)(2,1)S(1)}, bf16[197,768]{1,0:T(8,128)(2,1)}, u32[]{:S(2)}) copy-start(bf16[197,768]{1,0:T(8,128)(2,1)} %param.10) | copy-start | bytes 907780
  5.1 44.2 %copy-start.89 = (s32[2,197,2]{1,2,0:T(2,128)S(1)}, s32[2,197,2]{1,2,0:T(2,128)}, u32[]{:S(2)}) copy-start(s32[2,197,2]{1,2,0:T(2,128)} %param.12) | copy-start | bytes 9460
  46.5 7.2 %collective-permute-start = (bf16[768,1664]{1,0:T(8,128)(2,1)S(1)}, bf16[768,1664]{1,0:T(8,128)(2,1)S(1)}, u32[]{:S(2)}, u32[]{:S(2)}) collective-permute-start(bf16[768,1664]{1,0:T(8,128)(2,1)S(1)} %bitcast.111), channel_id=1, source_target_pairs={{0,1},{1,0},{2,3},{3,2},{4,5},{5,4},{6,7},{7,6},{8,9},{9,8},{10,11... | collective-permute-start | bytes 7667720 | tf_op jit(solution)/shard_map/ppermute | solution.py:38
  57.6 30.0 %copy-start.11 = (f32[197,768]{1,0:T(8,128)}, f32[197,768]{1,0:T(8,128)S(1)}, u32[]{:S(2)}) copy-start(f32[197,768]{1,0:T(8,128)S(1)} %get-tuple-element.73.after) | copy-start | bytes 1815556
  57.6 30.0 %copy-start.24 = (bf16[197,1152]{1,0:T(8,128)(2,1)}, bf16[197,1152]{1,0:T(8,128)(2,1)S(1)}, u32[]{:S(2)}) copy-start(bf16[197,1152]{1,0:T(8,128)(2,1)S(1)} %get-tuple-element.105.proj_o) | copy-start | bytes 1361668
  57.7 30.0 %copy-start.26 = (bf16[197,1152]{1,0:T(8,128)(2,1)}, bf16[197,1152]{1,0:T(8,128)(2,1)S(1)}, u32[]{:S(2)}) copy-start(bf16[197,1152]{1,0:T(8,128)(2,1)S(1)} %get-tuple-element.106.proj_x) | copy-start | bytes 1361668
  57.7 30.0 %copy-start.32 = (bf16[197,768]{1,0:T(8,128)(2,1)}, bf16[197,768]{1,0:T(8,128)(2,1)S(1)}, u32[]{:S(2)}) copy-start(bf16[197,768]{1,0:T(8,128)(2,1)S(1)} %get-tuple-element.108.normed) | copy-start | bytes 907780
  87.7 8.0 %collective-permute-start.1 = (bf16[1024,768]{1,0:T(8,128)(2,1)}, bf16[1024,768]{1,0:T(8,128)(2,1)}, u32[]{:S(2)}, u32[]{:S(2)}) collective-permute-start(bf16[1024,768]{1,0:T(8,128)(2,1)} %bitcast.13.rows), channel_id=1, source_target_pairs={{0,1},{1,0},{2,3},{3,2},{4,5},{5,4},{6,7},{7,6},{8,9},{9,8},{10,11... | collective-permute-start | bytes 4718600 | tf_op jit(solution)/shard_map/ppermute | solution.py:38
  91.7 39.5 %all-to-all-start.3 = ((bf16[32,24,1664]{2,1,0:T(8,128)(2,1)}), bf16[32,24,1664]{2,1,0:T(8,128)(2,1)S(1)}, u32[]{:S(2)}, u32[]{:S(2)}) async-start(bf16[32,24,1664]{2,1,0:T(8,128)(2,1)} %broadcast_in_dim.9), calls=%async_computation.3 | async-start | bytes 5111808 | tf_op jit(solution)/shard_map/all_to_all | solution.py:92
  108.8 23.2 %collective-permute-start.2 = (bf16[1024,768]{1,0:T(8,128)(2,1)}, bf16[1024,768]{1,0:T(8,128)(2,1)}, u32[]{:S(2)}, u32[]{:S(2)}) collective-permute-start(bf16[1024,768]{1,0:T(8,128)(2,1)} %get-tuple-element.77), channel_id=1, source_target_pairs={{0,1},{1,0},{2,3},{3,2},{4,5},{5,4},{6,7},{7,6},{8,9},{9,8},{10,11... | collective-permute-start | bytes 4718600 | tf_op jit(solution)/shard_map/ppermute | solution.py:38
  109.7 39.1 %copy-start.83 = (f32[394,32]{1,0:T(8,128)}, f32[394,32]{1,0:T(8,128)S(1)}, u32[]{:S(2)}) copy-start(f32[394,32]{1,0:T(8,128)S(1)} %fusion.53) | copy-start | bytes 151300
  131.2 37.8 %collective-permute-start.3 = (bf16[768,1664]{1,0:T(8,128)(2,1)S(1)}, bf16[768,1664]{1,0:T(8,128)(2,1)}, u32[]{:S(2)}, u32[]{:S(2)}) collective-permute-start(bf16[768,1664]{1,0:T(8,128)(2,1)S(1)} %bitcast.107), channel_id=1, source_target_pairs={{0,1},{1,0},{2,3},{3,2},{4,5},{5,4},{6,7},{7,6},{8,9},{9,8},{10,11... | collective-permute-start | bytes 7667720 | tf_op jit(solution)/shard_map/ppermute | solution.py:38
  135.4 30.1 %all-to-all-start.2 = ((bf16[64,16,768]{2,1,0:T(8,128)(2,1)}), bf16[64,16,768]{2,1,0:T(8,128)(2,1)}, u32[]{:S(2)}, u32[]{:S(2)}) async-start(bf16[64,16,768]{2,1,0:T(8,128)(2,1)} %bitcast.124), calls=%async_computation.2 | async-start | bytes 3145728 | tf_op jit(solution)/shard_map/all_to_all | solution.py:42
  179.1 52.0 %copy-start.47 = (bf16[2,1,768,768]{3,2,1,0:T(8,128)(2,1)S(1)}, bf16[2,1,768,768]{3,2,1,0:T(8,128)(2,1)}, u32[]{:S(2)}) copy-start(bf16[2,1,768,768]{3,2,1,0:T(8,128)(2,1)} %w_in.11) | copy-start | bytes 7077892
  179.1 52.0 %copy-start.50 = (bf16[2,1,768,768]{3,2,1,0:T(8,128)(2,1)S(1)}, bf16[2,1,768,768]{3,2,1,0:T(8,128)(2,1)}, u32[]{:S(2)}) copy-start(bf16[2,1,768,768]{3,2,1,0:T(8,128)(2,1)} %w_out.11) | copy-start | bytes 7077892
  222.3 8.8 %collective-permute-start.4 = (bf16[64,2,16,768]{3,2,1,0:T(8,128)(2,1)S(1)}, bf16[64,2,16,768]{3,2,1,0:T(8,128)(2,1)S(1)}, u32[]{:S(2)}, u32[]{:S(2)}) collective-permute-start(bf16[64,2,16,768]{3,2,1,0:T(8,128)(2,1)S(1)} %bitcast.115), channel_id=1, source_target_pairs={{0,1},{1,0},{2,3},{3,2},{4,5},{5,4},{6,7},{7,6},{8,9},{9,8},{10,11... | collective-permute-start | bytes 9437192 | tf_op jit(solution)/shard_map/ppermute | solution.py:38
  238.6 9.2 %collective-permute-start.5 = (bf16[64,2,16,768]{3,2,1,0:T(8,128)(2,1)S(1)}, bf16[64,2,16,768]{3,2,1,0:T(8,128)(2,1)S(1)}, u32[]{:S(2)}, u32[]{:S(2)}) collective-permute-start(bf16[64,2,16,768]{3,2,1,0:T(8,128)(2,1)S(1)} %get-tuple-element.83), channel_id=1, source_target_pairs={{0,1},{1,0},{2,3},{3,2},{4,5},{5,4},{6,7},{7,6},{8,9},{9,8},{10,11... | collective-permute-start | bytes 9437192 | tf_op jit(solution)/shard_map/ppermute | solution.py:38
  250.6 46.9 %all-to-all-start.5 = ((bf16[64,32,768]{2,1,0:T(8,128)(2,1)}), bf16[64,32,768]{2,1,0:T(8,128)(2,1)}, u32[]{:S(2)}, u32[]{:S(2)}) async-start(bf16[64,32,768]{2,1,0:T(8,128)(2,1)} %bitcast.120), calls=%async_computation.5 | async-start | bytes 6291456 | tf_op jit(solution)/shard_map/all_to_all | solution.py:42
  327.0 11.2 %collective-permute-start.6 = (bf16[768,1664]{1,0:T(8,128)(2,1)}, bf16[768,1664]{1,0:T(8,128)(2,1)}, u32[]{:S(2)}, u32[]{:S(2)}) collective-permute-start(bf16[768,1664]{1,0:T(8,128)(2,1)} %get-tuple-element.99), channel_id=1, source_target_pairs={{0,1},{1,0},{2,3},{3,2},{4,5},{5,4},{6,7},{7,6},{8,9},{9,8},{10,11... | collective-permute-start | bytes 7667720 | tf_op jit(solution)/shard_map/ppermute | solution.py:38
  332.4 29.3 %all-to-all-start.6 = ((bf16[64,16,768]{2,1,0:T(8,128)(2,1)}), bf16[64,16,768]{2,1,0:T(8,128)(2,1)}, u32[]{:S(2)}, u32[]{:S(2)}) async-start(bf16[64,16,768]{2,1,0:T(8,128)(2,1)} %bitcast.131), calls=%async_computation.6 | async-start | bytes 3145728 | tf_op jit(solution)/shard_map/all_to_all | solution.py:42
  361.7 4.8 collective-permute-start.7
  376.1 4.6 collective-permute-start.8
  382.4 28.5 %all-to-all-start.7 = ((bf16[64,16,768]{2,1,0:T(8,128)(2,1)}), bf16[64,16,768]{2,1,0:T(8,128)(2,1)S(1)}, u32[]{:S(2)}, u32[]{:S(2)}) async-start(bf16[64,16,768]{2,1,0:T(8,128)(2,1)} %bitcast.38), calls=%async_computation.7 | async-start | bytes 3145728 | tf_op jit(solution)/shard_map/all_to_all | solution.py:42
  431.0 6.5 %collective-permute-start.9 = (bf16[768,1664]{1,0:T(8,128)(2,1)}, bf16[768,1664]{1,0:T(8,128)(2,1)}, u32[]{:S(2)}, u32[]{:S(2)}) collective-permute-start(bf16[768,1664]{1,0:T(8,128)(2,1)} %get-tuple-element.115), channel_id=1, source_target_pairs={{0,1},{1,0},{2,3},{3,2},{4,5},{5,4},{6,7},{7,6},{8,9},{9,8},{10,11... | collective-permute-start | bytes 7667720 | tf_op jit(solution)/shard_map/ppermute | solution.py:38
  432.7 40.3 %all-to-all-start.8 = ((bf16[32,24,1664]{2,1,0:T(8,128)(2,1)}), bf16[32,24,1664]{2,1,0:T(8,128)(2,1)}, u32[]{:S(2)}, u32[]{:S(2)}) async-start(bf16[32,24,1664]{2,1,0:T(8,128)(2,1)} %bitcast.121), calls=%async_computation.8 | async-start | bytes 5111808 | tf_op jit(solution)/shard_map/all_to_all | solution.py:130
  472.9 43.9 %all-to-all-start.9 = ((bf16[32,24,1664]{2,1,0:T(8,128)(2,1)}), bf16[32,24,1664]{2,1,0:T(8,128)(2,1)}, u32[]{:S(2)}, u32[]{:S(2)}) async-start(bf16[32,24,1664]{2,1,0:T(8,128)(2,1)} %bitcast.122), calls=%async_computation.9 | async-start | bytes 5111808 | tf_op jit(solution)/shard_map/all_to_all | solution.py:130
  491.9 24.8 %collective-permute-start.11 = (f32[24,1664]{1,0:T(8,128)S(1)}, f32[24,1664]{1,0:T(8,128)S(1)}, u32[]{:S(2)}, u32[]{:S(2)}) collective-permute-start(f32[24,1664]{1,0:T(8,128)S(1)} %convert_reduce_fusion), channel_id=1, source_target_pairs={{0,2},{1,3},{2,0},{3,1},{4,6},{5,7},{6,4},{7,5},{8,10},{9,11},{10,... | collective-permute-start | bytes 479240 | tf_op jit(solution)/shard_map/ppermute | solution.py:136
  493.0 8.7 %collective-permute-start.14 = (f32[24,1536]{1,0:T(8,128)S(1)}, f32[24,1536]{1,0:T(8,128)S(1)}, u32[]{:S(2)}, u32[]{:S(2)}) collective-permute-start(f32[24,1536]{1,0:T(8,128)S(1)} %slice.347), channel_id=1, source_target_pairs={{0,1},{1,0},{2,3},{3,2},{4,5},{5,4},{6,7},{7,6},{8,9},{9,8},{10,11... | collective-permute-start | bytes 442376 | tf_op jit(solution)/shard_map/ppermute | solution.py:136
  494.3 22.4 %collective-permute-start.15 = (f32[24,1536]{1,0:T(8,128)S(1)}, f32[24,1536]{1,0:T(8,128)S(1)}, u32[]{:S(2)}, u32[]{:S(2)}) collective-permute-start(f32[24,1536]{1,0:T(8,128)S(1)} %slice.347), channel_id=1, source_target_pairs={{0,3},{1,2},{2,1},{3,0},{4,7},{5,6},{6,5},{7,4},{8,11},{9,10},{10,... | collective-permute-start | bytes 442376 | tf_op jit(solution)/shard_map/ppermute | solution.py:136
  518.9 10.9 %collective-permute-start.10 = (f32[24,1664]{1,0:T(8,128)S(1)}, f32[24,1664]{1,0:T(8,128)S(1)}, u32[]{:S(2)}, u32[]{:S(2)}) collective-permute-start(f32[24,1664]{1,0:T(8,128)S(1)} %convert_reduce_fusion.1), channel_id=1, source_target_pairs={{0,2},{1,3},{2,0},{3,1},{4,6},{5,7},{6,4},{7,5},{8,10},{9,11},{10,... | collective-permute-start | bytes 479240 | tf_op jit(solution)/shard_map/ppermute | solution.py:136
  522.2 1.5 collective-permute-start.12
  522.3 7.5 %collective-permute-start.13 = (f32[24,1536]{1,0:T(8,128)S(1)}, f32[24,1536]{1,0:T(8,128)S(1)}, u32[]{:S(2)}, u32[]{:S(2)}) collective-permute-start(f32[24,1536]{1,0:T(8,128)S(1)} %slice.340), channel_id=1, source_target_pairs={{0,3},{1,2},{2,1},{3,0},{4,7},{5,6},{6,5},{7,4},{8,11},{9,10},{10,... | collective-permute-start | bytes 442376 | tf_op jit(solution)/shard_map/ppermute | solution.py:136
  (81 other events, 314.5 us)

commit v5 on v4

--- a/solution.py
+++ b/solution.py
@@ -86,9 +86,9 @@
 
 def gather_cols(mine, after=None):
     groups = lax.axis_size("ea")
+    sent = jnp.broadcast_to(mine[None], (groups,) + mine.shape)
     if after is not None:
-        mine, _ = lax.optimization_barrier((mine, after))
-    sent = jnp.broadcast_to(mine[None], (groups,) + mine.shape)
+        sent, _ = lax.optimization_barrier((sent, after))
     got = lax.all_to_all(sent, "ea", split_axis=0, concat_axis=0)
     return got.reshape(-1, mine.shape[1])
 
@@ -123,10 +123,8 @@
     return (own.astype(F32) + swap_core(give).astype(F32)).astype(BF)
 
 
-def sum_exchange(pair, after=None):
+def sum_exchange(pair):
     groups = lax.axis_size("ea")
-    if after is not None:
-        pair, _ = lax.optimization_barrier((pair, after))
     return lax.all_to_all(
         pair.reshape(groups, -1, pair.shape[1]), "ea", split_axis=0, concat_axis=0
     )
@@ -255,7 +253,7 @@
         out_shape=[jax.ShapeDtypeStruct(shape, kind) for shape, kind in outs],
         scratch_shapes=list(scratch),
         compiler_params=pltpu.CompilerParams(vmem_limit_bytes=VMEM),
-        cost_estimate=pl.CostEstimate(flops=flops, bytes_accessed=1 << 16, transcendentals=0),
+        cost_estimate=pl.CostEstimate(flops=flops, bytes_accessed=8 << 20, transcendentals=0),
     )(core, *args)
 
 
@@ -269,7 +267,7 @@
             rows(width, BF), rows(1152, BF), rows(1152, BF), rows(width, BF), rows(width, F32),
             rows(width, BF), rows(128, F32),
         ],
-        1 << 20,
+        4 * tokens * width * (4 * width + 4 * tokens),
     )
     return after, normed_two, logits, (state, normed, proj_o, proj_x, mixed, after)
 
@@ -282,7 +280,7 @@
         functools.partial(attend_back_kernel, lax.axis_size("ea")),
         [grad, grad_two, state, after, proj_o, proj_x, *dense],
         [rows(width, F32), rows(width, BF), rows(1152, BF), rows(1152, BF), ((4, width), F32)],
-        1 << 20,
+        8 * tokens * width * (4 * width + 8 * tokens),
         [pltpu.VMEM((tokens, width), BF)],
     )
     return grad_in, stats, (normed, gp_o, gp_x, mixed, grad_attn)
@@ -506,7 +504,6 @@
     grad_rows = jnp.concatenate([(g * grad).astype(BF) for g in gate0], axis=0)
     arrived = exchange(dot(send, grad_rows).astype(BF))
     pair1 = sum_send(*dense_grads(*terms1, small_grads(grad_router_w1, stats1)))
-    arrived, pair1 = lax.optimization_barrier((arrived, pair1))
     grows0 = (arrived, swap_core(arrived))
     third = [
         expert_call(backward_kernel, 0, [r, s], weights, [r.shape] * 2, 2)
@@ -514,15 +511,18 @@
     ]
     grad_pre0, part = zip(*third)
     returned = exchange(join_cores(*part))
-    parts1 = sum_exchange(pair1, after=returned)
+    returned, pair1 = lax.optimization_barrier((returned, pair1))
+    parts1 = sum_exchange(pair1)
     picked = dot(fetch, returned)
     grad_sent = picked[:tokens] + picked[tokens:]
     extra, grad_router_w0 = router_back(
         grad, picked0, router0, onehot0, normed0, dense0[0][:, 1536 : 1536 + experts]
     )
     grad, stats0, terms0 = attention_back(grad, grad_sent + extra, kept0, dense0)
-    pair0 = sum_send(*dense_grads(*terms0, small_grads(grad_router_w0, stats0)))
-    pair0, parts1 = lax.optimization_barrier((pair0, parts1))
+    grads0, parts1 = lax.optimization_barrier(
+        (dense_grads(*terms0, small_grads(grad_router_w0, stats0)), parts1)
+    )
+    pair0 = sum_send(*grads0)
     parts0 = sum_exchange(pair0)
     (hidden0, grows0, rows0, grad_pre0), _ = lax.optimization_barrier(
         ((hidden0, grows0, rows0, grad_pre0), pair0)

time: 544 us -> 531 us (0.976)
  waiting for transfers between devices: 159 us -> 114 us
  blocking collectives: 114 us -> 142 us
  local copies, waits for them, and re-layouts: 43.2 us -> 49.3 us
    all_to_all x2 -> x3, blocking collectives: 72.5 us -> 101 us  [exchange(): return lax.all_to_all(rows, GROUP, split_axis=0, concat_axis=0, tiled=True)]
    all_to_all x2, waiting for transfers between devices: 31.7 us -> 6.27 us  [sum_exchange(): lax.all_to_all(pair.reshape(groups, -1, pair.shape[1]), 'ea', split_axis=...]
    all_to_all x4 -> x3, waiting for transfers between devices: 83.2 us -> 58.7 us  [exchange(): return lax.all_to_all(rows, GROUP, split_axis=0, concat_axis=0, tiled=True)]
    unnamed x190 -> x272, local copies, waits for them, and re-layouts: 36.2 us -> 42.4 us
    all_to_all x4 -> x3, starting transfers between devices: 23.2 us -> 18.2 us  [exchange(): return lax.all_to_all(rows, GROUP, split_axis=0, concat_axis=0, tiled=True)]
  transfers between devices with their start and end apart: 23 -> 22, of which waited for: 12 -> 11; matrix products, arithmetic and copies ran while one was open for 12% -> 12% of each run, Pallas kernels for 5% -> 8%
where the time goes in v5:
time: 531 us; the launch traced here: 521 us
  blocking collectives  142 us (27%)
  waiting for transfers between devices  114 us (21%)
  Pallas kernels  72 us (14%)
  starting transfers between devices  58.6 us (11%)
  local copies, waits for them, and re-layouts  49.3 us (9%)
  other arithmetic  46.9 us (9%)
  matrix products  35 us (7%)
    all_to_all x3, blocking collectives, exchange(): return lax.all_to_all(rows, GROUP, split_axis=0, concat_axis=0, tiled=True)  101 us
    all_to_all x3, waiting for transfers between devices, exchange(): return lax.all_to_all(rows, GROUP, split_axis=0, concat_axis=0, tiled=True)  58.7 us
    unnamed x272, local copies, waits for them, and re-layouts  42.4 us
    all_to_all x1, blocking collectives, gather_cols(): got = lax.all_to_all(sent, 'ea', split_axis=0, concat_axis=0)  41.4 us
    pallas_call x6, Pallas kernels, expert_call(): pl.pallas_call(kernel, grid=(count // (GROUPS * SLOTS),), in_specs=[spec(...  35.9 us
    dot_general x16, matrix products, dot(): return lax.dot_general(a, b, (dims, ((), ())), preferred_element_type=F32)  33.2 us
    pallas_call x4, Pallas kernels, whole_call(): pl.pallas_call(kernel, in_specs=[pl.BlockSpec(memory_space=pltpu.SMEM)] +...  31 us
    ppermute x6, waiting for transfers between devices, swap_row(): lax.ppermute(value, ('half', 'core'), [(i, i ^ flip) for i in range(4)])  24.3 us
  transfers between devices with their start and end apart: 22, of which 11 were waited for; matrix products, arithmetic and copies ran while one was open for 12% of the time, Pallas kernels for 8%

profile of v5, /device:TPU:1, one launch (start us, length us, event | category | flops | bytes accessed | tf_op | source)
XLA Modules:
  0.0 521.4 jit_solution(15295813871308724459)
XLA Ops:
  5.1 41.4 %all_to_all.87 = bf16[32,24,1664]{2,1,0:T(8,128)(2,1)S(1)} all-to-all(bf16[32,24,1664]{2,1,0:T(8,128)(2,1)S(1)} %broadcast_in_dim.8), channel_id=1, replica_groups=mesh['ea'=32,'half'=2,'core'=2] {'ea'}, dimensions={0} | all-to-all | bytes 5111808 | tf_op jit(solution)/shard_map/all_to_all | solution.py:92
  53.7 3.9 shard_map.169
  58.3 29.3 %all_to_all.88 = bf16[64,16,768]{2,1,0:T(8,128)(2,1)} all-to-all(bf16[64,16,768]{2,1,0:T(8,128)(2,1)S(1)} %bitcast.126), channel_id=1, replica_groups=mesh['ea'=32,'half'=2,'core'=2] {'ea','half'}, dimensions={0} | all-to-all | bytes 3145728 | tf_op jit(solution)/shard_map/all_to_all | solution.py:42
  91.7 4.1 all-to-all-start.3
  99.1 7.3 %shard_map.171 = (bf16[1024,768]{1,0:T(8,128)(2,1)S(1)}, bf16[1024,768]{1,0:T(8,128)(2,1)S(1)}, bf16[1024,768]{1,0:T(8,128)(2,1)}) custom-call(bf16[1024,768]{1,0:T(8,128)(2,1)} %collective-permute-done.1.rows, bf16[2,1,768,768]{3,2,1,0:T(8,128)(2,1)S(1)} %copy-done.44, bf16[2,1,768,768]{3,2,1,0:T(8,128)(2,1)S(1)} %copy-done.48), custom_call_target="tpu_custom_call" | custom-call | flops 2415919104 | bytes 8650752 | tf_op jit(solution)/shard_map/pallas_call | solution.py:356
  110.5 6.4 %shard_map.170 = (bf16[1024,768]{1,0:T(8,128)(2,1)S(1)}, bf16[1024,768]{1,0:T(8,128)(2,1)S(1)}, bf16[1024,768]{1,0:T(8,128)(2,1)S(1)}) custom-call(bf16[1024,768]{1,0:T(8,128)(2,1)} %bitcast.13.rows, bf16[2,1,768,768]{3,2,1,0:T(8,128)(2,1)S(1)} %copy-done.44, bf16[2,1,768,768]{3,2,1,0:T(8,128)(2,1)S(1)} %copy-done.48), custom_call_target="tpu_custom_call" | custom-call | flops 2415919104 | bytes 8650752 | tf_op jit(solution)/shard_map/pallas_call | solution.py:356
  120.4 10.7 %all-to-all-done.3 = bf16[32,24,1664]{2,1,0:T(8,128)(2,1)S(1)} async-done(((bf16[32,24,1664]{2,1,0:T(8,128)(2,1)}), bf16[32,24,1664]{2,1,0:T(8,128)(2,1)S(1)}, u32[]{:S(2)}, u32[]{:S(2)}) %all-to-all-start.3) | async-done | bytes 2555936 | tf_op jit(solution)/shard_map/all_to_all | solution.py:92
  135.4 6.9 %all-to-all-start.2 = ((bf16[64,16,768]{2,1,0:T(8,128)(2,1)}), bf16[64,16,768]{2,1,0:T(8,128)(2,1)}, u32[]{:S(2)}, u32[]{:S(2)}) async-start(bf16[64,16,768]{2,1,0:T(8,128)(2,1)} %bitcast.127), calls=%async_computation.2 | async-start | bytes 3145728 | tf_op jit(solution)/shard_map/all_to_all | solution.py:42
  142.4 5.1 and_convert_fusion.1
  149.8 15.2 %all-to-all-done.2 = bf16[64,16,768]{2,1,0:T(8,128)(2,1)} async-done(((bf16[64,16,768]{2,1,0:T(8,128)(2,1)}), bf16[64,16,768]{2,1,0:T(8,128)(2,1)}, u32[]{:S(2)}, u32[]{:S(2)}) %all-to-all-start.2) | async-done | bytes 1572896 | tf_op jit(solution)/shard_map/all_to_all | solution.py:42
  168.4 6.0 %shard_map.172 = (bf16[197,768]{1,0:T(8,128)(2,1)S(1)}, bf16[197,1152]{1,0:T(8,128)(2,1)S(1)}, bf16[197,1152]{1,0:T(8,128)(2,1)S(1)}, bf16[197,768]{1,0:T(8,128)...) custom-call(s32[1]{0:T(128)} %bitcast.core_ref, ...), custom_call_target="tpu_custom_call" | custom-call | flops 2336010240 | bytes 8388608 | tf_op jit(solution)/shard_map/pallas_call | solution.py:249
  179.0 44.2 %all_to_all.89 = bf16[64,32,768]{2,1,0:T(8,128)(2,1)S(1)} all-to-all(bf16[64,32,768]{2,1,0:T(8,128)(2,1)S(1)} %bitcast.129), channel_id=1, replica_groups=mesh['ea'=32,'half'=2,'core'=2] {'ea','half'}, dimensions={0} | all-to-all | bytes 6291456 | tf_op jit(solution)/shard_map/all_to_all | solution.py:42
  226.8 5.3 %collective-permute-done.4.rows = bf16[64,2,16,768]{3,2,1,0:T(8,128)(2,1)S(1)} collective-permute-done((bf16[64,2,16,768]{3,2,1,0:T(8,128)(2,1)S(1)}, bf16[64,2,16,768]{3,2,1,0:T(8,128)(2,1)S(1)}, u32[]{:S(2)}, u32[]{:S(2)}) %collective-permute-start.4) | collective-permute-done | bytes 3145760 | tf_op jit(solution)/shard_map/ppermute | solution.py:38
  232.1 7.5 %shard_map.174 = (bf16[1024,768]{1,0:T(8,128)(2,1)S(1)}, bf16[1024,768]{1,0:T(8,128)(2,1)S(1)}, bf16[64,2,16,768]{3,2,1,0:T(8,128)(2,1)S(1)}) custom-call(bf16[64,2,16,768]{3,2,1,0:T(8,128)(2,1)S(1)} %collective-permute-done.4.rows, bf16[2,1,768,768]{3,2,1,0:T(8,128)(2,1)S(1)} %copy-done.45, bf16[2,1,768,768]{3,2,1,0:T(8,128)(2,1)S(1)} %copy-done.49), custom_call_target="tpu_custom_call" | custom-call | flops 4831838208 | bytes 8650752 | tf_op jit(solution)/shard_map/pallas_call | solution.py:356
  242.4 7.6 %shard_map.173 = (bf16[1024,768]{1,0:T(8,128)(2,1)S(1)}, bf16[1024,768]{1,0:T(8,128)(2,1)S(1)}, bf16[64,2,16,768]{3,2,1,0:T(8,128)(2,1)S(1)}) custom-call(bf16[64,2,16,768]{3,2,1,0:T(8,128)(2,1)S(1)} %bitcast.108, bf16[2,1,768,768]{3,2,1,0:T(8,128)(2,1)S(1)} %copy-done.45, bf16[2,1,768,768]{3,2,1,0:T(8,128)(2,1)S(1)} %copy-done.49), custom_call_target="tpu_custom_call" | custom-call | flops 4831838208 | bytes 8650752 | tf_op jit(solution)/shard_map/pallas_call | solution.py:356
  254.0 5.6 %all-to-all-start.5 = ((bf16[64,32,768]{2,1,0:T(8,128)(2,1)}), bf16[64,32,768]{2,1,0:T(8,128)(2,1)}, u32[]{:S(2)}, u32[]{:S(2)}) async-start(bf16[64,32,768]{2,1,0:T(8,128)(2,1)} %bitcast.123), calls=%async_computation.5 | async-start | bytes 6291456 | tf_op jit(solution)/shard_map/all_to_all | solution.py:42
  276.8 24.1 %all-to-all-done.5 = bf16[64,32,768]{2,1,0:T(8,128)(2,1)} async-done(((bf16[64,32,768]{2,1,0:T(8,128)(2,1)}), bf16[64,32,768]{2,1,0:T(8,128)(2,1)}, u32[]{:S(2)}, u32[]{:S(2)}) %all-to-all-start.5) | async-done | bytes 3145760 | tf_op jit(solution)/shard_map/all_to_all | solution.py:42
  300.9 4.1 fusion.21
  307.4 11.1 %shard_map.175 = (f32[197,768]{1,0:T(8,128)S(1)}, bf16[197,768]{1,0:T(8,128)(2,1)S(1)}, bf16[197,1152]{1,0:T(8,128)(2,1)S(1)}, bf16[197,1152]{1,0:T(8,128)(2,1)S(1)}, f32[4,768]{1,0:T(4,128)S(1)}) custom-call(s32[1]{0:T(128)} %bitcast.core_ref, f32[197,768]{1,0:T(8,128)S(1)} %copy-done.12, f32[197,768]{1,0:T(8,128)S(1)} %convolution_add_fusion.5.grad_two, ...), custom_call_target="tpu_custom_call" | custom-call | flops 5625790464 | bytes 8388608 | tf_op jit(solution)/shard_map/pallas_call | solution.py:249
  321.2 27.5 %all_to_all.90 = bf16[64,16,768]{2,1,0:T(8,128)(2,1)S(1)} all-to-all(bf16[64,16,768]{2,1,0:T(8,128)(2,1)S(1)} %bitcast.134), channel_id=1, replica_groups=mesh['ea'=32,'half'=2,'core'=2] {'ea','half'}, dimensions={0} | all-to-all | bytes 3145728 | tf_op jit(solution)/shard_map/all_to_all | solution.py:42
  354.7 4.0 shard_map.177
  381.9 5.7 %all-to-all-start.7 = ((bf16[64,16,768]{2,1,0:T(8,128)(2,1)}), bf16[64,16,768]{2,1,0:T(8,128)(2,1)}, u32[]{:S(2)}, u32[]{:S(2)}) async-start(bf16[64,16,768]{2,1,0:T(8,128)(2,1)} %bitcast.128), calls=%async_computation.7 | async-start | bytes 3145728 | tf_op jit(solution)/shard_map/all_to_all | solution.py:42
  391.5 19.4 %all-to-all-done.7 = bf16[64,16,768]{2,1,0:T(8,128)(2,1)} async-done(((bf16[64,16,768]{2,1,0:T(8,128)(2,1)}), bf16[64,16,768]{2,1,0:T(8,128)(2,1)}, u32[]{:S(2)}, u32[]{:S(2)}) %all-to-all-start.7) | async-done | bytes 1572896 | tf_op jit(solution)/shard_map/all_to_all | solution.py:42
  410.9 5.0 all-to-all-start.8
  420.1 9.9 %shard_map.179 = (f32[197,768]{1,0:T(8,128)}, bf16[197,768]{1,0:T(8,128)(2,1)S(1)}, bf16[197,1152]{1,0:T(8,128)(2,1)S(1)}, bf16[197,1152]{1,0:T(8,128)(2,1)S(1)}, f32[4,768]{1,0:T(4,128)S(1)}) custom-call(s32[1]{0:T(128)} %bitcast.core_ref, f32[197,768]{1,0:T(8,128)S(1)} %get-tuple-element.91.grad, f32[197,768]{1,0:T(8,128)S(1)} %convolution_add_fusion.4.grad_two, ...), custom_call_target="tpu_custom_call" | custom-call | flops 5625790464 | bytes 8388608 | tf_op jit(solution)/shard_map/pallas_call | solution.py:249
  441.0 6.3 %all-to-all-done.8 = bf16[32,24,1664]{2,1,0:T(8,128)(2,1)} async-done(((bf16[32,24,1664]{2,1,0:T(8,128)(2,1)}), bf16[32,24,1664]{2,1,0:T(8,128)(2,1)}, u32[]{:S(2)}, u32[]{:S(2)}) %all-to-all-start.8) | async-done | bytes 2555936 | tf_op jit(solution)/shard_map/all_to_all | solution.py:128
  447.3 5.5 %collective-permute-start.9 = (bf16[768,1664]{1,0:T(8,128)(2,1)}, bf16[768,1664]{1,0:T(8,128)(2,1)}, u32[]{:S(2)}, u32[]{:S(2)}) collective-permute-start(bf16[768,1664]{1,0:T(8,128)(2,1)} %copy-done.43), channel_id=1, source_target_pairs={{0,1},{1,0},{2,3},{3,2},{4,5},{5,4},{6,7},{7,6},{8,9},{9,8},{10,11... | collective-permute-start | bytes 7667720 | tf_op jit(solution)/shard_map/ppermute | solution.py:38
  452.7 4.8 collective-permute-done.9
  457.5 3.8 add_convert_fusion.1
  461.4 5.2 %all-to-all-start.9 = ((bf16[32,24,1664]{2,1,0:T(8,128)(2,1)}), bf16[32,24,1664]{2,1,0:T(8,128)(2,1)}, u32[]{:S(2)}, u32[]{:S(2)}) async-start(bf16[32,24,1664]{2,1,0:T(8,128)(2,1)} %bitcast.124), calls=%async_computation.9 | async-start | bytes 5111808 | tf_op jit(solution)/shard_map/all_to_all | solution.py:128
  487.3 17.2 %collective-permute-done.15 = f32[24,1536]{1,0:T(8,128)S(1)} collective-permute-done((f32[24,1536]{1,0:T(8,128)S(1)}, f32[24,1536]{1,0:T(8,128)S(1)}, u32[]{:S(2)}, u32[]{:S(2)}) %collective-permute-start.15) | collective-permute-done | bytes 147488 | tf_op jit(solution)/shard_map/ppermute | solution.py:134
  510.3 7.0 %collective-permute-done.13 = f32[24,1536]{1,0:T(8,128)S(1)} collective-permute-done((f32[24,1536]{1,0:T(8,128)S(1)}, f32[24,1536]{1,0:T(8,128)S(1)}, u32[]{:S(2)}, u32[]{:S(2)}) %collective-permute-start.13) | collective-permute-done | bytes 147488 | tf_op jit(solution)/shard_map/ppermute | solution.py:134
  (410 shorter events, 151.6 us)
Async XLA Ops:
  5.0 44.2 %copy-start.98 = (bf16[197,768]{1,0:T(8,128)(2,1)S(1)}, bf16[197,768]{1,0:T(8,128)(2,1)}, u32[]{:S(2)}) copy-start(bf16[197,768]{1,0:T(8,128)(2,1)} %param.10) | copy-start | bytes 907780
  5.1 44.2 %copy-start.128 = (s32[2,197,2]{1,2,0:T(2,128)S(1)}, s32[2,197,2]{1,2,0:T(2,128)}, u32[]{:S(2)}) copy-start(s32[2,197,2]{1,2,0:T(2,128)} %param.12) | copy-start | bytes 9460
  46.5 7.2 %collective-permute-start = (bf16[768,1664]{1,0:T(8,128)(2,1)S(1)}, bf16[768,1664]{1,0:T(8,128)(2,1)S(1)}, u32[]{:S(2)}, u32[]{:S(2)}) collective-permute-start(bf16[768,1664]{1,0:T(8,128)(2,1)S(1)} %bitcast.114), channel_id=1, source_target_pairs={{0,1},{1,0},{2,3},{3,2},{4,5},{5,4},{6,7},{7,6},{8,9},{9,8},{10,11... | collective-permute-start | bytes 7667720 | tf_op jit(solution)/shard_map/ppermute | solution.py:38
  49.3 115.7 %copy-start.129 = (pred[1024]{0:T(1024)(128)(4,1)}, pred[1024]{0:T(1024)(128)(4,1)S(1)}, u32[]{:S(2)}) copy-start(pred[1024]{0:T(1024)(128)(4,1)S(1)} %fusion.89) | copy-start | bytes 3076
  49.4 115.6 %copy-start.108 = (s32[1024]{0:T(1024)}, s32[1024]{0:T(1024)S(1)}, u32[]{:S(2)}) copy-start(s32[1024]{0:T(1024)S(1)} %broadcast_add_fusion.1) | copy-start | bytes 12292
  49.4 115.6 %copy-start.110 = (s32[1024]{0:T(1024)}, s32[1024]{0:T(1024)S(1)}, u32[]{:S(2)}) copy-start(s32[1024]{0:T(1024)S(1)} %get-tuple-element.217) | copy-start | bytes 12292
  49.4 115.6 %copy-start.112 = (s32[1024]{0:T(1024)}, s32[1024]{0:T(1024)S(1)}, u32[]{:S(2)}) copy-start(s32[1024]{0:T(1024)S(1)} %get-tuple-element.218) | copy-start | bytes 12292
  50.0 115.0 %copy-start.126 = (s32[394]{0:T(512)}, s32[394]{0:T(512)S(1)}, u32[]{:S(2)}) copy-start(s32[394]{0:T(512)S(1)} %convert_add_fusion.1) | copy-start | bytes 4732
  57.7 109.6 %copy-start.13 = (f32[197,768]{1,0:T(8,128)}, f32[197,768]{1,0:T(8,128)S(1)}, u32[]{:S(2)}) copy-start(f32[197,768]{1,0:T(8,128)S(1)} %get-tuple-element.73.after) | copy-start | bytes 1815556
  87.7 8.0 %collective-permute-start.1 = (bf16[1024,768]{1,0:T(8,128)(2,1)}, bf16[1024,768]{1,0:T(8,128)(2,1)}, u32[]{:S(2)}, u32[]{:S(2)}) collective-permute-start(bf16[1024,768]{1,0:T(8,128)(2,1)} %bitcast.13.rows), channel_id=1, source_target_pairs={{0,1},{1,0},{2,3},{3,2},{4,5},{5,4},{6,7},{7,6},{8,9},{9,8},{10,11... | collective-permute-start | bytes 4718600 | tf_op jit(solution)/shard_map/ppermute | solution.py:38
  91.7 39.5 %all-to-all-start.3 = ((bf16[32,24,1664]{2,1,0:T(8,128)(2,1)}), bf16[32,24,1664]{2,1,0:T(8,128)(2,1)S(1)}, u32[]{:S(2)}, u32[]{:S(2)}) async-start(bf16[32,24,1664]{2,1,0:T(8,128)(2,1)} %broadcast_in_dim.9), calls=%async_computation.3 | async-start | bytes 5111808 | tf_op jit(solution)/shard_map/all_to_all | solution.py:92
  108.7 23.2 %collective-permute-start.2 = (bf16[1024,768]{1,0:T(8,128)(2,1)}, bf16[1024,768]{1,0:T(8,128)(2,1)}, u32[]{:S(2)}, u32[]{:S(2)}) collective-permute-start(bf16[1024,768]{1,0:T(8,128)(2,1)} %get-tuple-element.77), channel_id=1, source_target_pairs={{0,1},{1,0},{2,3},{3,2},{4,5},{5,4},{6,7},{7,6},{8,9},{9,8},{10,11... | collective-permute-start | bytes 4718600 | tf_op jit(solution)/shard_map/ppermute | solution.py:38
  131.2 37.2 %collective-permute-start.3 = (bf16[768,1664]{1,0:T(8,128)(2,1)S(1)}, bf16[768,1664]{1,0:T(8,128)(2,1)}, u32[]{:S(2)}, u32[]{:S(2)}) collective-permute-start(bf16[768,1664]{1,0:T(8,128)(2,1)S(1)} %bitcast.110), channel_id=1, source_target_pairs={{0,1},{1,0},{2,3},{3,2},{4,5},{5,4},{6,7},{7,6},{8,9},{9,8},{10,11... | collective-permute-start | bytes 7667720 | tf_op jit(solution)/shard_map/ppermute | solution.py:38
  135.4 29.5 %all-to-all-start.2 = ((bf16[64,16,768]{2,1,0:T(8,128)(2,1)}), bf16[64,16,768]{2,1,0:T(8,128)(2,1)}, u32[]{:S(2)}, u32[]{:S(2)}) async-start(bf16[64,16,768]{2,1,0:T(8,128)(2,1)} %bitcast.127), calls=%async_computation.2 | async-start | bytes 3145728 | tf_op jit(solution)/shard_map/all_to_all | solution.py:42
  179.0 53.1 %copy-start.45 = (bf16[2,1,768,768]{3,2,1,0:T(8,128)(2,1)S(1)}, bf16[2,1,768,768]{3,2,1,0:T(8,128)(2,1)}, u32[]{:S(2)}) copy-start(bf16[2,1,768,768]{3,2,1,0:T(8,128)(2,1)} %w_in.11) | copy-start | bytes 7077892
  179.0 53.1 %copy-start.49 = (bf16[2,1,768,768]{3,2,1,0:T(8,128)(2,1)S(1)}, bf16[2,1,768,768]{3,2,1,0:T(8,128)(2,1)}, u32[]{:S(2)}) copy-start(bf16[2,1,768,768]{3,2,1,0:T(8,128)(2,1)} %w_out.11) | copy-start | bytes 7077892
  223.2 8.9 %collective-permute-start.4 = (bf16[64,2,16,768]{3,2,1,0:T(8,128)(2,1)S(1)}, bf16[64,2,16,768]{3,2,1,0:T(8,128)(2,1)S(1)}, u32[]{:S(2)}, u32[]{:S(2)}) collective-permute-start(bf16[64,2,16,768]{3,2,1,0:T(8,128)(2,1)S(1)} %bitcast.107), channel_id=1, source_target_pairs={{0,1},{1,0},{2,3},{3,2},{4,5},{5,4},{6,7},{7,6},{8,9},{9,8},{10,11... | collective-permute-start | bytes 9437192 | tf_op jit(solution)/shard_map/ppermute | solution.py:38
  242.0 9.2 %collective-permute-start.5 = (bf16[64,2,16,768]{3,2,1,0:T(8,128)(2,1)S(1)}, bf16[64,2,16,768]{3,2,1,0:T(8,128)(2,1)S(1)}, u32[]{:S(2)}, u32[]{:S(2)}) collective-permute-start(bf16[64,2,16,768]{3,2,1,0:T(8,128)(2,1)S(1)} %get-tuple-element.83), channel_id=1, source_target_pairs={{0,1},{1,0},{2,3},{3,2},{4,5},{5,4},{6,7},{7,6},{8,9},{9,8},{10,11... | collective-permute-start | bytes 9437192 | tf_op jit(solution)/shard_map/ppermute | solution.py:38
  254.0 46.9 %all-to-all-start.5 = ((bf16[64,32,768]{2,1,0:T(8,128)(2,1)}), bf16[64,32,768]{2,1,0:T(8,128)(2,1)}, u32[]{:S(2)}, u32[]{:S(2)}) async-start(bf16[64,32,768]{2,1,0:T(8,128)(2,1)} %bitcast.123), calls=%async_computation.5 | async-start | bytes 6291456 | tf_op jit(solution)/shard_map/all_to_all | solution.py:42
  348.6 6.0 %collective-permute-start.6 = (bf16[1024,768]{1,0:T(8,128)(2,1)S(1)}, bf16[1024,768]{1,0:T(8,128)(2,1)S(1)}, u32[]{:S(2)}, u32[]{:S(2)}) collective-permute-start(bf16[1024,768]{1,0:T(8,128)(2,1)S(1)} %bitcast.118), channel_id=1, source_target_pairs={{0,1},{1,0},{2,3},{3,2},{4,5},{5,4},{6,7},{7,6},{8,9},{9,8},{10,11... | collective-permute-start | bytes 4718600 | tf_op jit(solution)/shard_map/ppermute | solution.py:38
  359.9 18.4 %collective-permute-start.7 = (bf16[1024,768]{1,0:T(8,128)(2,1)}, bf16[1024,768]{1,0:T(8,128)(2,1)}, u32[]{:S(2)}, u32[]{:S(2)}) collective-permute-start(bf16[1024,768]{1,0:T(8,128)(2,1)} %get-tuple-element.95), channel_id=1, source_target_pairs={{0,1},{1,0},{2,3},{3,2},{4,5},{5,4},{6,7},{7,6},{8,9},{9,8},{10,11... | collective-permute-start | bytes 4718600 | tf_op jit(solution)/shard_map/ppermute | solution.py:38
  369.0 18.7 %collective-permute-start.8 = (bf16[768,1664]{1,0:T(8,128)(2,1)}, bf16[768,1664]{1,0:T(8,128)(2,1)}, u32[]{:S(2)}, u32[]{:S(2)}) collective-permute-start(bf16[768,1664]{1,0:T(8,128)(2,1)} %get-tuple-element.103), channel_id=1, source_target_pairs={{0,1},{1,0},{2,3},{3,2},{4,5},{5,4},{6,7},{7,6},{8,9},{9,8},{10,11... | collective-permute-start | bytes 7667720 | tf_op jit(solution)/shard_map/ppermute | solution.py:38
  381.9 28.9 %all-to-all-start.7 = ((bf16[64,16,768]{2,1,0:T(8,128)(2,1)}), bf16[64,16,768]{2,1,0:T(8,128)(2,1)}, u32[]{:S(2)}, u32[]{:S(2)}) async-start(bf16[64,16,768]{2,1,0:T(8,128)(2,1)} %bitcast.128), calls=%async_computation.7 | async-start | bytes 3145728 | tf_op jit(solution)/shard_map/all_to_all | solution.py:42
  410.9 36.4 %all-to-all-start.8 = ((bf16[32,24,1664]{2,1,0:T(8,128)(2,1)}), bf16[32,24,1664]{2,1,0:T(8,128)(2,1)}, u32[]{:S(2)}, u32[]{:S(2)}) async-start(bf16[32,24,1664]{2,1,0:T(8,128)(2,1)} %bitcast.125), calls=%async_computation.8 | async-start | bytes 5111808 | tf_op jit(solution)/shard_map/all_to_all | solution.py:128
  447.3 10.2 %collective-permute-start.9 = (bf16[768,1664]{1,0:T(8,128)(2,1)}, bf16[768,1664]{1,0:T(8,128)(2,1)}, u32[]{:S(2)}, u32[]{:S(2)}) collective-permute-start(bf16[768,1664]{1,0:T(8,128)(2,1)} %copy-done.43), channel_id=1, source_target_pairs={{0,1},{1,0},{2,3},{3,2},{4,5},{5,4},{6,7},{7,6},{8,9},{9,8},{10,11... | collective-permute-start | bytes 7667720 | tf_op jit(solution)/shard_map/ppermute | solution.py:38
  461.4 43.3 %all-to-all-start.9 = ((bf16[32,24,1664]{2,1,0:T(8,128)(2,1)}), bf16[32,24,1664]{2,1,0:T(8,128)(2,1)}, u32[]{:S(2)}, u32[]{:S(2)}) async-start(bf16[32,24,1664]{2,1,0:T(8,128)(2,1)} %bitcast.124), calls=%async_computation.9 | async-start | bytes 5111808 | tf_op jit(solution)/shard_map/all_to_all | solution.py:128
  478.1 26.4 %collective-permute-start.11 = (f32[24,1664]{1,0:T(8,128)S(1)}, f32[24,1664]{1,0:T(8,128)S(1)}, u32[]{:S(2)}, u32[]{:S(2)}) collective-permute-start(f32[24,1664]{1,0:T(8,128)S(1)} %convert_reduce_fusion), channel_id=1, source_target_pairs={{0,2},{1,3},{2,0},{3,1},{4,6},{5,7},{6,4},{7,5},{8,10},{9,11},{10,... | collective-permute-start | bytes 479240 | tf_op jit(solution)/shard_map/ppermute | solution.py:134
  479.4 7.9 %collective-permute-start.14 = (f32[24,1536]{1,0:T(8,128)S(1)}, f32[24,1536]{1,0:T(8,128)S(1)}, u32[]{:S(2)}, u32[]{:S(2)}) collective-permute-start(f32[24,1536]{1,0:T(8,128)S(1)} %slice.347), channel_id=1, source_target_pairs={{0,1},{1,0},{2,3},{3,2},{4,5},{5,4},{6,7},{7,6},{8,9},{9,8},{10,11... | collective-permute-start | bytes 442376 | tf_op jit(solution)/shard_map/ppermute | solution.py:134
  480.4 24.1 %collective-permute-start.15 = (f32[24,1536]{1,0:T(8,128)S(1)}, f32[24,1536]{1,0:T(8,128)S(1)}, u32[]{:S(2)}, u32[]{:S(2)}) collective-permute-start(f32[24,1536]{1,0:T(8,128)S(1)} %slice.347), channel_id=1, source_target_pairs={{0,3},{1,2},{2,1},{3,0},{4,7},{5,6},{6,5},{7,4},{8,11},{9,10},{10,... | collective-permute-start | bytes 442376 | tf_op jit(solution)/shard_map/ppermute | solution.py:134
  506.8 10.6 %collective-permute-start.10 = (f32[24,1664]{1,0:T(8,128)S(1)}, f32[24,1664]{1,0:T(8,128)S(1)}, u32[]{:S(2)}, u32[]{:S(2)}) collective-permute-start(f32[24,1664]{1,0:T(8,128)S(1)} %convert_reduce_fusion.1), channel_id=1, source_target_pairs={{0,2},{1,3},{2,0},{3,1},{4,6},{5,7},{6,4},{7,5},{8,10},{9,11},{10,... | collective-permute-start | bytes 479240 | tf_op jit(solution)/shard_map/ppermute | solution.py:134
  508.6 1.7 collective-permute-start.12
  508.9 8.5 %collective-permute-start.13 = (f32[24,1536]{1,0:T(8,128)S(1)}, f32[24,1536]{1,0:T(8,128)S(1)}, u32[]{:S(2)}, u32[]{:S(2)}) collective-permute-start(f32[24,1536]{1,0:T(8,128)S(1)} %slice.340), channel_id=1, source_target_pairs={{0,3},{1,2},{2,1},{3,0},{4,7},{5,6},{6,5},{7,4},{8,11},{9,10},{10,... | collective-permute-start | bytes 442376 | tf_op jit(solution)/shard_map/ppermute | solution.py:134
  (121 other events, 924.3 us)

commit v6 on v3

--- a/solution.py
+++ b/solution.py
@@ -86,9 +86,9 @@
 
 def gather_cols(mine, after=None):
     groups = lax.axis_size("ea")
+    sent = jnp.broadcast_to(mine[None], (groups,) + mine.shape)
     if after is not None:
-        mine, _ = lax.optimization_barrier((mine, after))
-    sent = jnp.broadcast_to(mine[None], (groups,) + mine.shape)
+        sent, _ = lax.optimization_barrier((sent, after))
     got = lax.all_to_all(sent, "ea", split_axis=0, concat_axis=0)
     return got.reshape(-1, mine.shape[1])
 
@@ -119,18 +119,12 @@
     return own, swap_core(own)
 
 
-def sum_send(grad_qkv, grad_out, small):
-    give = [grad_qkv[1].astype(BF), grad_out[1].astype(BF), small.astype(BF)]
-    own = [grad_qkv[0], grad_out[0], small]
-    return jnp.concatenate(
-        [(o + swap_core(g).astype(F32)).astype(BF) for o, g in zip(own, give)], axis=1
-    )
-
-
-def sum_exchange(pair, after=None):
+def sum_send(own, give):
+    return (own.astype(F32) + swap_core(give).astype(F32)).astype(BF)
+
+
+def sum_exchange(pair):
     groups = lax.axis_size("ea")
-    if after is not None:
-        pair, _ = lax.optimization_barrier((pair, after))
     return lax.all_to_all(
         pair.reshape(groups, -1, pair.shape[1]), "ea", split_axis=0, concat_axis=0
     )
@@ -140,11 +134,11 @@
     return lax.ppermute(value, ("half", "core"), [(i, i ^ flip) for i in range(4)])
 
 
-def sum_finish(parts):
-    part = jnp.sum(parts.astype(F32), axis=0)
-    full = part + swap_row(part, 2)
+def sum_finish(*parts):
+    part = jnp.concatenate([jnp.sum(p.astype(F32), axis=0) for p in parts], axis=1).astype(BF)
+    full = part.astype(F32) + swap_row(part, 2).astype(F32)
     dense = part[:, :1536]
-    other = swap_row(dense, 1) + swap_row(dense, 3)
+    other = swap_row(dense, 1).astype(F32) + swap_row(dense, 3).astype(F32)
     qkv = [
         in_order(own, more) for own, more in zip(thirds(full[:, :1152]), thirds(other[:, :1152]))
     ]
@@ -189,7 +183,7 @@
 
 
 def attend_kernel(
-    experts, core_ref, state, own, other, normed, proj_o, proj_x, mixed, after, normed_two, logits
+    experts, core_ref, state, own, other, proj_o, proj_x, mixed, after, normed_two, logits, normed
 ):
     core = core_ref[0]
     norms = norms_of(own, experts)
@@ -213,8 +207,8 @@
 
 
 def attend_back_kernel(
-    experts, core_ref, grad, grad_two, state, after, proj_o, proj_x, own, other, grad_in, grad_attn,
-    gp_o, gp_x, stats, grad_mixed,
+    experts, core_ref, grad, grad_two, state, after, proj_o, proj_x, mixed, small, own, other,
+    grad_in, sum_o, sum_x, grad_attn, grad_mixed, gp_o, gp_x, normed, stats,
 ):
     core = core_ref[0]
     norms = norms_of(own, experts)
@@ -242,11 +236,20 @@
             for i in range(3):
                 gp[:, i * 384 + at : i * 384 + at + 128] = merge(found[0][i], found[1][i]).astype(BF)
     grad_normed = dot_nt(gp_o[...], own[:, QKV]) + dot_nt(gp_x[...], other[:, QKV])
-    _, unit, inv = normalize(state[...], norms[0:1], norms[2:3])
+    wide, unit, inv = normalize(state[...], norms[0:1], norms[2:3])
+    normed[...] = wide.astype(BF)
     part, gain_one, bias_one = normalize_back(grad_normed, unit, inv, norms[0:1])
     grad_in[...] = grad_in[...] + part
+    stats[...] = jnp.zeros_like(stats)
     for i, row in enumerate((gain_one, gain_two, bias_one, bias_two)):
-        stats[i : i + 1, :] = row[None, :]
+        stats[experts + i : experts + i + 1, :] = row[None, :]
+    narrow = (stats[...].T + small[...]).astype(BF)
+    for side, gp, out in ((1, gp_x, sum_x), (0, gp_o, sum_o)):
+        for at in range(0, 768, 256):
+            rows = slice(at, at + 256)
+            out[rows, QKV] = dot_tn(normed[:, rows], gp[...]).astype(BF)
+            out[rows, OUT] = dot_tn(mixed[:, rows], grad_attn[:, place(core, side, 0, 384)]).astype(BF)
+        out[:, SMALL] = narrow
 
 
 def whole_call(kernel, args, outs, flops, scratch=()):
@@ -258,7 +261,7 @@
         out_specs=[vmem] * len(outs),
         out_shape=[jax.ShapeDtypeStruct(shape, kind) for shape, kind in outs],
         scratch_shapes=list(scratch),
-        compiler_params=pltpu.CompilerParams(vmem_limit_bytes=VMEM),
+        compiler_params=pltpu.CompilerParams(vmem_limit_bytes=VMEM + (12 << 20)),
         cost_estimate=pl.CostEstimate(flops=flops, bytes_accessed=8 << 20, transcendentals=0),
     )(core, *args)
 
@@ -266,35 +269,32 @@
 def attention(state, dense):
     tokens, width = state.shape
     rows = lambda n, kind: ((tokens, n), kind)
-    normed, proj_o, proj_x, mixed, after, normed_two, logits = whole_call(
+    proj_o, proj_x, mixed, after, normed_two, logits = whole_call(
         functools.partial(attend_kernel, lax.axis_size("ea")),
         [state, *dense],
         [
-            rows(width, BF), rows(1152, BF), rows(1152, BF), rows(width, BF), rows(width, F32),
-            rows(width, BF), rows(128, F32),
+            rows(1152, BF), rows(1152, BF), rows(width, BF), rows(width, F32), rows(width, BF),
+            rows(128, F32),
         ],
         4 * tokens * width * (4 * width + 4 * tokens),
-    )
-    return after, normed_two, logits, (state, normed, proj_o, proj_x, mixed, after)
-
-
-def attention_back(grad, grad_two, kept, dense):
-    state, normed, proj_o, proj_x, mixed, after = kept
+        [pltpu.VMEM((tokens, width), BF)],
+    )
+    return after, normed_two, logits, (state, proj_o, proj_x, mixed, after)
+
+
+def attention_back(grad, grad_two, grad_router_w, kept, dense):
+    state, proj_o, proj_x, mixed, after = kept
     tokens, width = grad.shape
     rows = lambda n, kind: ((tokens, n), kind)
-    grad_in, grad_attn, gp_o, gp_x, stats = whole_call(
+    scratch = [rows(width, BF), rows(width, BF), rows(1152, BF), rows(1152, BF), rows(width, BF)]
+    grad_in, sum_o, sum_x = whole_call(
         functools.partial(attend_back_kernel, lax.axis_size("ea")),
-        [grad, grad_two, state, after, proj_o, proj_x, *dense],
-        [rows(width, F32), rows(width, BF), rows(1152, BF), rows(1152, BF), ((4, width), F32)],
-        8 * tokens * width * (4 * width + 8 * tokens),
-        [pltpu.VMEM((tokens, width), BF)],
-    )
-    return grad_in, stats, (normed, gp_o, gp_x, mixed, grad_attn)
-
-
-def dense_grads(normed, gp_o, gp_x, mixed, grad_attn):
-    grad_out = [dot_tn(mixed, core_half(grad_attn, which)) for which in (0, 1)]
-    return [dot_tn(normed, gp_o), dot_tn(normed, gp_x)], grad_out
+        [grad, grad_two, state, after, proj_o, proj_x, mixed, pad_cols(grad_router_w, 128), *dense],
+        [rows(width, F32), ((width, 1664), BF), ((width, 1664), BF)],
+        12 * tokens * width * (4 * width + 8 * tokens),
+        [pltpu.VMEM(*dims) for dims in scratch + [((128, width), F32)]],
+    )
+    return grad_in, (sum_o, sum_x)
 
 
 def forward_kernel(rows, w_in, w_out, hidden, slope, part):
@@ -404,10 +404,6 @@
     grad_normed = jnp.dot(grad_logit, router_w.astype(F32).T, precision=HIGH)
     grad_router_w = jnp.dot(normed_two.astype(F32).T, grad_logit, precision=HIGH)
     return grad_normed, grad_router_w
-
-
-def small_grads(grad_router_w, stats):
-    return pad_cols(jnp.concatenate([grad_router_w, stats.T], axis=1), 128)
 
 
 def per_device(
@@ -481,35 +477,41 @@
     extra, grad_router_w1 = router_back(
         grad, picked1, router1, onehot1, normed1, dense1[0][:, 1536 : 1536 + experts]
     )
-    grad, stats1, terms1 = attention_back(grad, grad_sent + extra, kept1, dense1)
+    grad, grads1 = attention_back(grad, grad_sent + extra, grad_router_w1, kept1, dense1)
 
     grad_rows = jnp.concatenate([(g * grad).astype(BF) for g in gate0], axis=0)
     arrived = exchange(dot(send, grad_rows).astype(BF))
-    pair1 = sum_send(*dense_grads(*terms1), small_grads(grad_router_w1, stats1))
+    pair1 = sum_send(*grads1)
     arrived, pair1 = lax.optimization_barrier((arrived, pair1))
+    parts1a = sum_exchange(pair1[:, :768])
     grows0 = (arrived, swap_core(arrived))
     third = [
         expert_call(backward_kernel, 0, [r, s], weights, [r.shape] * 2, 2)
         for r, s in zip(grows0, slope0)
     ]
     grad_pre0, part = zip(*third)
-    returned = exchange(join_cores(*part))
-    parts1 = sum_exchange(pair1, after=returned)
+    back, parts1a = lax.optimization_barrier((join_cores(*part), parts1a))
+    returned = exchange(back)
+    returned, pair1 = lax.optimization_barrier((returned, pair1))
+    parts1b = sum_exchange(pair1[:, 768:])
     picked = dot(fetch, returned)
     grad_sent = picked[:tokens] + picked[tokens:]
     extra, grad_router_w0 = router_back(
         grad, picked0, router0, onehot0, normed0, dense0[0][:, 1536 : 1536 + experts]
     )
-    grad, stats0, terms0 = attention_back(grad, grad_sent + extra, kept0, dense0)
-    terms0, parts1 = lax.optimization_barrier((terms0, parts1))
-    pair0 = sum_send(*dense_grads(*terms0), small_grads(grad_router_w0, stats0))
+    grad, grads0 = attention_back(grad, grad_sent + extra, grad_router_w0, kept0, dense0)
+    grads0, parts1b = lax.optimization_barrier((grads0, parts1b))
+    pair0 = sum_send(*grads0)
     parts0 = sum_exchange(pair0)
-    (hidden0, grows0, rows0, grad_pre0), pair0 = lax.optimization_barrier(
+    (hidden0, grows0, rows0, grad_pre0), _ = lax.optimization_barrier(
         ((hidden0, grows0, rows0, grad_pre0), pair0)
     )
     grad_w_out0 = sum(dot_tn(h, g) for h, g in zip(hidden0, grows0))
     grad_w_in0 = sum(dot_tn(r, g) for r, g in zip(rows0, grad_pre0))
-    sums1 = sum_finish(parts1)
+    (grad_w_out0, grad_w_in0), parts1b = lax.optimization_barrier(
+        ((grad_w_out0, grad_w_in0), parts1b)
+    )
+    sums1 = sum_finish(parts1a, parts1b)
     sums0 = sum_finish(parts0)
 
     qkv_sum, out_sum, small = (jnp.stack(pair) for pair in zip(sums0, sums1))

time: 525 us -> 542 us (1.032)
  waiting for transfers between devices: 110 us -> 141 us
  blocking collectives: 143 us -> 115 us
  local copies, waits for them, and re-layouts: 33.9 us -> 45.2 us
  matrix products: 49 us -> 39.3 us
  starting transfers between devices: 63.8 us -> 70.9 us
    all_to_all x3 -> x4, waiting for transfers between devices: 48.9 us -> 79.1 us  [exchange(): return lax.all_to_all(rows, GROUP, split_axis=0, concat_axis=0, tiled=True)]
    all_to_all x3 -> x2, blocking collectives: 102 us -> 73.8 us  [exchange(): return lax.all_to_all(rows, GROUP, split_axis=0, concat_axis=0, tiled=True)]
    dot_general x24 -> x16, matrix products: 46.1 us -> 36.9 us  [dot(): return lax.dot_general(a, b, (dims, ((), ())), preferred_element_type=F32)]
    unnamed x280 -> x234, local copies, waits for them, and re-layouts: 25.2 us -> 32.8 us
    all_to_all x3 -> x4, starting transfers between devices: 18.2 us -> 25 us  [exchange(): return lax.all_to_all(rows, GROUP, split_axis=0, concat_axis=0, tiled=True)]
    convert_element_type x2, other arithmetic: 1.11 us -> 7.77 us  [sum_send(): return (own.astype(F32) + swap_core(give).astype(F32)).astype(BF)]
    all_to_all x2 -> x3, starting transfers between devices: 10.2 us -> 15.8 us  [sum_exchange(): lax.all_to_all(pair.reshape(groups, -1, pair.shape[1]), 'ea', split_axis=...]
    ppermute x14 -> x10, starting transfers between devices: 22.1 us -> 16.8 us  [swap_core(): return lax.ppermute(value, 'core', [(0, 1), (1, 0)])]
  transfers between devices with their start and end apart: 26 -> 24, of which waited for: 13 -> 14; matrix products, arithmetic and copies ran while one was open for 15% -> 11% of each run, Pallas kernels for 7% -> 7%
where the time goes in v6:
time: 542 us; the launch traced here: 533 us
  waiting for transfers between devices  141 us (26%)
  blocking collectives  115 us (21%)
  Pallas kernels  71 us (13%)
  starting transfers between devices  70.9 us (13%)
  other arithmetic  47.7 us (9%)
  local copies, waits for them, and re-layouts  45.2 us (8%)
  matrix products  39.3 us (7%)
    all_to_all x4, waiting for transfers between devices, exchange(): return lax.all_to_all(rows, GROUP, split_axis=0, concat_axis=0, tiled=True)  79.1 us
    all_to_all x2, blocking collectives, exchange(): return lax.all_to_all(rows, GROUP, split_axis=0, concat_axis=0, tiled=True)  73.8 us
    all_to_all x1, blocking collectives, gather_cols(): got = lax.all_to_all(sent, 'ea', split_axis=0, concat_axis=0)  41.4 us
    pallas_call x6, Pallas kernels, expert_call(): pl.pallas_call(kernel, grid=(count // (GROUPS * SLOTS),), in_specs=[spec(...  37 us
    dot_general x16, matrix products, dot(): return lax.dot_general(a, b, (dims, ((), ())), preferred_element_type=F32)  36.9 us
    pallas_call x4, Pallas kernels, whole_call(): pl.pallas_call(kernel, in_specs=[pl.BlockSpec(memory_space=pltpu.SMEM)] +...  34 us
    all_to_all x3, waiting for transfers between devices, sum_exchange(): lax.all_to_all(pair.reshape(groups, -1, pair.shape[1]), 'ea', split_axis=...  33.7 us
    unnamed x234, local copies, waits for them, and re-layouts  32.8 us
  transfers between devices with their start and end apart: 24, of which 14 were waited for; matrix products, arithmetic and copies ran while one was open for 11% of the time, Pallas kernels for 7%

profile of v6, /device:TPU:1, one launch (start us, length us, event | category | flops | bytes accessed | tf_op | source)
XLA Modules:
  0.0 533.2 jit_solution(5966693080327655199)
XLA Ops:
  5.1 41.4 %all_to_all.93 = bf16[32,24,1664]{2,1,0:T(8,128)(2,1)S(1)} all-to-all(bf16[32,24,1664]{2,1,0:T(8,128)(2,1)S(1)} %broadcast_in_dim.8), channel_id=1, replica_groups=mesh['ea'=32,'half'=2,'core'=2] {'ea'}, dimensions={0} | all-to-all | bytes 5111808 | tf_op jit(solution)/shard_map/all_to_all | solution.py:92
  58.4 29.3 %all_to_all.94 = bf16[64,16,768]{2,1,0:T(8,128)(2,1)} all-to-all(bf16[64,16,768]{2,1,0:T(8,128)(2,1)S(1)} %bitcast.119), channel_id=1, replica_groups=mesh['ea'=32,'half'=2,'core'=2] {'ea','half'}, dimensions={0} | all-to-all | bytes 3145728 | tf_op jit(solution)/shard_map/all_to_all | solution.py:42
  91.6 4.1 all-to-all-start.3
  99.1 7.3 %shard_map.171 = (bf16[1024,768]{1,0:T(8,128)(2,1)S(1)}, bf16[1024,768]{1,0:T(8,128)(2,1)S(1)}, bf16[1024,768]{1,0:T(8,128)(2,1)}) custom-call(bf16[1024,768]{1,0:T(8,128)(2,1)} %collective-permute-done.1.rows, bf16[2,1,768,768]{3,2,1,0:T(8,128)(2,1)S(1)} %copy-done.24, bf16[2,1,768,768]{3,2,1,0:T(8,128)(2,1)S(1)} %copy-done.28), custom_call_target="tpu_custom_call" | custom-call | flops 2415919104 | bytes 8650752 | tf_op jit(solution)/shard_map/pallas_call | solution.py:338
  110.6 6.4 %shard_map.170 = (bf16[1024,768]{1,0:T(8,128)(2,1)S(1)}, bf16[1024,768]{1,0:T(8,128)(2,1)S(1)}, bf16[1024,768]{1,0:T(8,128)(2,1)S(1)}) custom-call(bf16[1024,768]{1,0:T(8,128)(2,1)} %bitcast.13.rows, bf16[2,1,768,768]{3,2,1,0:T(8,128)(2,1)S(1)} %copy-done.24, bf16[2,1,768,768]{3,2,1,0:T(8,128)(2,1)S(1)} %copy-done.28), custom_call_target="tpu_custom_call" | custom-call | flops 2415919104 | bytes 8650752 | tf_op jit(solution)/shard_map/pallas_call | solution.py:338
  120.5 10.6 %all-to-all-done.3 = bf16[32,24,1664]{2,1,0:T(8,128)(2,1)S(1)} async-done(((bf16[32,24,1664]{2,1,0:T(8,128)(2,1)}), bf16[32,24,1664]{2,1,0:T(8,128)(2,1)S(1)}, u32[]{:S(2)}, u32[]{:S(2)}) %all-to-all-start.3) | async-done | bytes 2555936 | tf_op jit(solution)/shard_map/all_to_all | solution.py:92
  135.4 6.9 %all-to-all-start.2 = ((bf16[64,16,768]{2,1,0:T(8,128)(2,1)}), bf16[64,16,768]{2,1,0:T(8,128)(2,1)}, u32[]{:S(2)}, u32[]{:S(2)}) async-start(bf16[64,16,768]{2,1,0:T(8,128)(2,1)} %bitcast.120), calls=%async_computation.2 | async-start | bytes 3145728 | tf_op jit(solution)/shard_map/all_to_all | solution.py:42
  142.4 5.1 and_convert_fusion.1
  149.4 15.6 %all-to-all-done.2 = bf16[64,16,768]{2,1,0:T(8,128)(2,1)} async-done(((bf16[64,16,768]{2,1,0:T(8,128)(2,1)}), bf16[64,16,768]{2,1,0:T(8,128)(2,1)}, u32[]{:S(2)}, u32[]{:S(2)}) %all-to-all-start.2) | async-done | bytes 1572896 | tf_op jit(solution)/shard_map/all_to_all | solution.py:42
  168.4 6.0 %shard_map.172 = (bf16[197,1152]{1,0:T(8,128)(2,1)S(1)}, bf16[197,1152]{1,0:T(8,128)(2,1)S(1)}, bf16[197,768]{1,0:T(8,128)(2,1)S(1)}, f32[197,768]{1,0:T(8,128)S...) custom-call(s32[1]{0:T(128)} %bitcast.core_ref, f32[197,768]{1,0:T(8,128)S(1)} %multiply_add_fusion.state, ...), custom_call_target="tpu_custom_call" | custom-call | flops 2336010240 | bytes 8388608 | tf_op jit(solution)/shard_map/pallas_call | solution.py:258
  179.1 44.4 %all_to_all.95 = bf16[64,32,768]{2,1,0:T(8,128)(2,1)S(1)} all-to-all(bf16[64,32,768]{2,1,0:T(8,128)(2,1)S(1)} %bitcast.122), channel_id=1, replica_groups=mesh['ea'=32,'half'=2,'core'=2] {'ea','half'}, dimensions={0} | all-to-all | bytes 6291456 | tf_op jit(solution)/shard_map/all_to_all | solution.py:42
  227.2 5.3 collective-permute-done.4.rows
  232.5 7.5 %shard_map.174 = (bf16[1024,768]{1,0:T(8,128)(2,1)S(1)}, bf16[1024,768]{1,0:T(8,128)(2,1)S(1)}, bf16[64,2,16,768]{3,2,1,0:T(8,128)(2,1)S(1)}) custom-call(bf16[64,2,16,768]{3,2,1,0:T(8,128)(2,1)S(1)} %collective-permute-done.4.rows, bf16[2,1,768,768]{3,2,1,0:T(8,128)(2,1)S(1)} %copy-done.25, bf16[2,1,768,768]{3,2,1,0:T(8,128)(2,1)S(1)} %copy-done.29), custom_call_target="tpu_custom_call" | custom-call | flops 4831838208 | bytes 8650752 | tf_op jit(solution)/shard_map/pallas_call | solution.py:338
  242.8 7.6 %shard_map.173 = (bf16[1024,768]{1,0:T(8,128)(2,1)S(1)}, bf16[1024,768]{1,0:T(8,128)(2,1)S(1)}, bf16[64,2,16,768]{3,2,1,0:T(8,128)(2,1)S(1)}) custom-call(bf16[64,2,16,768]{3,2,1,0:T(8,128)(2,1)S(1)} %bitcast.107, bf16[2,1,768,768]{3,2,1,0:T(8,128)(2,1)S(1)} %copy-done.25, bf16[2,1,768,768]{3,2,1,0:T(8,128)(2,1)S(1)} %copy-done.29), custom_call_target="tpu_custom_call" | custom-call | flops 4831838208 | bytes 8650752 | tf_op jit(solution)/shard_map/pallas_call | solution.py:338
  254.4 5.6 %all-to-all-start.5 = ((bf16[64,32,768]{2,1,0:T(8,128)(2,1)}), bf16[64,32,768]{2,1,0:T(8,128)(2,1)}, u32[]{:S(2)}, u32[]{:S(2)}) async-start(bf16[64,32,768]{2,1,0:T(8,128)(2,1)} %bitcast.117), calls=%async_computation.5 | async-start | bytes 6291456 | tf_op jit(solution)/shard_map/all_to_all | solution.py:42
  276.9 24.3 %all-to-all-done.5 = bf16[64,32,768]{2,1,0:T(8,128)(2,1)} async-done(((bf16[64,32,768]{2,1,0:T(8,128)(2,1)}), bf16[64,32,768]{2,1,0:T(8,128)(2,1)}, u32[]{:S(2)}, u32[]{:S(2)}) %all-to-all-start.5) | async-done | bytes 3145760 | tf_op jit(solution)/shard_map/all_to_all | solution.py:42
  301.3 4.0 fusion.21
  308.3 13.9 %shard_map.175 = (f32[197,768]{1,0:T(8,128)S(1)}, bf16[768,1664]{1,0:T(8,128)(2,1)S(1)}, bf16[768,1664]{1,0:T(8,128)(2,1)}) custom-call(s32[1]{0:T(128)} %bitcast.core_ref, f32[197,768]{1,0:T(8,128)S(1)} %copy-done.11, f32[197,768]{1,0:T(8,128)S(1)} %convolution_add_fusion.5.grad_two, f32[197,768]{1,0:T(8,128)S(1)} %copy-done.15, f32[197,768]{1,0:T(8,128)S(1)} %copy-done.17, ...), custom_call_target="tpu_custom_call" | custom-call | flops 8438685696 | bytes 8388608 | tf_op jit(solution)/shard_map/pallas_call | solution.py:258
  326.5 5.9 %all-to-all-start.6 = ((bf16[64,16,768]{2,1,0:T(8,128)(2,1)}), bf16[64,16,768]{2,1,0:T(8,128)(2,1)}, u32[]{:S(2)}, u32[]{:S(2)}) async-start(bf16[64,16,768]{2,1,0:T(8,128)(2,1)} %bitcast.128), calls=%async_computation.6 | async-start | bytes 3145728 | tf_op jit(solution)/shard_map/all_to_all | solution.py:42
  336.3 19.3 %all-to-all-done.6 = bf16[64,16,768]{2,1,0:T(8,128)(2,1)} async-done(((bf16[64,16,768]{2,1,0:T(8,128)(2,1)}), bf16[64,16,768]{2,1,0:T(8,128)(2,1)}, u32[]{:S(2)}, u32[]{:S(2)}) %all-to-all-start.6) | async-done | bytes 1572896 | tf_op jit(solution)/shard_map/all_to_all | solution.py:42
  373.9 4.8 all-to-all-start.7
  381.8 4.3 shard_map.176
  390.3 6.4 %all-to-all-done.7 = bf16[32,24,768]{2,1,0:T(8,128)(2,1)} async-done(((bf16[32,24,768]{2,1,0:T(8,128)(2,1)}), bf16[32,24,768]{2,1,0:T(8,128)(2,1)}, u32[]{:S(2)}, u32[]{:S(2)}) %all-to-all-start.7) | async-done | bytes 1179680 | tf_op jit(solution)/shard_map/all_to_all | solution.py:128
  396.7 6.6 %all-to-all-start.8 = ((bf16[64,16,768]{2,1,0:T(8,128)(2,1)}), bf16[64,16,768]{2,1,0:T(8,128)(2,1)S(1)}, u32[]{:S(2)}, u32[]{:S(2)}) async-start(bf16[64,16,768]{2,1,0:T(8,128)(2,1)} %bitcast.38), calls=%async_computation.8 | async-start | bytes 3145728 | tf_op jit(solution)/shard_map/all_to_all | solution.py:42
  405.1 20.0 %all-to-all-done.8 = bf16[64,16,768]{2,1,0:T(8,128)(2,1)S(1)} async-done(((bf16[64,16,768]{2,1,0:T(8,128)(2,1)}), bf16[64,16,768]{2,1,0:T(8,128)(2,1)S(1)}, u32[]{:S(2)}, u32[]{:S(2)}) %all-to-all-start.8) | async-done | bytes 1572896 | tf_op jit(solution)/shard_map/all_to_all | solution.py:42
  427.6 5.3 all-to-all-start.9
  436.1 10.2 %shard_map.178 = (f32[197,768]{1,0:T(8,128)}, bf16[768,1664]{1,0:T(8,128)(2,1)S(1)}, bf16[768,1664]{1,0:T(8,128)(2,1)S(1)}) custom-call(s32[1]{0:T(128)} %bitcast.core_ref, f32[197,768]{1,0:T(8,128)S(1)} %get-tuple-element.86.grad, f32[197,768]{1,0:T(8,128)S(1)} %convolution_add_fusion.4.grad_two, f32[197,768]{1,0:T(8,128)S(1)} %copy-done.10, ...), custom_call_target="tpu_custom_call" | custom-call | flops 8438685696 | bytes 8388608 | tf_op jit(solution)/shard_map/pallas_call | solution.py:258
  467.1 4.5 convolution_add_fusion
  471.6 4.4 convolution_add_fusion.1
  481.0 5.7 %all-to-all-start.10 = ((bf16[32,24,1664]{2,1,0:T(8,128)(2,1)}), bf16[32,24,1664]{2,1,0:T(8,128)(2,1)S(1)}, u32[]{:S(2)}, u32[]{:S(2)}) async-start(bf16[32,24,1664]{2,1,0:T(8,128)(2,1)} %bitcast.118), calls=%async_computation.10 | async-start | bytes 5111808 | tf_op jit(solution)/shard_map/all_to_all | solution.py:128
  486.7 5.0 maximum_bitcast_fusion.1
  494.4 25.0 %all-to-all-done.10 = bf16[32,24,1664]{2,1,0:T(8,128)(2,1)S(1)} async-done(((bf16[32,24,1664]{2,1,0:T(8,128)(2,1)}), bf16[32,24,1664]{2,1,0:T(8,128)(2,1)S(1)}, u32[]{:S(2)}, u32[]{:S(2)}) %all-to-all-start.10) | async-done | bytes 2555936 | tf_op jit(solution)/shard_map/all_to_all | solution.py:128
  (373 shorter events, 158.3 us)
Async XLA Ops:
  46.5 7.2 %collective-permute-start = (bf16[768,1664]{1,0:T(8,128)(2,1)S(1)}, bf16[768,1664]{1,0:T(8,128)(2,1)S(1)}, u32[]{:S(2)}, u32[]{:S(2)}) collective-permute-start(bf16[768,1664]{1,0:T(8,128)(2,1)S(1)} %bitcast.113), channel_id=1, source_target_pairs={{0,1},{1,0},{2,3},{3,2},{4,5},{5,4},{6,7},{7,6},{8,9},{9,8},{10,11... | collective-permute-start | bytes 7667720 | tf_op jit(solution)/shard_map/ppermute | solution.py:38
  49.3 115.7 %copy-start.110 = (pred[1024]{0:T(1024)(128)(4,1)}, pred[1024]{0:T(1024)(128)(4,1)S(1)}, u32[]{:S(2)}) copy-start(pred[1024]{0:T(1024)(128)(4,1)S(1)} %fusion.90) | copy-start | bytes 3076
  49.4 115.5 %copy-start.91 = (s32[1024]{0:T(1024)}, s32[1024]{0:T(1024)S(1)}, u32[]{:S(2)}) copy-start(s32[1024]{0:T(1024)S(1)} %broadcast_add_fusion.1) | copy-start | bytes 12292
  49.4 115.5 %copy-start.93 = (s32[1024]{0:T(1024)}, s32[1024]{0:T(1024)S(1)}, u32[]{:S(2)}) copy-start(s32[1024]{0:T(1024)S(1)} %get-tuple-element.196) | copy-start | bytes 12292
  49.4 115.5 %copy-start.95 = (s32[1024]{0:T(1024)}, s32[1024]{0:T(1024)S(1)}, u32[]{:S(2)}) copy-start(s32[1024]{0:T(1024)S(1)} %get-tuple-element.197) | copy-start | bytes 12292
  50.0 115.0 %copy-start.107 = (s32[394]{0:T(512)}, s32[394]{0:T(512)S(1)}, u32[]{:S(2)}) copy-start(s32[394]{0:T(512)S(1)} %convert_add_fusion.5) | copy-start | bytes 4732
  57.7 109.6 %copy-start.12 = (f32[197,768]{1,0:T(8,128)}, f32[197,768]{1,0:T(8,128)S(1)}, u32[]{:S(2)}) copy-start(f32[197,768]{1,0:T(8,128)S(1)} %get-tuple-element.67.after) | copy-start | bytes 1815556
  87.7 8.0 %collective-permute-start.1 = (bf16[1024,768]{1,0:T(8,128)(2,1)}, bf16[1024,768]{1,0:T(8,128)(2,1)}, u32[]{:S(2)}, u32[]{:S(2)}) collective-permute-start(bf16[1024,768]{1,0:T(8,128)(2,1)} %bitcast.13.rows), channel_id=1, source_target_pairs={{0,1},{1,0},{2,3},{3,2},{4,5},{5,4},{6,7},{7,6},{8,9},{9,8},{10,11... | collective-permute-start | bytes 4718600 | tf_op jit(solution)/shard_map/ppermute | solution.py:38
  91.6 39.5 %all-to-all-start.3 = ((bf16[32,24,1664]{2,1,0:T(8,128)(2,1)}), bf16[32,24,1664]{2,1,0:T(8,128)(2,1)S(1)}, u32[]{:S(2)}, u32[]{:S(2)}) async-start(bf16[32,24,1664]{2,1,0:T(8,128)(2,1)} %broadcast_in_dim.9), calls=%async_computation.3 | async-start | bytes 5111808 | tf_op jit(solution)/shard_map/all_to_all | solution.py:92
  108.7 23.2 %collective-permute-start.2 = (bf16[1024,768]{1,0:T(8,128)(2,1)}, bf16[1024,768]{1,0:T(8,128)(2,1)}, u32[]{:S(2)}, u32[]{:S(2)}) collective-permute-start(bf16[1024,768]{1,0:T(8,128)(2,1)} %get-tuple-element.71), channel_id=1, source_target_pairs={{0,1},{1,0},{2,3},{3,2},{4,5},{5,4},{6,7},{7,6},{8,9},{9,8},{10,11... | collective-permute-start | bytes 4718600 | tf_op jit(solution)/shard_map/ppermute | solution.py:38
  131.2 37.2 %collective-permute-start.3 = (bf16[768,1664]{1,0:T(8,128)(2,1)S(1)}, bf16[768,1664]{1,0:T(8,128)(2,1)}, u32[]{:S(2)}, u32[]{:S(2)}) collective-permute-start(bf16[768,1664]{1,0:T(8,128)(2,1)S(1)} %bitcast.109), channel_id=1, source_target_pairs={{0,1},{1,0},{2,3},{3,2},{4,5},{5,4},{6,7},{7,6},{8,9},{9,8},{10,11... | collective-permute-start | bytes 7667720 | tf_op jit(solution)/shard_map/ppermute | solution.py:38
  135.4 29.5 %all-to-all-start.2 = ((bf16[64,16,768]{2,1,0:T(8,128)(2,1)}), bf16[64,16,768]{2,1,0:T(8,128)(2,1)}, u32[]{:S(2)}, u32[]{:S(2)}) async-start(bf16[64,16,768]{2,1,0:T(8,128)(2,1)} %bitcast.120), calls=%async_computation.2 | async-start | bytes 3145728 | tf_op jit(solution)/shard_map/all_to_all | solution.py:42
  179.1 53.4 %copy-start.25 = (bf16[2,1,768,768]{3,2,1,0:T(8,128)(2,1)S(1)}, bf16[2,1,768,768]{3,2,1,0:T(8,128)(2,1)}, u32[]{:S(2)}) copy-start(bf16[2,1,768,768]{3,2,1,0:T(8,128)(2,1)} %w_in.11) | copy-start | bytes 7077892
  179.1 53.4 %copy-start.29 = (bf16[2,1,768,768]{3,2,1,0:T(8,128)(2,1)S(1)}, bf16[2,1,768,768]{3,2,1,0:T(8,128)(2,1)}, u32[]{:S(2)}) copy-start(bf16[2,1,768,768]{3,2,1,0:T(8,128)(2,1)} %w_out.11) | copy-start | bytes 7077892
  223.6 8.9 %collective-permute-start.4 = (bf16[64,2,16,768]{3,2,1,0:T(8,128)(2,1)S(1)}, bf16[64,2,16,768]{3,2,1,0:T(8,128)(2,1)S(1)}, u32[]{:S(2)}, u32[]{:S(2)}) collective-permute-start(bf16[64,2,16,768]{3,2,1,0:T(8,128)(2,1)S(1)} %bitcast.106), channel_id=1, source_target_pairs={{0,1},{1,0},{2,3},{3,2},{4,5},{5,4},{6,7},{7,6},{8,9},{9,8},{10,11... | collective-permute-start | bytes 9437192 | tf_op jit(solution)/shard_map/ppermute | solution.py:38
  242.4 9.2 %collective-permute-start.5 = (bf16[64,2,16,768]{3,2,1,0:T(8,128)(2,1)S(1)}, bf16[64,2,16,768]{3,2,1,0:T(8,128)(2,1)S(1)}, u32[]{:S(2)}, u32[]{:S(2)}) collective-permute-start(bf16[64,2,16,768]{3,2,1,0:T(8,128)(2,1)S(1)} %get-tuple-element.77), channel_id=1, source_target_pairs={{0,1},{1,0},{2,3},{3,2},{4,5},{5,4},{6,7},{7,6},{8,9},{9,8},{10,11... | collective-permute-start | bytes 9437192 | tf_op jit(solution)/shard_map/ppermute | solution.py:38
  254.4 46.9 %all-to-all-start.5 = ((bf16[64,32,768]{2,1,0:T(8,128)(2,1)}), bf16[64,32,768]{2,1,0:T(8,128)(2,1)}, u32[]{:S(2)}, u32[]{:S(2)}) async-start(bf16[64,32,768]{2,1,0:T(8,128)(2,1)} %bitcast.117), calls=%async_computation.5 | async-start | bytes 6291456 | tf_op jit(solution)/shard_map/all_to_all | solution.py:42
  322.2 10.2 %collective-permute-start.6 = (bf16[768,1664]{1,0:T(8,128)(2,1)}, bf16[768,1664]{1,0:T(8,128)(2,1)}, u32[]{:S(2)}, u32[]{:S(2)}) collective-permute-start(bf16[768,1664]{1,0:T(8,128)(2,1)} %get-tuple-element.88), channel_id=1, source_target_pairs={{0,1},{1,0},{2,3},{3,2},{4,5},{5,4},{6,7},{7,6},{8,9},{9,8},{10,11... | collective-permute-start | bytes 7667720 | tf_op jit(solution)/shard_map/ppermute | solution.py:38
  326.5 29.1 %all-to-all-start.6 = ((bf16[64,16,768]{2,1,0:T(8,128)(2,1)}), bf16[64,16,768]{2,1,0:T(8,128)(2,1)}, u32[]{:S(2)}, u32[]{:S(2)}) async-start(bf16[64,16,768]{2,1,0:T(8,128)(2,1)} %bitcast.128), calls=%async_computation.6 | async-start | bytes 3145728 | tf_op jit(solution)/shard_map/all_to_all | solution.py:42
  355.5 5.0 collective-permute-start.7
  371.0 16.4 %collective-permute-start.8 = (bf16[1024,768]{1,0:T(8,128)(2,1)}, bf16[1024,768]{1,0:T(8,128)(2,1)}, u32[]{:S(2)}, u32[]{:S(2)}) collective-permute-start(bf16[1024,768]{1,0:T(8,128)(2,1)} %get-tuple-element.93), channel_id=1, source_target_pairs={{0,1},{1,0},{2,3},{3,2},{4,5},{5,4},{6,7},{7,6},{8,9},{9,8},{10,11... | collective-permute-start | bytes 4718600 | tf_op jit(solution)/shard_map/ppermute | solution.py:38
  373.9 22.8 %all-to-all-start.7 = ((bf16[32,24,768]{2,1,0:T(8,128)(2,1)}), bf16[32,24,768]{2,1,0:T(8,128)(2,1)}, u32[]{:S(2)}, u32[]{:S(2)}) async-start(bf16[32,24,768]{2,1,0:T(8,128)(2,1)} %bitcast.121), calls=%async_computation.7 | async-start | bytes 2359296 | tf_op jit(solution)/shard_map/all_to_all | solution.py:128
  396.7 28.4 %all-to-all-start.8 = ((bf16[64,16,768]{2,1,0:T(8,128)(2,1)}), bf16[64,16,768]{2,1,0:T(8,128)(2,1)S(1)}, u32[]{:S(2)}, u32[]{:S(2)}) async-start(bf16[64,16,768]{2,1,0:T(8,128)(2,1)} %bitcast.38), calls=%async_computation.8 | async-start | bytes 3145728 | tf_op jit(solution)/shard_map/all_to_all | solution.py:42
  427.6 22.6 %all-to-all-start.9 = ((bf16[32,24,896]{2,1,0:T(8,128)(2,1)}), bf16[32,24,896]{2,1,0:T(8,128)(2,1)}, u32[]{:S(2)}, u32[]{:S(2)}) async-start(bf16[32,24,896]{2,1,0:T(8,128)(2,1)} %bitcast.40), calls=%async_computation.9 | async-start | bytes 2752512 | tf_op jit(solution)/shard_map/all_to_all | solution.py:128
  450.1 8.5 %collective-permute-start.9 = (bf16[768,1664]{1,0:T(8,128)(2,1)}, bf16[768,1664]{1,0:T(8,128)(2,1)}, u32[]{:S(2)}, u32[]{:S(2)}) collective-permute-start(bf16[768,1664]{1,0:T(8,128)(2,1)} %copy-done.23), channel_id=1, source_target_pairs={{0,1},{1,0},{2,3},{3,2},{4,5},{5,4},{6,7},{7,6},{8,9},{9,8},{10,11... | collective-permute-start | bytes 7667720 | tf_op jit(solution)/shard_map/ppermute | solution.py:38
  477.6 16.7 %collective-permute-start.14 = (bf16[24,1536]{1,0:T(8,128)(2,1)S(1)}, bf16[24,1536]{1,0:T(8,128)(2,1)S(1)}, u32[]{:S(2)}, u32[]{:S(2)}) collective-permute-start(bf16[24,1536]{1,0:T(8,128)(2,1)S(1)} %fusion.70), channel_id=1, source_target_pairs={{0,1},{1,0},{2,3},{3,2},{4,5},{5,4},{6,7},{7,6},{8,9},{9,8},{10,11... | collective-permute-start | bytes 221192 | tf_op jit(solution)/shard_map/ppermute | solution.py:134
  478.0 16.2 %collective-permute-start.15 = (bf16[24,1536]{1,0:T(8,128)(2,1)S(1)}, bf16[24,1536]{1,0:T(8,128)(2,1)S(1)}, u32[]{:S(2)}, u32[]{:S(2)}) collective-permute-start(bf16[24,1536]{1,0:T(8,128)(2,1)S(1)} %fusion.70), channel_id=1, source_target_pairs={{0,3},{1,2},{2,1},{3,0},{4,7},{5,6},{6,5},{7,4},{8,11},{9,10},{10,... | collective-permute-start | bytes 221192 | tf_op jit(solution)/shard_map/ppermute | solution.py:134
  479.9 14.3 %collective-permute-start.11 = (bf16[24,1664]{1,0:T(8,128)(2,1)S(1)}, bf16[24,1664]{1,0:T(8,128)(2,1)S(1)}, u32[]{:S(2)}, u32[]{:S(2)}) collective-permute-start(bf16[24,1664]{1,0:T(8,128)(2,1)S(1)} %pad_maximum_fusion.2), channel_id=1, source_target_pairs={{0,2},{1,3},{2,0},{3,1},{4,6},{5,7},{6,4},{7,5},{8,10},{9,11},{10,... | collective-permute-start | bytes 239624 | tf_op jit(solution)/shard_map/ppermute | solution.py:134
  481.0 38.4 %all-to-all-start.10 = ((bf16[32,24,1664]{2,1,0:T(8,128)(2,1)}), bf16[32,24,1664]{2,1,0:T(8,128)(2,1)S(1)}, u32[]{:S(2)}, u32[]{:S(2)}) async-start(bf16[32,24,1664]{2,1,0:T(8,128)(2,1)} %bitcast.118), calls=%async_computation.10 | async-start | bytes 5111808 | tf_op jit(solution)/shard_map/all_to_all | solution.py:128
  519.8 5.9 %collective-permute-start.12 = (bf16[24,1536]{1,0:T(8,128)(2,1)S(1)}, bf16[24,1536]{1,0:T(8,128)(2,1)S(1)}, u32[]{:S(2)}, u32[]{:S(2)}) collective-permute-start(bf16[24,1536]{1,0:T(8,128)(2,1)S(1)} %slice.348), channel_id=1, source_target_pairs={{0,1},{1,0},{2,3},{3,2},{4,5},{5,4},{6,7},{7,6},{8,9},{9,8},{10,11... | collective-permute-start | bytes 221192 | tf_op jit(solution)/shard_map/ppermute | solution.py:134
  522.7 5.5 %collective-permute-start.13 = (bf16[24,1536]{1,0:T(8,128)(2,1)S(1)}, bf16[24,1536]{1,0:T(8,128)(2,1)S(1)}, u32[]{:S(2)}, u32[]{:S(2)}) collective-permute-start(bf16[24,1536]{1,0:T(8,128)(2,1)S(1)} %slice.348), channel_id=1, source_target_pairs={{0,3},{1,2},{2,1},{3,0},{4,7},{5,6},{6,5},{7,4},{8,11},{9,10},{10,... | collective-permute-start | bytes 221192 | tf_op jit(solution)/shard_map/ppermute | solution.py:134
  524.6 4.8 collective-permute-start.10
  (104 other events, 881.1 us)

commit v7 on v6

--- a/solution.py
+++ b/solution.py
@@ -135,18 +135,22 @@
 
 
 def sum_finish(*parts):
-    part = jnp.concatenate([jnp.sum(p.astype(F32), axis=0) for p in parts], axis=1).astype(BF)
+    blocks = len(parts)
+    part = jnp.concatenate([jnp.sum(p.astype(F32), axis=0) for p in parts], axis=0).astype(BF)
     full = part.astype(F32) + swap_row(part, 2).astype(F32)
     dense = part[:, :1536]
     other = swap_row(dense, 1).astype(F32) + swap_row(dense, 3).astype(F32)
     qkv = [
         in_order(own, more) for own, more in zip(thirds(full[:, :1152]), thirds(other[:, :1152]))
     ]
-    return (
-        jnp.concatenate(qkv, axis=1),
-        in_order(full[:, 1152:1536], other[:, 1152:]),
-        full[:, 1536:],
-    )
+    return [
+        value.reshape(blocks, -1, value.shape[1])
+        for value in (
+            jnp.concatenate(qkv, axis=1),
+            in_order(full[:, 1152:1536], other[:, 1152:]),
+            full[:, 1536:],
+        )
+    ]
 
 
 def pad_cols(value, cols):
@@ -446,7 +450,8 @@
         expert_call(forward_kernel, 0, [r], weights, [r.shape] * 3, 2) for r in rows0
     ]
     hidden0, slope0, part = zip(*first)
-    returned = exchange(join_cores(*part))
+    back, gathered1 = lax.optimization_barrier((join_cores(*part), gathered1))
+    returned = exchange(back)
     dense1 = split_dense(gathered1)
     picked = dot(fetch, returned)
     picked0 = (picked[:tokens], picked[tokens:])
@@ -483,38 +488,29 @@
     arrived = exchange(dot(send, grad_rows).astype(BF))
     pair1 = sum_send(*grads1)
     arrived, pair1 = lax.optimization_barrier((arrived, pair1))
-    parts1a = sum_exchange(pair1[:, :768])
     grows0 = (arrived, swap_core(arrived))
     third = [
         expert_call(backward_kernel, 0, [r, s], weights, [r.shape] * 2, 2)
         for r, s in zip(grows0, slope0)
     ]
     grad_pre0, part = zip(*third)
-    back, parts1a = lax.optimization_barrier((join_cores(*part), parts1a))
-    returned = exchange(back)
-    returned, pair1 = lax.optimization_barrier((returned, pair1))
-    parts1b = sum_exchange(pair1[:, 768:])
+    returned = exchange(join_cores(*part))
+    grad_w_out0 = sum(dot_tn(h, g) for h, g in zip(hidden0, grows0))
+    grad_w_in0 = sum(dot_tn(r, g) for r, g in zip(rows0, grad_pre0))
+    returned, pair1, grad_w_out0, grad_w_in0 = lax.optimization_barrier(
+        (returned, pair1, grad_w_out0, grad_w_in0)
+    )
+    parts1 = sum_exchange(pair1)
     picked = dot(fetch, returned)
     grad_sent = picked[:tokens] + picked[tokens:]
     extra, grad_router_w0 = router_back(
         grad, picked0, router0, onehot0, normed0, dense0[0][:, 1536 : 1536 + experts]
     )
     grad, grads0 = attention_back(grad, grad_sent + extra, grad_router_w0, kept0, dense0)
-    grads0, parts1b = lax.optimization_barrier((grads0, parts1b))
-    pair0 = sum_send(*grads0)
-    parts0 = sum_exchange(pair0)
-    (hidden0, grows0, rows0, grad_pre0), _ = lax.optimization_barrier(
-        ((hidden0, grows0, rows0, grad_pre0), pair0)
-    )
-    grad_w_out0 = sum(dot_tn(h, g) for h, g in zip(hidden0, grows0))
-    grad_w_in0 = sum(dot_tn(r, g) for r, g in zip(rows0, grad_pre0))
-    (grad_w_out0, grad_w_in0), parts1b = lax.optimization_barrier(
-        ((grad_w_out0, grad_w_in0), parts1b)
-    )
-    sums1 = sum_finish(parts1a, parts1b)
-    sums0 = sum_finish(parts0)
-
-    qkv_sum, out_sum, small = (jnp.stack(pair) for pair in zip(sums0, sums1))
+    grads0, parts1 = lax.optimization_barrier((grads0, parts1))
+    parts0 = sum_exchange(sum_send(*grads0))
+    qkv_sum, out_sum, small = sum_finish(parts0, parts1)
+
     return (
         block_out,
         grad,

time: 542 us -> 511 us (0.943)
  local copies, waits for them, and re-layouts: 45.2 us -> 30 us
  starting transfers between devices: 70.9 us -> 61.1 us
  other arithmetic: 47.7 us -> 40.5 us
    unnamed x234 -> x228, local copies, waits for them, and re-layouts: 32.8 us -> 23.3 us
    all_to_all x4, waiting for transfers between devices: 79.1 us -> 69.8 us  [exchange(): return lax.all_to_all(rows, GROUP, split_axis=0, concat_axis=0, tiled=True)]
    all_to_all x3 -> x2, starting transfers between devices: 15.8 us -> 10.2 us  [sum_exchange(): lax.all_to_all(pair.reshape(groups, -1, pair.shape[1]), 'ea', split_axis=...]
    all_to_all x3 -> x2, waiting for transfers between devices: 33.7 us -> 39 us  [sum_exchange(): lax.all_to_all(pair.reshape(groups, -1, pair.shape[1]), 'ea', split_axis=...]
  transfers between devices with their start and end apart: 24 -> 20, of which waited for: 14 -> 13; matrix products, arithmetic and copies ran while one was open for 11% -> 13% of each run, Pallas kernels for 7% -> 7%
where the time goes in v7:
time: 511 us; the launch traced here: 502 us
  waiting for transfers between devices  143 us (28%)
  blocking collectives  114 us (22%)
  Pallas kernels  70 us (14%)
  starting transfers between devices  61.1 us (12%)
  matrix products  40.9 us (8%)
  other arithmetic  40.5 us (8%)
  local copies, waits for them, and re-layouts  30 us (6%)
    all_to_all x2, blocking collectives, exchange(): return lax.all_to_all(rows, GROUP, split_axis=0, concat_axis=0, tiled=True)  72.9 us
    all_to_all x4, waiting for transfers between devices, exchange(): return lax.all_to_all(rows, GROUP, split_axis=0, concat_axis=0, tiled=True)  69.8 us
    all_to_all x1, blocking collectives, gather_cols(): got = lax.all_to_all(sent, 'ea', split_axis=0, concat_axis=0)  41.4 us
    all_to_all x2, waiting for transfers between devices, sum_exchange(): lax.all_to_all(pair.reshape(groups, -1, pair.shape[1]), 'ea', split_axis=...  39 us
    dot_general x16, matrix products, dot(): return lax.dot_general(a, b, (dims, ((), ())), preferred_element_type=F32)  38.5 us
    pallas_call x6, Pallas kernels, expert_call(): pl.pallas_call(kernel, grid=(count // (GROUPS * SLOTS),), in_specs=[spec(...  36.1 us
    pallas_call x4, Pallas kernels, whole_call(): pl.pallas_call(kernel, in_specs=[pl.BlockSpec(memory_space=pltpu.SMEM)] +...  33.9 us
    all_to_all x4, starting transfers between devices, exchange(): return lax.all_to_all(rows, GROUP, split_axis=0, concat_axis=0, tiled=True)  23.7 us
  transfers between devices with their start and end apart: 20, of which 13 were waited for; matrix products, arithmetic and copies ran while one was open for 13% of the time, Pallas kernels for 7%

profile of v7, /device:TPU:1, one launch (start us, length us, event | category | flops | bytes accessed | tf_op | source)
XLA Modules:
  0.0 501.9 jit_solution(287109416322234514)
XLA Ops:
  5.1 41.4 %all_to_all.88 = bf16[32,24,1664]{2,1,0:T(8,128)(2,1)S(1)} all-to-all(bf16[32,24,1664]{2,1,0:T(8,128)(2,1)S(1)} %broadcast_in_dim.8), channel_id=1, replica_groups=mesh['ea'=32,'half'=2,'core'=2] {'ea'}, dimensions={0} | all-to-all | bytes 5111808 | tf_op jit(solution)/shard_map/all_to_all | solution.py:92
  58.4 29.4 %all_to_all.89 = bf16[64,16,768]{2,1,0:T(8,128)(2,1)} all-to-all(bf16[64,16,768]{2,1,0:T(8,128)(2,1)S(1)} %bitcast.113), channel_id=1, replica_groups=mesh['ea'=32,'half'=2,'core'=2] {'ea','half'}, dimensions={0} | all-to-all | bytes 3145728 | tf_op jit(solution)/shard_map/all_to_all | solution.py:42
  99.1 6.6 %shard_map.171 = (bf16[1024,768]{1,0:T(8,128)(2,1)S(1)}, bf16[1024,768]{1,0:T(8,128)(2,1)S(1)}, bf16[1024,768]{1,0:T(8,128)(2,1)S(1)}) custom-call(bf16[1024,768]{1,0:T(8,128)(2,1)} %collective-permute-done.1.rows, bf16[2,1,768,768]{3,2,1,0:T(8,128)(2,1)S(1)} %copy-done.24, bf16[2,1,768,768]{3,2,1,0:T(8,128)(2,1)S(1)} %copy-done.29), custom_call_target="tpu_custom_call" | custom-call | flops 2415919104 | bytes 8650752 | tf_op jit(solution)/shard_map/pallas_call | solution.py:342
  109.9 6.4 %shard_map.170 = (bf16[1024,768]{1,0:T(8,128)(2,1)S(1)}, bf16[1024,768]{1,0:T(8,128)(2,1)S(1)}, bf16[1024,768]{1,0:T(8,128)(2,1)S(1)}) custom-call(bf16[1024,768]{1,0:T(8,128)(2,1)} %bitcast.13.rows, bf16[2,1,768,768]{3,2,1,0:T(8,128)(2,1)S(1)} %copy-done.25, bf16[2,1,768,768]{3,2,1,0:T(8,128)(2,1)S(1)} %copy-done.29), custom_call_target="tpu_custom_call" | custom-call | flops 2415919104 | bytes 8650752 | tf_op jit(solution)/shard_map/pallas_call | solution.py:342
  120.2 11.0 %all-to-all-done.2 = bf16[32,24,1664]{2,1,0:T(8,128)(2,1)S(1)} async-done(((bf16[32,24,1664]{2,1,0:T(8,128)(2,1)}), bf16[32,24,1664]{2,1,0:T(8,128)(2,1)S(1)}, u32[]{:S(2)}, u32[]{:S(2)}) %all-to-all-start.2) | async-done | bytes 2555936 | tf_op jit(solution)/shard_map/all_to_all | solution.py:92
  132.0 6.7 %all-to-all-start.3 = ((bf16[64,16,768]{2,1,0:T(8,128)(2,1)}), bf16[64,16,768]{2,1,0:T(8,128)(2,1)}, u32[]{:S(2)}, u32[]{:S(2)}) async-start(bf16[64,16,768]{2,1,0:T(8,128)(2,1)} %bitcast.114), calls=%async_computation.3 | async-start | bytes 3145728 | tf_op jit(solution)/shard_map/all_to_all | solution.py:42
  138.8 5.1 %and_convert_fusion.1 = (bf16[2048,394]{1,0:T(8,128)(2,1)S(1)}, bf16[2048,394]{1,0:T(8,128)(2,1)}) fusion(s32[2048]{0:T(1024)S(1)} %get-tuple-element.170, s32[2048]{0:T(1024)S(1)} %broadcast_add_fusion, pred[2048]{0:T(1024)(128)(4,1)S(1)} %fusion.80, s32[394]{0:T(512)S(1)} %convert_add_fusion.2, s32[2048]{0:T(1024)S(1)} %get-tuple-element.171), kind=kLoop, calls=%fused_computation.35 | loop fusion | flops 22593536 | bytes 3255848 | tf_op jit(solution)/shard_map/convert_element_type | solution.py:387
  145.8 16.3 %all-to-all-done.3 = bf16[64,16,768]{2,1,0:T(8,128)(2,1)} async-done(((bf16[64,16,768]{2,1,0:T(8,128)(2,1)}), bf16[64,16,768]{2,1,0:T(8,128)(2,1)}, u32[]{:S(2)}, u32[]{:S(2)}) %all-to-all-start.3) | async-done | bytes 1572896 | tf_op jit(solution)/shard_map/all_to_all | solution.py:42
  165.5 6.0 %shard_map.172 = (bf16[197,1152]{1,0:T(8,128)(2,1)S(1)}, bf16[197,1152]{1,0:T(8,128)(2,1)S(1)}, bf16[197,768]{1,0:T(8,128)(2,1)S(1)}, f32[197,768]{1,0:T(8,128)S...) custom-call(s32[1]{0:T(128)} %bitcast.core_ref, f32[197,768]{1,0:T(8,128)S(1)} %multiply_add_fusion.state, ...), custom_call_target="tpu_custom_call" | custom-call | flops 2336010240 | bytes 8388608 | tf_op jit(solution)/shard_map/pallas_call | solution.py:262
  176.3 43.6 %all_to_all.90 = bf16[64,32,768]{2,1,0:T(8,128)(2,1)S(1)} all-to-all(bf16[64,32,768]{2,1,0:T(8,128)(2,1)S(1)} %bitcast.116), channel_id=1, replica_groups=mesh['ea'=32,'half'=2,'core'=2] {'ea','half'}, dimensions={0} | all-to-all | bytes 6291456 | tf_op jit(solution)/shard_map/all_to_all | solution.py:42
  223.3 5.3 %collective-permute-done.4.rows = bf16[64,2,16,768]{3,2,1,0:T(8,128)(2,1)S(1)} collective-permute-done((bf16[64,2,16,768]{3,2,1,0:T(8,128)(2,1)S(1)}, bf16[64,2,16,768]{3,2,1,0:T(8,128)(2,1)S(1)}, u32[]{:S(2)}, u32[]{:S(2)}) %collective-permute-start.4) | collective-permute-done | bytes 3145760 | tf_op jit(solution)/shard_map/ppermute | solution.py:38
  228.6 7.7 %shard_map.174 = (bf16[1024,768]{1,0:T(8,128)(2,1)S(1)}, bf16[1024,768]{1,0:T(8,128)(2,1)S(1)}, bf16[64,2,16,768]{3,2,1,0:T(8,128)(2,1)S(1)}) custom-call(bf16[64,2,16,768]{3,2,1,0:T(8,128)(2,1)S(1)} %collective-permute-done.4.rows, bf16[2,1,768,768]{3,2,1,0:T(8,128)(2,1)S(1)} %copy-done.26, bf16[2,1,768,768]{3,2,1,0:T(8,128)(2,1)S(1)} %copy-done.30), custom_call_target="tpu_custom_call" | custom-call | flops 4831838208 | bytes 8650752 | tf_op jit(solution)/shard_map/pallas_call | solution.py:342
  239.0 7.8 %shard_map.173 = (bf16[1024,768]{1,0:T(8,128)(2,1)S(1)}, bf16[1024,768]{1,0:T(8,128)(2,1)S(1)}, bf16[64,2,16,768]{3,2,1,0:T(8,128)(2,1)S(1)}) custom-call(bf16[64,2,16,768]{3,2,1,0:T(8,128)(2,1)S(1)} %bitcast.100, bf16[2,1,768,768]{3,2,1,0:T(8,128)(2,1)S(1)} %copy-done.26, bf16[2,1,768,768]{3,2,1,0:T(8,128)(2,1)S(1)} %copy-done.30), custom_call_target="tpu_custom_call" | custom-call | flops 4831838208 | bytes 8650752 | tf_op jit(solution)/shard_map/pallas_call | solution.py:342
  249.7 5.6 %all-to-all-start.5 = ((bf16[64,32,768]{2,1,0:T(8,128)(2,1)}), bf16[64,32,768]{2,1,0:T(8,128)(2,1)}, u32[]{:S(2)}, u32[]{:S(2)}) async-start(bf16[64,32,768]{2,1,0:T(8,128)(2,1)} %bitcast.110), calls=%async_computation.5 | async-start | bytes 6291456 | tf_op jit(solution)/shard_map/all_to_all | solution.py:42
  272.3 24.3 %all-to-all-done.5 = bf16[64,32,768]{2,1,0:T(8,128)(2,1)} async-done(((bf16[64,32,768]{2,1,0:T(8,128)(2,1)}), bf16[64,32,768]{2,1,0:T(8,128)(2,1)}, u32[]{:S(2)}, u32[]{:S(2)}) %all-to-all-start.5) | async-done | bytes 3145760 | tf_op jit(solution)/shard_map/all_to_all | solution.py:42
  303.6 13.7 %shard_map.175 = (f32[197,768]{1,0:T(8,128)S(1)}, bf16[768,1664]{1,0:T(8,128)(2,1)S(1)}, bf16[768,1664]{1,0:T(8,128)(2,1)}) custom-call(s32[1]{0:T(128)} %bitcast.core_ref, f32[197,768]{1,0:T(8,128)S(1)} %copy-done.10, f32[197,768]{1,0:T(8,128)S(1)} %convolution_add_fusion.4.grad_two, f32[197,768]{1,0:T(8,128)S(1)} %copy-done.16, f32[197,768]{1,0:T(8,128)S(1)} %copy-done.18, ...), custom_call_target="tpu_custom_call" | custom-call | flops 8438685696 | bytes 8388608 | tf_op jit(solution)/shard_map/pallas_call | solution.py:262
  321.6 5.9 %all-to-all-start.6 = ((bf16[64,16,768]{2,1,0:T(8,128)(2,1)}), bf16[64,16,768]{2,1,0:T(8,128)(2,1)}, u32[]{:S(2)}, u32[]{:S(2)}) async-start(bf16[64,16,768]{2,1,0:T(8,128)(2,1)} %bitcast.121), calls=%async_computation.6 | async-start | bytes 3145728 | tf_op jit(solution)/shard_map/all_to_all | solution.py:42
  331.4 19.3 %all-to-all-done.6 = bf16[64,16,768]{2,1,0:T(8,128)(2,1)} async-done(((bf16[64,16,768]{2,1,0:T(8,128)(2,1)}), bf16[64,16,768]{2,1,0:T(8,128)(2,1)}, u32[]{:S(2)}, u32[]{:S(2)}) %all-to-all-start.6) | async-done | bytes 1572896 | tf_op jit(solution)/shard_map/all_to_all | solution.py:42
  363.9 4.6 shard_map.176
  370.2 5.5 %all-to-all-start.7 = ((bf16[64,16,768]{2,1,0:T(8,128)(2,1)}), bf16[64,16,768]{2,1,0:T(8,128)(2,1)}, u32[]{:S(2)}, u32[]{:S(2)}) async-start(bf16[64,16,768]{2,1,0:T(8,128)(2,1)} %bitcast.115), calls=%async_computation.7 | async-start | bytes 3145728 | tf_op jit(solution)/shard_map/all_to_all | solution.py:42
  380.7 4.3 fusion.113
  385.0 4.2 convolution_add_fusion
  389.2 10.0 %all-to-all-done.7 = bf16[64,16,768]{2,1,0:T(8,128)(2,1)} async-done(((bf16[64,16,768]{2,1,0:T(8,128)(2,1)}), bf16[64,16,768]{2,1,0:T(8,128)(2,1)}, u32[]{:S(2)}, u32[]{:S(2)}) %all-to-all-start.7) | async-done | bytes 1572896 | tf_op jit(solution)/shard_map/all_to_all | solution.py:42
  399.2 5.1 %all-to-all-start.8 = ((bf16[32,24,1664]{2,1,0:T(8,128)(2,1)}), bf16[32,24,1664]{2,1,0:T(8,128)(2,1)}, u32[]{:S(2)}, u32[]{:S(2)}) async-start(bf16[32,24,1664]{2,1,0:T(8,128)(2,1)} %bitcast.111), calls=%async_computation.8 | async-start | bytes 5111808 | tf_op jit(solution)/shard_map/all_to_all | solution.py:128
  409.1 10.2 %shard_map.178 = (f32[197,768]{1,0:T(8,128)}, bf16[768,1664]{1,0:T(8,128)(2,1)S(1)}, bf16[768,1664]{1,0:T(8,128)(2,1)S(1)}) custom-call(s32[1]{0:T(128)} %bitcast.core_ref, f32[197,768]{1,0:T(8,128)S(1)} %copy-done.14, f32[197,768]{1,0:T(8,128)S(1)} %convolution_add_fusion.3.grad_two, f32[197,768]{1,0:T(8,128)S(1)} %copy-done.9, f32[197,768]{1,0:T(8,128)S(1)} %copy-done.12, ...), custom_call_target="tpu_custom_call" | custom-call | flops 8438685696 | bytes 8388608 | tf_op jit(solution)/shard_map/pallas_call | solution.py:262
  420.8 15.5 %all-to-all-done.8 = bf16[32,24,1664]{2,1,0:T(8,128)(2,1)} async-done(((bf16[32,24,1664]{2,1,0:T(8,128)(2,1)}), bf16[32,24,1664]{2,1,0:T(8,128)(2,1)}, u32[]{:S(2)}, u32[]{:S(2)}) %all-to-all-start.8) | async-done | bytes 2555936 | tf_op jit(solution)/shard_map/all_to_all | solution.py:128
  436.3 4.7 collective-permute-start.9
  441.0 4.7 collective-permute-done.9
  447.9 5.1 %all-to-all-start.9 = ((bf16[32,24,1664]{2,1,0:T(8,128)(2,1)}), bf16[32,24,1664]{2,1,0:T(8,128)(2,1)S(1)}, u32[]{:S(2)}, u32[]{:S(2)}) async-start(bf16[32,24,1664]{2,1,0:T(8,128)(2,1)} %bitcast.112), calls=%async_computation.9 | async-start | bytes 5111808 | tf_op jit(solution)/shard_map/all_to_all | solution.py:128
  453.0 5.0 %maximum_bitcast_fusion.1 = f32[2,1,768,768]{3,2,1,0:T(8,128)} fusion(f32[1,768,768]{2,1,0:T(8,128)} %bitcast.118, f32[1,768,768]{2,1,0:T(8,128)} %bitcast.119), kind=kLoop, calls=%fused_computation.24 | loop fusion | flops 1179648 | bytes 9437184
  462.6 23.6 %all-to-all-done.9 = bf16[32,24,1664]{2,1,0:T(8,128)(2,1)S(1)} async-done(((bf16[32,24,1664]{2,1,0:T(8,128)(2,1)}), bf16[32,24,1664]{2,1,0:T(8,128)(2,1)S(1)}, u32[]{:S(2)}, u32[]{:S(2)}) %all-to-all-start.9) | async-done | bytes 2555936 | tf_op jit(solution)/shard_map/all_to_all | solution.py:128
  492.2 4.6 collective-permute-done.12
  (342 shorter events, 130.6 us)
Async XLA Ops:
  5.0 44.2 %copy-start.74 = (bf16[197,768]{1,0:T(8,128)(2,1)S(1)}, bf16[197,768]{1,0:T(8,128)(2,1)}, u32[]{:S(2)}) copy-start(bf16[197,768]{1,0:T(8,128)(2,1)} %param.10) | copy-start | bytes 907780
  5.1 44.2 %copy-start.106 = (s32[2,197,2]{1,2,0:T(2,128)S(1)}, s32[2,197,2]{1,2,0:T(2,128)}, u32[]{:S(2)}) copy-start(s32[2,197,2]{1,2,0:T(2,128)} %param.12) | copy-start | bytes 9460
  46.5 7.2 %collective-permute-start = (bf16[768,1664]{1,0:T(8,128)(2,1)S(1)}, bf16[768,1664]{1,0:T(8,128)(2,1)S(1)}, u32[]{:S(2)}, u32[]{:S(2)}) collective-permute-start(bf16[768,1664]{1,0:T(8,128)(2,1)S(1)} %bitcast.106), channel_id=1, source_target_pairs={{0,1},{1,0},{2,3},{3,2},{4,5},{5,4},{6,7},{7,6},{8,9},{9,8},{10,11... | collective-permute-start | bytes 7667720 | tf_op jit(solution)/shard_map/ppermute | solution.py:38
  49.3 112.8 %copy-start.107 = (pred[1024]{0:T(1024)(128)(4,1)}, pred[1024]{0:T(1024)(128)(4,1)S(1)}, u32[]{:S(2)}) copy-start(pred[1024]{0:T(1024)(128)(4,1)S(1)} %fusion.86) | copy-start | bytes 3076
  49.4 112.7 %copy-start.87 = (s32[1024]{0:T(1024)}, s32[1024]{0:T(1024)S(1)}, u32[]{:S(2)}) copy-start(s32[1024]{0:T(1024)S(1)} %broadcast_add_fusion.1) | copy-start | bytes 12292
  49.4 112.7 %copy-start.89 = (s32[1024]{0:T(1024)}, s32[1024]{0:T(1024)S(1)}, u32[]{:S(2)}) copy-start(s32[1024]{0:T(1024)S(1)} %get-tuple-element.175) | copy-start | bytes 12292
  49.4 112.7 %copy-start.91 = (s32[1024]{0:T(1024)}, s32[1024]{0:T(1024)S(1)}, u32[]{:S(2)}) copy-start(s32[1024]{0:T(1024)S(1)} %get-tuple-element.176) | copy-start | bytes 12292
  50.0 112.1 %copy-start.104 = (s32[394]{0:T(512)}, s32[394]{0:T(512)S(1)}, u32[]{:S(2)}) copy-start(s32[394]{0:T(512)S(1)} %convert_add_fusion.3) | copy-start | bytes 4732
  57.7 106.7 %copy-start.11 = (f32[197,768]{1,0:T(8,128)}, f32[197,768]{1,0:T(8,128)S(1)}, u32[]{:S(2)}) copy-start(f32[197,768]{1,0:T(8,128)S(1)} %get-tuple-element.58.after) | copy-start | bytes 1815556
  87.8 8.0 %collective-permute-start.1 = (bf16[1024,768]{1,0:T(8,128)(2,1)}, bf16[1024,768]{1,0:T(8,128)(2,1)}, u32[]{:S(2)}, u32[]{:S(2)}) collective-permute-start(bf16[1024,768]{1,0:T(8,128)(2,1)} %bitcast.13.rows), channel_id=1, source_target_pairs={{0,1},{1,0},{2,3},{3,2},{4,5},{5,4},{6,7},{7,6},{8,9},{9,8},{10,11... | collective-permute-start | bytes 4718600 | tf_op jit(solution)/shard_map/ppermute | solution.py:38
  91.7 39.5 %all-to-all-start.2 = ((bf16[32,24,1664]{2,1,0:T(8,128)(2,1)}), bf16[32,24,1664]{2,1,0:T(8,128)(2,1)S(1)}, u32[]{:S(2)}, u32[]{:S(2)}) async-start(bf16[32,24,1664]{2,1,0:T(8,128)(2,1)} %broadcast_in_dim.9), calls=%async_computation.2 | async-start | bytes 5111808 | tf_op jit(solution)/shard_map/all_to_all | solution.py:92
  108.1 10.6 %collective-permute-start.2 = (bf16[1024,768]{1,0:T(8,128)(2,1)S(1)}, bf16[1024,768]{1,0:T(8,128)(2,1)S(1)}, u32[]{:S(2)}, u32[]{:S(2)}) collective-permute-start(bf16[1024,768]{1,0:T(8,128)(2,1)S(1)} %get-tuple-element.62), channel_id=1, source_target_pairs={{0,1},{1,0},{2,3},{3,2},{4,5},{5,4},{6,7},{7,6},{8,9},{9,8},{10,11... | collective-permute-start | bytes 4718600 | tf_op jit(solution)/shard_map/ppermute | solution.py:38
  108.4 30.3 %copy-start.77 = (s32[2048]{0:T(1024)}, s32[2048]{0:T(1024)S(1)}, u32[]{:S(2)}) copy-start(s32[2048]{0:T(1024)S(1)} %get-tuple-element.170) | copy-start | bytes 24580
  131.2 34.3 %copy-start.2 = (bf16[32,24,1664]{2,1,0:T(8,128)(2,1)}, bf16[32,24,1664]{2,1,0:T(8,128)(2,1)S(1)}, u32[]{:S(2)}) copy-start(bf16[32,24,1664]{2,1,0:T(8,128)(2,1)S(1)} %all-to-all-done.2) | copy-start | bytes 7667716
  131.2 34.3 %collective-permute-start.3 = (bf16[768,1664]{1,0:T(8,128)(2,1)S(1)}, bf16[768,1664]{1,0:T(8,128)(2,1)}, u32[]{:S(2)}, u32[]{:S(2)}) collective-permute-start(bf16[768,1664]{1,0:T(8,128)(2,1)S(1)} %bitcast.102), channel_id=1, source_target_pairs={{0,1},{1,0},{2,3},{3,2},{4,5},{5,4},{6,7},{7,6},{8,9},{9,8},{10,11... | collective-permute-start | bytes 7667720 | tf_op jit(solution)/shard_map/ppermute | solution.py:38
  132.0 30.1 %all-to-all-start.3 = ((bf16[64,16,768]{2,1,0:T(8,128)(2,1)}), bf16[64,16,768]{2,1,0:T(8,128)(2,1)}, u32[]{:S(2)}, u32[]{:S(2)}) async-start(bf16[64,16,768]{2,1,0:T(8,128)(2,1)} %bitcast.114), calls=%async_computation.3 | async-start | bytes 3145728 | tf_op jit(solution)/shard_map/all_to_all | solution.py:42
  176.2 52.4 %copy-start.26 = (bf16[2,1,768,768]{3,2,1,0:T(8,128)(2,1)S(1)}, bf16[2,1,768,768]{3,2,1,0:T(8,128)(2,1)}, u32[]{:S(2)}) copy-start(bf16[2,1,768,768]{3,2,1,0:T(8,128)(2,1)} %w_in.11) | copy-start | bytes 7077892
  176.3 52.4 %copy-start.30 = (bf16[2,1,768,768]{3,2,1,0:T(8,128)(2,1)S(1)}, bf16[2,1,768,768]{3,2,1,0:T(8,128)(2,1)}, u32[]{:S(2)}) copy-start(bf16[2,1,768,768]{3,2,1,0:T(8,128)(2,1)} %w_out.11) | copy-start | bytes 7077892
  219.9 8.7 %collective-permute-start.4 = (bf16[64,2,16,768]{3,2,1,0:T(8,128)(2,1)S(1)}, bf16[64,2,16,768]{3,2,1,0:T(8,128)(2,1)S(1)}, u32[]{:S(2)}, u32[]{:S(2)}) collective-permute-start(bf16[64,2,16,768]{3,2,1,0:T(8,128)(2,1)S(1)} %bitcast.99), channel_id=1, source_target_pairs={{0,1},{1,0},{2,3},{3,2},{4,5},{5,4},{6,7},{7,6},{8,9},{9,8},{10,11... | collective-permute-start | bytes 9437192 | tf_op jit(solution)/shard_map/ppermute | solution.py:38
  238.6 8.2 %collective-permute-start.5 = (bf16[64,2,16,768]{3,2,1,0:T(8,128)(2,1)S(1)}, bf16[64,2,16,768]{3,2,1,0:T(8,128)(2,1)S(1)}, u32[]{:S(2)}, u32[]{:S(2)}) collective-permute-start(bf16[64,2,16,768]{3,2,1,0:T(8,128)(2,1)S(1)} %get-tuple-element.70), channel_id=1, source_target_pairs={{0,1},{1,0},{2,3},{3,2},{4,5},{5,4},{6,7},{7,6},{8,9},{9,8},{10,11... | collective-permute-start | bytes 9437192 | tf_op jit(solution)/shard_map/ppermute | solution.py:38
  249.7 46.9 %all-to-all-start.5 = ((bf16[64,32,768]{2,1,0:T(8,128)(2,1)}), bf16[64,32,768]{2,1,0:T(8,128)(2,1)}, u32[]{:S(2)}, u32[]{:S(2)}) async-start(bf16[64,32,768]{2,1,0:T(8,128)(2,1)} %bitcast.110), calls=%async_computation.5 | async-start | bytes 6291456 | tf_op jit(solution)/shard_map/all_to_all | solution.py:42
  317.3 10.2 %collective-permute-start.6 = (bf16[768,1664]{1,0:T(8,128)(2,1)}, bf16[768,1664]{1,0:T(8,128)(2,1)}, u32[]{:S(2)}, u32[]{:S(2)}) collective-permute-start(bf16[768,1664]{1,0:T(8,128)(2,1)} %get-tuple-element.81), channel_id=1, source_target_pairs={{0,1},{1,0},{2,3},{3,2},{4,5},{5,4},{6,7},{7,6},{8,9},{9,8},{10,11... | collective-permute-start | bytes 7667720 | tf_op jit(solution)/shard_map/ppermute | solution.py:38
  321.6 29.1 %all-to-all-start.6 = ((bf16[64,16,768]{2,1,0:T(8,128)(2,1)}), bf16[64,16,768]{2,1,0:T(8,128)(2,1)}, u32[]{:S(2)}, u32[]{:S(2)}) async-start(bf16[64,16,768]{2,1,0:T(8,128)(2,1)} %bitcast.121), calls=%async_computation.6 | async-start | bytes 3145728 | tf_op jit(solution)/shard_map/all_to_all | solution.py:42
  350.6 5.0 collective-permute-start.7
  363.5 5.1 %collective-permute-start.8 = (bf16[1024,768]{1,0:T(8,128)(2,1)S(1)}, bf16[1024,768]{1,0:T(8,128)(2,1)S(1)}, u32[]{:S(2)}, u32[]{:S(2)}) collective-permute-start(bf16[1024,768]{1,0:T(8,128)(2,1)S(1)} %get-tuple-element.86), channel_id=1, source_target_pairs={{0,1},{1,0},{2,3},{3,2},{4,5},{5,4},{6,7},{7,6},{8,9},{9,8},{10,11... | collective-permute-start | bytes 4718600 | tf_op jit(solution)/shard_map/ppermute | solution.py:38
  370.2 28.9 %all-to-all-start.7 = ((bf16[64,16,768]{2,1,0:T(8,128)(2,1)}), bf16[64,16,768]{2,1,0:T(8,128)(2,1)}, u32[]{:S(2)}, u32[]{:S(2)}) async-start(bf16[64,16,768]{2,1,0:T(8,128)(2,1)} %bitcast.115), calls=%async_computation.7 | async-start | bytes 3145728 | tf_op jit(solution)/shard_map/all_to_all | solution.py:42
  399.2 37.1 %all-to-all-start.8 = ((bf16[32,24,1664]{2,1,0:T(8,128)(2,1)}), bf16[32,24,1664]{2,1,0:T(8,128)(2,1)}, u32[]{:S(2)}, u32[]{:S(2)}) async-start(bf16[32,24,1664]{2,1,0:T(8,128)(2,1)} %bitcast.111), calls=%async_computation.8 | async-start | bytes 5111808 | tf_op jit(solution)/shard_map/all_to_all | solution.py:128
  436.3 9.4 %collective-permute-start.9 = (bf16[768,1664]{1,0:T(8,128)(2,1)}, bf16[768,1664]{1,0:T(8,128)(2,1)S(1)}, u32[]{:S(2)}, u32[]{:S(2)}) collective-permute-start(bf16[768,1664]{1,0:T(8,128)(2,1)} %copy-done.23), channel_id=1, source_target_pairs={{0,1},{1,0},{2,3},{3,2},{4,5},{5,4},{6,7},{7,6},{8,9},{9,8},{10,11... | collective-permute-start | bytes 7667720 | tf_op jit(solution)/shard_map/ppermute | solution.py:38
  447.9 38.3 %all-to-all-start.9 = ((bf16[32,24,1664]{2,1,0:T(8,128)(2,1)}), bf16[32,24,1664]{2,1,0:T(8,128)(2,1)S(1)}, u32[]{:S(2)}, u32[]{:S(2)}) async-start(bf16[32,24,1664]{2,1,0:T(8,128)(2,1)} %bitcast.112), calls=%async_computation.9 | async-start | bytes 5111808 | tf_op jit(solution)/shard_map/all_to_all | solution.py:128
  486.6 5.6 %collective-permute-start.11 = (bf16[48,1536]{1,0:T(8,128)(2,1)S(1)}, bf16[48,1536]{1,0:T(8,128)(2,1)S(1)}, u32[]{:S(2)}, u32[]{:S(2)}) collective-permute-start(bf16[48,1536]{1,0:T(8,128)(2,1)S(1)} %fusion.56), channel_id=1, source_target_pairs={{0,1},{1,0},{2,3},{3,2},{4,5},{5,4},{6,7},{7,6},{8,9},{9,8},{10,11... | collective-permute-start | bytes 442376 | tf_op jit(solution)/shard_map/ppermute | solution.py:134
  489.1 7.6 %collective-permute-start.12 = (bf16[48,1536]{1,0:T(8,128)(2,1)S(1)}, bf16[48,1536]{1,0:T(8,128)(2,1)S(1)}, u32[]{:S(2)}, u32[]{:S(2)}) collective-permute-start(bf16[48,1536]{1,0:T(8,128)(2,1)S(1)} %fusion.56), channel_id=1, source_target_pairs={{0,3},{1,2},{2,1},{3,0},{4,7},{5,6},{6,5},{7,4},{8,11},{9,10},{10,... | collective-permute-start | bytes 442376 | tf_op jit(solution)/shard_map/ppermute | solution.py:134
  490.7 8.6 %collective-permute-start.10 = (bf16[48,1664]{1,0:T(8,128)(2,1)S(1)}, bf16[48,1664]{1,0:T(8,128)(2,1)S(1)}, u32[]{:S(2)}, u32[]{:S(2)}) collective-permute-start(bf16[48,1664]{1,0:T(8,128)(2,1)S(1)} %pad_maximum_fusion), channel_id=1, source_target_pairs={{0,2},{1,3},{2,0},{3,1},{4,6},{5,7},{6,4},{7,5},{8,10},{9,11},{10,... | collective-permute-start | bytes 479240 | tf_op jit(solution)/shard_map/ppermute | solution.py:134
  (97 other events, 667.9 us)

commit v8 on v7

--- a/solution.py
+++ b/solution.py
@@ -84,13 +84,13 @@
     return matrix.reshape(SEQ, HEADS, HEAD)
 
 
-def gather_cols(mine, after=None):
-    groups = lax.axis_size("ea")
-    sent = jnp.broadcast_to(mine[None], (groups,) + mine.shape)
-    if after is not None:
-        sent, _ = lax.optimization_barrier((sent, after))
+def copies(mine):
+    return jnp.broadcast_to(mine[None], (lax.axis_size("ea"),) + mine.shape)
+
+
+def gather_cols(sent):
     got = lax.all_to_all(sent, "ea", split_axis=0, concat_axis=0)
-    return got.reshape(-1, mine.shape[1])
+    return got.reshape(-1, sent.shape[2])
 
 
 def core_half(value, which=0):
@@ -428,7 +428,8 @@
     for b in range(LAYERS):
         small = jnp.concatenate([router_weight[b], norm_gains[b].T, norm_biases[b].T], axis=1)
         mine.append(core_dense(qkv_weight[b], out_weight[b], pad_cols(small, 128)))
-    dense0 = split_dense(gather_cols(mine[0]))
+    gathered0, sent1 = lax.optimization_barrier((gather_cols(copies(mine[0])), copies(mine[1])))
+    dense0 = split_dense(gathered0)
     weights = [expert_in, expert_out]
     onehot0, code = routing(routes[0], experts)
     send, fetch = one_hots(code, experts * 2 * SLOTS, 1, 0)
@@ -444,7 +445,8 @@
     after0, normed0, logits, kept0 = attention(state, dense0)
     router0, gate0 = router_forward(logits[:, :experts], onehot0)
     arrived = exchange(dot(send[:, :tokens] + send[:, tokens:], normed0).astype(BF))
-    gathered1 = gather_cols(mine[1], after=arrived)
+    sent1, arrived = lax.optimization_barrier((sent1, arrived))
+    gathered1 = gather_cols(sent1)
     rows0 = (arrived, swap_core(arrived))
     first = [
         expert_call(forward_kernel, 0, [r], weights, [r.shape] * 3, 2) for r in rows0

time: 511 us -> 514 us (level)
  blocking collectives: 114 us -> 74.9 us
  waiting for transfers between devices: 143 us -> 175 us
  starting transfers between devices: 61.1 us -> 71.2 us
    all_to_all x1 -> x0, blocking collectives: 41.4 us -> none  [gather_cols(): got = lax.all_to_all(sent, 'ea', split_axis=0, concat_axis=0)]
    all_to_all x1 -> x2, waiting for transfers between devices: 11 us -> 43.8 us  [gather_cols(): got = lax.all_to_all(sent, 'ea', split_axis=0, concat_axis=0)]
    all_to_all x1 -> x2, starting transfers between devices: 4.06 us -> 13.9 us  [gather_cols(): got = lax.all_to_all(sent, 'ea', split_axis=0, concat_axis=0)]
    unnamed x228 -> x230, local copies, waits for them, and re-layouts: 23.3 us -> 22.9 us
  transfers between devices with their start and end apart: 20 -> 21, of which waited for: 13 -> 14; matrix products, arithmetic and copies ran while one was open for 13% -> 12% of each run, Pallas kernels for 7% -> 7%
where the time goes in v8:
time: 514 us; the launch traced here: 505 us
  waiting for transfers between devices  175 us (34%)
  blocking collectives  74.9 us (15%)
  starting transfers between devices  71.2 us (14%)
  Pallas kernels  69.6 us (14%)
  matrix products  41.1 us (8%)
  other arithmetic  39.6 us (8%)
  local copies, waits for them, and re-layouts  31.1 us (6%)
    all_to_all x2, blocking collectives, exchange(): return lax.all_to_all(rows, GROUP, split_axis=0, concat_axis=0, tiled=True)  74.9 us
    all_to_all x4, waiting for transfers between devices, exchange(): return lax.all_to_all(rows, GROUP, split_axis=0, concat_axis=0, tiled=True)  69.7 us
    all_to_all x2, waiting for transfers between devices, gather_cols(): got = lax.all_to_all(sent, 'ea', split_axis=0, concat_axis=0)  43.8 us
    all_to_all x2, waiting for transfers between devices, sum_exchange(): lax.all_to_all(pair.reshape(groups, -1, pair.shape[1]), 'ea', split_axis=...  39.1 us
    dot_general x16, matrix products, dot(): return lax.dot_general(a, b, (dims, ((), ())), preferred_element_type=F32)  38.7 us
    pallas_call x6, Pallas kernels, expert_call(): pl.pallas_call(kernel, grid=(count // (GROUPS * SLOTS),), in_specs=[spec(...  35.9 us
    pallas_call x4, Pallas kernels, whole_call(): pl.pallas_call(kernel, in_specs=[pl.BlockSpec(memory_space=pltpu.SMEM)] +...  33.7 us
    all_to_all x4, starting transfers between devices, exchange(): return lax.all_to_all(rows, GROUP, split_axis=0, concat_axis=0, tiled=True)  23.7 us
  transfers between devices with their start and end apart: 21, of which 14 were waited for; matrix products, arithmetic and copies ran while one was open for 12% of the time, Pallas kernels for 7%

profile of v8, /device:TPU:1, one launch (start us, length us, event | category | flops | bytes accessed | tf_op | source)
XLA Modules:
  0.0 505.4 jit_solution(5060147436990323748)
XLA Ops:
  6.5 9.8 %all-to-all-start = ((bf16[32,24,1664]{2,1,0:T(8,128)(2,1)}), bf16[32,24,1664]{2,1,0:T(8,128)(2,1)S(1)}, u32[]{:S(2)}, u32[]{:S(2)}) async-start(bf16[32,24,1664]{2,1,0:T(8,128)(2,1)} %broadcast_in_dim.8), calls=%async_computation | async-start | bytes 5111808 | tf_op jit(solution)/shard_map/all_to_all | solution.py:92
  16.7 32.2 %all-to-all-done = bf16[32,24,1664]{2,1,0:T(8,128)(2,1)S(1)} async-done(((bf16[32,24,1664]{2,1,0:T(8,128)(2,1)}), bf16[32,24,1664]{2,1,0:T(8,128)(2,1)S(1)}, u32[]{:S(2)}, u32[]{:S(2)}) %all-to-all-start) | async-done | bytes 2555936 | tf_op jit(solution)/shard_map/all_to_all | solution.py:92
  62.7 31.3 %all_to_all.89 = bf16[64,16,768]{2,1,0:T(8,128)(2,1)} all-to-all(bf16[64,16,768]{2,1,0:T(8,128)(2,1)S(1)} %bitcast.113), channel_id=1, replica_groups=mesh['ea'=32,'half'=2,'core'=2] {'ea','half'}, dimensions={0} | all-to-all | bytes 3145728 | tf_op jit(solution)/shard_map/all_to_all | solution.py:42
  103.5 6.5 %shard_map.171 = (bf16[1024,768]{1,0:T(8,128)(2,1)S(1)}, bf16[1024,768]{1,0:T(8,128)(2,1)S(1)}, bf16[1024,768]{1,0:T(8,128)(2,1)S(1)}) custom-call(bf16[1024,768]{1,0:T(8,128)(2,1)} %collective-permute-done.1.rows, bf16[2,1,768,768]{3,2,1,0:T(8,128)(2,1)S(1)} %copy-done.25, bf16[2,1,768,768]{3,2,1,0:T(8,128)(2,1)S(1)} %copy-done.30), custom_call_target="tpu_custom_call" | custom-call | flops 2415919104 | bytes 8650752 | tf_op jit(solution)/shard_map/pallas_call | solution.py:342
  113.6 6.5 %shard_map.170 = (bf16[1024,768]{1,0:T(8,128)(2,1)S(1)}, bf16[1024,768]{1,0:T(8,128)(2,1)S(1)}, bf16[1024,768]{1,0:T(8,128)(2,1)S(1)}) custom-call(bf16[1024,768]{1,0:T(8,128)(2,1)} %bitcast.20.rows, bf16[2,1,768,768]{3,2,1,0:T(8,128)(2,1)S(1)} %copy-done.26, bf16[2,1,768,768]{3,2,1,0:T(8,128)(2,1)S(1)} %copy-done.30), custom_call_target="tpu_custom_call" | custom-call | flops 2415919104 | bytes 8650752 | tf_op jit(solution)/shard_map/pallas_call | solution.py:342
  123.9 11.6 %all-to-all-done.2 = bf16[32,24,1664]{2,1,0:T(8,128)(2,1)S(1)} async-done(((bf16[32,24,1664]{2,1,0:T(8,128)(2,1)}), bf16[32,24,1664]{2,1,0:T(8,128)(2,1)S(1)}, u32[]{:S(2)}, u32[]{:S(2)}) %all-to-all-start.2) | async-done | bytes 2555936 | tf_op jit(solution)/shard_map/all_to_all | solution.py:92
  136.3 6.8 %all-to-all-start.3 = ((bf16[64,16,768]{2,1,0:T(8,128)(2,1)}), bf16[64,16,768]{2,1,0:T(8,128)(2,1)}, u32[]{:S(2)}, u32[]{:S(2)}) async-start(bf16[64,16,768]{2,1,0:T(8,128)(2,1)} %bitcast.114), calls=%async_computation.3 | async-start | bytes 3145728 | tf_op jit(solution)/shard_map/all_to_all | solution.py:42
  143.1 5.1 %and_convert_fusion.1 = (bf16[2048,394]{1,0:T(8,128)(2,1)S(1)}, bf16[2048,394]{1,0:T(8,128)(2,1)}) fusion(s32[2048]{0:T(1024)S(1)} %get-tuple-element.176, s32[2048]{0:T(1024)S(1)} %broadcast_add_fusion, pred[2048]{0:T(1024)(128)(4,1)S(1)} %fusion.80, s32[394]{0:T(512)S(1)} %convert_add_fusion.2, s32[2048]{0:T(1024)S(1)} %get-tuple-element.177), kind=kLoop, calls=%fused_computation.35 | loop fusion | flops 22593536 | bytes 3255848 | tf_op jit(solution)/shard_map/convert_element_type | solution.py:387
  150.1 16.3 %all-to-all-done.3 = bf16[64,16,768]{2,1,0:T(8,128)(2,1)} async-done(((bf16[64,16,768]{2,1,0:T(8,128)(2,1)}), bf16[64,16,768]{2,1,0:T(8,128)(2,1)}, u32[]{:S(2)}, u32[]{:S(2)}) %all-to-all-start.3) | async-done | bytes 1572896 | tf_op jit(solution)/shard_map/all_to_all | solution.py:42
  170.0 6.0 %shard_map.172 = (bf16[197,1152]{1,0:T(8,128)(2,1)S(1)}, bf16[197,1152]{1,0:T(8,128)(2,1)S(1)}, bf16[197,768]{1,0:T(8,128)(2,1)S(1)}, f32[197,768]{1,0:T(8,128)S...) custom-call(s32[1]{0:T(128)} %bitcast.core_ref, f32[197,768]{1,0:T(8,128)S(1)} %multiply_add_fusion.state, ...), custom_call_target="tpu_custom_call" | custom-call | flops 2336010240 | bytes 8388608 | tf_op jit(solution)/shard_map/pallas_call | solution.py:262
  180.1 43.6 %all_to_all.90 = bf16[64,32,768]{2,1,0:T(8,128)(2,1)S(1)} all-to-all(bf16[64,32,768]{2,1,0:T(8,128)(2,1)S(1)} %bitcast.116), channel_id=1, replica_groups=mesh['ea'=32,'half'=2,'core'=2] {'ea','half'}, dimensions={0} | all-to-all | bytes 6291456 | tf_op jit(solution)/shard_map/all_to_all | solution.py:42
  227.2 5.3 %collective-permute-done.4.rows = bf16[64,2,16,768]{3,2,1,0:T(8,128)(2,1)S(1)} collective-permute-done((bf16[64,2,16,768]{3,2,1,0:T(8,128)(2,1)S(1)}, bf16[64,2,16,768]{3,2,1,0:T(8,128)(2,1)S(1)}, u32[]{:S(2)}, u32[]{:S(2)}) %collective-permute-start.4) | collective-permute-done | bytes 3145760 | tf_op jit(solution)/shard_map/ppermute | solution.py:38
  232.5 7.5 %shard_map.174 = (bf16[1024,768]{1,0:T(8,128)(2,1)S(1)}, bf16[1024,768]{1,0:T(8,128)(2,1)S(1)}, bf16[64,2,16,768]{3,2,1,0:T(8,128)(2,1)S(1)}) custom-call(bf16[64,2,16,768]{3,2,1,0:T(8,128)(2,1)S(1)} %collective-permute-done.4.rows, bf16[2,1,768,768]{3,2,1,0:T(8,128)(2,1)S(1)} %copy-done.27, bf16[2,1,768,768]{3,2,1,0:T(8,128)(2,1)S(1)} %copy-done.31), custom_call_target="tpu_custom_call" | custom-call | flops 4831838208 | bytes 8650752 | tf_op jit(solution)/shard_map/pallas_call | solution.py:342
  242.7 7.6 %shard_map.173 = (bf16[1024,768]{1,0:T(8,128)(2,1)S(1)}, bf16[1024,768]{1,0:T(8,128)(2,1)S(1)}, bf16[64,2,16,768]{3,2,1,0:T(8,128)(2,1)S(1)}) custom-call(bf16[64,2,16,768]{3,2,1,0:T(8,128)(2,1)S(1)} %bitcast.100, bf16[2,1,768,768]{3,2,1,0:T(8,128)(2,1)S(1)} %copy-done.27, bf16[2,1,768,768]{3,2,1,0:T(8,128)(2,1)S(1)} %copy-done.31), custom_call_target="tpu_custom_call" | custom-call | flops 4831838208 | bytes 8650752 | tf_op jit(solution)/shard_map/pallas_call | solution.py:342
  253.2 5.6 %all-to-all-start.5 = ((bf16[64,32,768]{2,1,0:T(8,128)(2,1)}), bf16[64,32,768]{2,1,0:T(8,128)(2,1)}, u32[]{:S(2)}, u32[]{:S(2)}) async-start(bf16[64,32,768]{2,1,0:T(8,128)(2,1)} %bitcast.110), calls=%async_computation.5 | async-start | bytes 6291456 | tf_op jit(solution)/shard_map/all_to_all | solution.py:42
  275.8 24.3 %all-to-all-done.5 = bf16[64,32,768]{2,1,0:T(8,128)(2,1)} async-done(((bf16[64,32,768]{2,1,0:T(8,128)(2,1)}), bf16[64,32,768]{2,1,0:T(8,128)(2,1)}, u32[]{:S(2)}, u32[]{:S(2)}) %all-to-all-start.5) | async-done | bytes 3145760 | tf_op jit(solution)/shard_map/all_to_all | solution.py:42
  307.1 13.7 %shard_map.175 = (f32[197,768]{1,0:T(8,128)S(1)}, bf16[768,1664]{1,0:T(8,128)(2,1)S(1)}, bf16[768,1664]{1,0:T(8,128)(2,1)}) custom-call(s32[1]{0:T(128)} %bitcast.core_ref, f32[197,768]{1,0:T(8,128)S(1)} %copy-done.10, f32[197,768]{1,0:T(8,128)S(1)} %convolution_add_fusion.4.grad_two, f32[197,768]{1,0:T(8,128)S(1)} %copy-done.17, f32[197,768]{1,0:T(8,128)S(1)} %copy-done.19, ...), custom_call_target="tpu_custom_call" | custom-call | flops 8438685696 | bytes 8388608 | tf_op jit(solution)/shard_map/pallas_call | solution.py:262
  325.1 5.9 %all-to-all-start.6 = ((bf16[64,16,768]{2,1,0:T(8,128)(2,1)}), bf16[64,16,768]{2,1,0:T(8,128)(2,1)}, u32[]{:S(2)}, u32[]{:S(2)}) async-start(bf16[64,16,768]{2,1,0:T(8,128)(2,1)} %bitcast.121), calls=%async_computation.6 | async-start | bytes 3145728 | tf_op jit(solution)/shard_map/all_to_all | solution.py:42
  334.8 19.3 %all-to-all-done.6 = bf16[64,16,768]{2,1,0:T(8,128)(2,1)} async-done(((bf16[64,16,768]{2,1,0:T(8,128)(2,1)}), bf16[64,16,768]{2,1,0:T(8,128)(2,1)}, u32[]{:S(2)}, u32[]{:S(2)}) %all-to-all-start.6) | async-done | bytes 1572896 | tf_op jit(solution)/shard_map/all_to_all | solution.py:42
  367.4 4.6 shard_map.176
  373.7 5.5 %all-to-all-start.7 = ((bf16[64,16,768]{2,1,0:T(8,128)(2,1)}), bf16[64,16,768]{2,1,0:T(8,128)(2,1)}, u32[]{:S(2)}, u32[]{:S(2)}) async-start(bf16[64,16,768]{2,1,0:T(8,128)(2,1)} %bitcast.115), calls=%async_computation.7 | async-start | bytes 3145728 | tf_op jit(solution)/shard_map/all_to_all | solution.py:42
  384.2 4.4 fusion.113
  392.9 9.8 %all-to-all-done.7 = bf16[64,16,768]{2,1,0:T(8,128)(2,1)} async-done(((bf16[64,16,768]{2,1,0:T(8,128)(2,1)}), bf16[64,16,768]{2,1,0:T(8,128)(2,1)}, u32[]{:S(2)}, u32[]{:S(2)}) %all-to-all-start.7) | async-done | bytes 1572896 | tf_op jit(solution)/shard_map/all_to_all | solution.py:42
  402.7 5.1 %all-to-all-start.8 = ((bf16[32,24,1664]{2,1,0:T(8,128)(2,1)}), bf16[32,24,1664]{2,1,0:T(8,128)(2,1)}, u32[]{:S(2)}, u32[]{:S(2)}) async-start(bf16[32,24,1664]{2,1,0:T(8,128)(2,1)} %bitcast.111), calls=%async_computation.8 | async-start | bytes 5111808 | tf_op jit(solution)/shard_map/all_to_all | solution.py:128
  412.6 10.1 %shard_map.178 = (f32[197,768]{1,0:T(8,128)}, bf16[768,1664]{1,0:T(8,128)(2,1)S(1)}, bf16[768,1664]{1,0:T(8,128)(2,1)S(1)}) custom-call(s32[1]{0:T(128)} %bitcast.core_ref, f32[197,768]{1,0:T(8,128)S(1)} %copy-done.15, f32[197,768]{1,0:T(8,128)S(1)} %convolution_add_fusion.3.grad_two, f32[197,768]{1,0:T(8,128)S(1)} %copy-done.9, f32[197,768]{1,0:T(8,128)S(1)} %copy-done.13, ...), custom_call_target="tpu_custom_call" | custom-call | flops 8438685696 | bytes 8388608 | tf_op jit(solution)/shard_map/pallas_call | solution.py:262
  424.2 15.6 %all-to-all-done.8 = bf16[32,24,1664]{2,1,0:T(8,128)(2,1)} async-done(((bf16[32,24,1664]{2,1,0:T(8,128)(2,1)}), bf16[32,24,1664]{2,1,0:T(8,128)(2,1)}, u32[]{:S(2)}, u32[]{:S(2)}) %all-to-all-start.8) | async-done | bytes 2555936 | tf_op jit(solution)/shard_map/all_to_all | solution.py:128
  439.8 4.7 collective-permute-start.9
  444.6 4.7 collective-permute-done.9
  451.4 5.1 %all-to-all-start.9 = ((bf16[32,24,1664]{2,1,0:T(8,128)(2,1)}), bf16[32,24,1664]{2,1,0:T(8,128)(2,1)S(1)}, u32[]{:S(2)}, u32[]{:S(2)}) async-start(bf16[32,24,1664]{2,1,0:T(8,128)(2,1)} %bitcast.112), calls=%async_computation.9 | async-start | bytes 5111808 | tf_op jit(solution)/shard_map/all_to_all | solution.py:128
  456.5 5.0 maximum_bitcast_fusion.1
  466.1 23.6 %all-to-all-done.9 = bf16[32,24,1664]{2,1,0:T(8,128)(2,1)S(1)} async-done(((bf16[32,24,1664]{2,1,0:T(8,128)(2,1)}), bf16[32,24,1664]{2,1,0:T(8,128)(2,1)S(1)}, u32[]{:S(2)}, u32[]{:S(2)}) %all-to-all-start.9) | async-done | bytes 2555936 | tf_op jit(solution)/shard_map/all_to_all | solution.py:128
  495.7 4.6 collective-permute-done.12
  (345 shorter events, 135.4 us)
Async XLA Ops:
  6.5 42.4 %all-to-all-start = ((bf16[32,24,1664]{2,1,0:T(8,128)(2,1)}), bf16[32,24,1664]{2,1,0:T(8,128)(2,1)S(1)}, u32[]{:S(2)}, u32[]{:S(2)}) async-start(bf16[32,24,1664]{2,1,0:T(8,128)(2,1)} %broadcast_in_dim.8), calls=%async_computation | async-start | bytes 5111808 | tf_op jit(solution)/shard_map/all_to_all | solution.py:92
  16.3 37.3 %copy-start.75 = (bf16[197,768]{1,0:T(8,128)(2,1)S(1)}, bf16[197,768]{1,0:T(8,128)(2,1)}, u32[]{:S(2)}) copy-start(bf16[197,768]{1,0:T(8,128)(2,1)} %param.10) | copy-start | bytes 907780
  16.3 37.3 %copy-start.107 = (s32[2,197,2]{1,2,0:T(2,128)S(1)}, s32[2,197,2]{1,2,0:T(2,128)}, u32[]{:S(2)}) copy-start(s32[2,197,2]{1,2,0:T(2,128)} %param.12) | copy-start | bytes 9460
  50.7 7.3 %collective-permute-start = (bf16[768,1664]{1,0:T(8,128)(2,1)S(1)}, bf16[768,1664]{1,0:T(8,128)(2,1)S(1)}, u32[]{:S(2)}, u32[]{:S(2)}) collective-permute-start(bf16[768,1664]{1,0:T(8,128)(2,1)S(1)} %bitcast.106), channel_id=1, source_target_pairs={{0,1},{1,0},{2,3},{3,2},{4,5},{5,4},{6,7},{7,6},{8,9},{9,8},{10,11... | collective-permute-start | bytes 7667720 | tf_op jit(solution)/shard_map/ppermute | solution.py:38
  53.7 112.8 %copy-start.108 = (pred[1024]{0:T(1024)(128)(4,1)}, pred[1024]{0:T(1024)(128)(4,1)S(1)}, u32[]{:S(2)}) copy-start(pred[1024]{0:T(1024)(128)(4,1)S(1)} %fusion.86) | copy-start | bytes 3076
  53.8 112.7 %copy-start.88 = (s32[1024]{0:T(1024)}, s32[1024]{0:T(1024)S(1)}, u32[]{:S(2)}) copy-start(s32[1024]{0:T(1024)S(1)} %broadcast_add_fusion.1) | copy-start | bytes 12292
  53.8 112.7 %copy-start.90 = (s32[1024]{0:T(1024)}, s32[1024]{0:T(1024)S(1)}, u32[]{:S(2)}) copy-start(s32[1024]{0:T(1024)S(1)} %get-tuple-element.181) | copy-start | bytes 12292
  53.8 112.7 %copy-start.92 = (s32[1024]{0:T(1024)}, s32[1024]{0:T(1024)S(1)}, u32[]{:S(2)}) copy-start(s32[1024]{0:T(1024)S(1)} %get-tuple-element.182) | copy-start | bytes 12292
  54.4 112.1 %copy-start.105 = (s32[394]{0:T(512)}, s32[394]{0:T(512)S(1)}, u32[]{:S(2)}) copy-start(s32[394]{0:T(512)S(1)} %convert_add_fusion.3) | copy-start | bytes 4732
  94.1 6.0 %collective-permute-start.1 = (bf16[1024,768]{1,0:T(8,128)(2,1)}, bf16[1024,768]{1,0:T(8,128)(2,1)}, u32[]{:S(2)}, u32[]{:S(2)}) collective-permute-start(bf16[1024,768]{1,0:T(8,128)(2,1)} %bitcast.20.rows), channel_id=1, source_target_pairs={{0,1},{1,0},{2,3},{3,2},{4,5},{5,4},{6,7},{7,6},{8,9},{9,8},{10,11... | collective-permute-start | bytes 4718600 | tf_op jit(solution)/shard_map/ppermute | solution.py:38
  96.0 39.4 %all-to-all-start.2 = ((bf16[32,24,1664]{2,1,0:T(8,128)(2,1)}), bf16[32,24,1664]{2,1,0:T(8,128)(2,1)S(1)}, u32[]{:S(2)}, u32[]{:S(2)}) async-start(bf16[32,24,1664]{2,1,0:T(8,128)(2,1)} %broadcast_in_dim.9), calls=%async_computation.2 | async-start | bytes 5111808 | tf_op jit(solution)/shard_map/all_to_all | solution.py:92
  112.4 10.0 %collective-permute-start.2 = (bf16[1024,768]{1,0:T(8,128)(2,1)S(1)}, bf16[1024,768]{1,0:T(8,128)(2,1)S(1)}, u32[]{:S(2)}, u32[]{:S(2)}) collective-permute-start(bf16[1024,768]{1,0:T(8,128)(2,1)S(1)} %get-tuple-element.68), channel_id=1, source_target_pairs={{0,1},{1,0},{2,3},{3,2},{4,5},{5,4},{6,7},{7,6},{8,9},{9,8},{10,11... | collective-permute-start | bytes 4718600 | tf_op jit(solution)/shard_map/ppermute | solution.py:38
  113.6 62.7 %copy-start.70 = (f32[394,32]{1,0:T(8,128)}, f32[394,32]{1,0:T(8,128)S(1)}, u32[]{:S(2)}) copy-start(f32[394,32]{1,0:T(8,128)S(1)} %fusion.52) | copy-start | bytes 151300
  135.5 34.5 %copy-start.2 = (bf16[32,24,1664]{2,1,0:T(8,128)(2,1)}, bf16[32,24,1664]{2,1,0:T(8,128)(2,1)S(1)}, u32[]{:S(2)}) copy-start(bf16[32,24,1664]{2,1,0:T(8,128)(2,1)S(1)} %all-to-all-done.2) | copy-start | bytes 7667716
  135.5 34.5 %collective-permute-start.3 = (bf16[768,1664]{1,0:T(8,128)(2,1)S(1)}, bf16[768,1664]{1,0:T(8,128)(2,1)}, u32[]{:S(2)}, u32[]{:S(2)}) collective-permute-start(bf16[768,1664]{1,0:T(8,128)(2,1)S(1)} %bitcast.102), channel_id=1, source_target_pairs={{0,1},{1,0},{2,3},{3,2},{4,5},{5,4},{6,7},{7,6},{8,9},{9,8},{10,11... | collective-permute-start | bytes 7667720 | tf_op jit(solution)/shard_map/ppermute | solution.py:38
  136.3 30.2 %all-to-all-start.3 = ((bf16[64,16,768]{2,1,0:T(8,128)(2,1)}), bf16[64,16,768]{2,1,0:T(8,128)(2,1)}, u32[]{:S(2)}, u32[]{:S(2)}) async-start(bf16[64,16,768]{2,1,0:T(8,128)(2,1)} %bitcast.114), calls=%async_computation.3 | async-start | bytes 3145728 | tf_op jit(solution)/shard_map/all_to_all | solution.py:42
  180.1 52.4 %copy-start.27 = (bf16[2,1,768,768]{3,2,1,0:T(8,128)(2,1)S(1)}, bf16[2,1,768,768]{3,2,1,0:T(8,128)(2,1)}, u32[]{:S(2)}) copy-start(bf16[2,1,768,768]{3,2,1,0:T(8,128)(2,1)} %w_in.11) | copy-start | bytes 7077892
  180.1 52.3 %copy-start.31 = (bf16[2,1,768,768]{3,2,1,0:T(8,128)(2,1)S(1)}, bf16[2,1,768,768]{3,2,1,0:T(8,128)(2,1)}, u32[]{:S(2)}) copy-start(bf16[2,1,768,768]{3,2,1,0:T(8,128)(2,1)} %w_out.11) | copy-start | bytes 7077892
  223.7 8.8 %collective-permute-start.4 = (bf16[64,2,16,768]{3,2,1,0:T(8,128)(2,1)S(1)}, bf16[64,2,16,768]{3,2,1,0:T(8,128)(2,1)S(1)}, u32[]{:S(2)}, u32[]{:S(2)}) collective-permute-start(bf16[64,2,16,768]{3,2,1,0:T(8,128)(2,1)S(1)} %bitcast.99), channel_id=1, source_target_pairs={{0,1},{1,0},{2,3},{3,2},{4,5},{5,4},{6,7},{7,6},{8,9},{9,8},{10,11... | collective-permute-start | bytes 9437192 | tf_op jit(solution)/shard_map/ppermute | solution.py:38
  242.3 8.0 %collective-permute-start.5 = (bf16[64,2,16,768]{3,2,1,0:T(8,128)(2,1)S(1)}, bf16[64,2,16,768]{3,2,1,0:T(8,128)(2,1)S(1)}, u32[]{:S(2)}, u32[]{:S(2)}) collective-permute-start(bf16[64,2,16,768]{3,2,1,0:T(8,128)(2,1)S(1)} %get-tuple-element.76), channel_id=1, source_target_pairs={{0,1},{1,0},{2,3},{3,2},{4,5},{5,4},{6,7},{7,6},{8,9},{9,8},{10,11... | collective-permute-start | bytes 9437192 | tf_op jit(solution)/shard_map/ppermute | solution.py:38
  253.2 46.9 %all-to-all-start.5 = ((bf16[64,32,768]{2,1,0:T(8,128)(2,1)}), bf16[64,32,768]{2,1,0:T(8,128)(2,1)}, u32[]{:S(2)}, u32[]{:S(2)}) async-start(bf16[64,32,768]{2,1,0:T(8,128)(2,1)} %bitcast.110), calls=%async_computation.5 | async-start | bytes 6291456 | tf_op jit(solution)/shard_map/all_to_all | solution.py:42
  320.8 10.2 %collective-permute-start.6 = (bf16[768,1664]{1,0:T(8,128)(2,1)}, bf16[768,1664]{1,0:T(8,128)(2,1)}, u32[]{:S(2)}, u32[]{:S(2)}) collective-permute-start(bf16[768,1664]{1,0:T(8,128)(2,1)} %get-tuple-element.87), channel_id=1, source_target_pairs={{0,1},{1,0},{2,3},{3,2},{4,5},{5,4},{6,7},{7,6},{8,9},{9,8},{10,11... | collective-permute-start | bytes 7667720 | tf_op jit(solution)/shard_map/ppermute | solution.py:38
  325.1 29.1 %all-to-all-start.6 = ((bf16[64,16,768]{2,1,0:T(8,128)(2,1)}), bf16[64,16,768]{2,1,0:T(8,128)(2,1)}, u32[]{:S(2)}, u32[]{:S(2)}) async-start(bf16[64,16,768]{2,1,0:T(8,128)(2,1)} %bitcast.121), calls=%async_computation.6 | async-start | bytes 3145728 | tf_op jit(solution)/shard_map/all_to_all | solution.py:42
  354.2 5.0 collective-permute-start.7
  367.0 5.1 %collective-permute-start.8 = (bf16[1024,768]{1,0:T(8,128)(2,1)S(1)}, bf16[1024,768]{1,0:T(8,128)(2,1)S(1)}, u32[]{:S(2)}, u32[]{:S(2)}) collective-permute-start(bf16[1024,768]{1,0:T(8,128)(2,1)S(1)} %get-tuple-element.92), channel_id=1, source_target_pairs={{0,1},{1,0},{2,3},{3,2},{4,5},{5,4},{6,7},{7,6},{8,9},{9,8},{10,11... | collective-permute-start | bytes 4718600 | tf_op jit(solution)/shard_map/ppermute | solution.py:38
  373.7 28.9 %all-to-all-start.7 = ((bf16[64,16,768]{2,1,0:T(8,128)(2,1)}), bf16[64,16,768]{2,1,0:T(8,128)(2,1)}, u32[]{:S(2)}, u32[]{:S(2)}) async-start(bf16[64,16,768]{2,1,0:T(8,128)(2,1)} %bitcast.115), calls=%async_computation.7 | async-start | bytes 3145728 | tf_op jit(solution)/shard_map/all_to_all | solution.py:42
  402.7 37.1 %all-to-all-start.8 = ((bf16[32,24,1664]{2,1,0:T(8,128)(2,1)}), bf16[32,24,1664]{2,1,0:T(8,128)(2,1)}, u32[]{:S(2)}, u32[]{:S(2)}) async-start(bf16[32,24,1664]{2,1,0:T(8,128)(2,1)} %bitcast.111), calls=%async_computation.8 | async-start | bytes 5111808 | tf_op jit(solution)/shard_map/all_to_all | solution.py:128
  439.8 9.4 %collective-permute-start.9 = (bf16[768,1664]{1,0:T(8,128)(2,1)}, bf16[768,1664]{1,0:T(8,128)(2,1)S(1)}, u32[]{:S(2)}, u32[]{:S(2)}) collective-permute-start(bf16[768,1664]{1,0:T(8,128)(2,1)} %copy-done.24), channel_id=1, source_target_pairs={{0,1},{1,0},{2,3},{3,2},{4,5},{5,4},{6,7},{7,6},{8,9},{9,8},{10,11... | collective-permute-start | bytes 7667720 | tf_op jit(solution)/shard_map/ppermute | solution.py:38
  451.4 38.3 %all-to-all-start.9 = ((bf16[32,24,1664]{2,1,0:T(8,128)(2,1)}), bf16[32,24,1664]{2,1,0:T(8,128)(2,1)S(1)}, u32[]{:S(2)}, u32[]{:S(2)}) async-start(bf16[32,24,1664]{2,1,0:T(8,128)(2,1)} %bitcast.112), calls=%async_computation.9 | async-start | bytes 5111808 | tf_op jit(solution)/shard_map/all_to_all | solution.py:128
  490.1 5.6 %collective-permute-start.11 = (bf16[48,1536]{1,0:T(8,128)(2,1)S(1)}, bf16[48,1536]{1,0:T(8,128)(2,1)S(1)}, u32[]{:S(2)}, u32[]{:S(2)}) collective-permute-start(bf16[48,1536]{1,0:T(8,128)(2,1)S(1)} %fusion.56), channel_id=1, source_target_pairs={{0,1},{1,0},{2,3},{3,2},{4,5},{5,4},{6,7},{7,6},{8,9},{9,8},{10,11... | collective-permute-start | bytes 442376 | tf_op jit(solution)/shard_map/ppermute | solution.py:134
  492.6 7.6 %collective-permute-start.12 = (bf16[48,1536]{1,0:T(8,128)(2,1)S(1)}, bf16[48,1536]{1,0:T(8,128)(2,1)S(1)}, u32[]{:S(2)}, u32[]{:S(2)}) collective-permute-start(bf16[48,1536]{1,0:T(8,128)(2,1)S(1)} %fusion.56), channel_id=1, source_target_pairs={{0,3},{1,2},{2,1},{3,0},{4,7},{5,6},{6,5},{7,4},{8,11},{9,10},{10,... | collective-permute-start | bytes 442376 | tf_op jit(solution)/shard_map/ppermute | solution.py:134
  494.2 8.6 %collective-permute-start.10 = (bf16[48,1664]{1,0:T(8,128)(2,1)S(1)}, bf16[48,1664]{1,0:T(8,128)(2,1)S(1)}, u32[]{:S(2)}, u32[]{:S(2)}) collective-permute-start(bf16[48,1664]{1,0:T(8,128)(2,1)S(1)} %pad_maximum_fusion), channel_id=1, source_target_pairs={{0,2},{1,3},{2,0},{3,1},{4,6},{5,7},{6,4},{7,5},{8,10},{9,11},{10,... | collective-permute-start | bytes 479240 | tf_op jit(solution)/shard_map/ppermute | solution.py:134
  (99 other events, 732.2 us)
